TPU v7x, 512 devices: a whole 4x8x8 slice. The times are simulated.
512 devices in a mesh: seq: 64 (over z_lo, y, core), tp: 8 (over z_hi, x).
Axes of the slice: x: 4, y: 8, z: 8 (z_hi: 2, z_lo: 4; z = z_hi * 4 + z_lo), core: 2. Of those that a mesh axis runs over, the one named last changes fastest.
Arguments:
- queries: bfloat16 [16384, 4096], P('seq', 'tp'), may hold values from -64 to 64
- keys: bfloat16 [16384, 1024], P('seq', 'tp'), may hold values from -6 to 6
- values: bfloat16 [16384, 1024], P('seq', 'tp'), may hold values from -6 to 6
- key_head_scale: float32 [8], P('tp'), may hold values from 0.5 to 2
- retained: int32 [64, 1], P('seq'), may hold values from 0 to 1
- out_weight: bfloat16 [4096, 4096], P('tp'), may hold values from -0.09375 to 0.09375
- norm_gain: float32 [4096], P('tp'), may hold values from 0.5 to 1.5
Outputs:
- normed: bfloat16 [16384, 4096], P('seq', 'tp')
All inputs are finite; a program needn't handle non-finite values.
Results may differ from a plain program's by a relative error of at most 0.02.
Values may be sent and summed in bfloat16 or wider, within the bound.
No kernel may reach another device: no remote copies, remote signals or barrier semaphores. Data moves between devices by JAX's collectives and lax.ppermute only.
A program may use at most 128 MiB of HBM per device.

v0:
```python
import math

import jax
import jax.numpy as jnp
from jax import lax
from jax.sharding import PartitionSpec as P

HEAD_WIDTH = 128
KEY_BLOCK_TOKENS = 128
KEEP = 1


def spread(value, axis, source):
    kept = jnp.where(lax.axis_index(axis) == source, value, 0).astype(value.dtype)
    return lax.psum(kept, axis)


def attend(running, query_heads, scaled, key_part, value_part, visible):
    count = key_part.shape[0]
    kv_dev = query_heads.shape[1]
    key_heads = key_part.reshape(count, kv_dev, HEAD_WIDTH)
    value_heads = value_part.reshape(count, kv_dev, HEAD_WIDTH)
    scores = jnp.einsum(
        "chgd,khd->chgk", query_heads, key_heads, preferred_element_type=jnp.float32
    )
    scores = scores * scaled[None, :, None, None]
    shown = visible[:, None, None, :]
    run_max, run_total, run_acc = running
    new_max = jnp.maximum(run_max, jnp.max(jnp.where(shown, scores, -1e30), -1))
    weights = jnp.where(shown, jnp.exp(scores - new_max[..., None]), 0.0)
    rescale = jnp.exp(run_max - new_max)
    new_total = run_total * rescale + jnp.sum(weights, -1)
    added = jnp.einsum(
        "chgk,khd->chgd",
        weights.astype(jnp.bfloat16),
        value_heads,
        preferred_element_type=jnp.float32,
    )
    return (new_max, new_total, run_acc * rescale[..., None] + added)


def shards(queries, keys, values, key_head_scale, retained, out_weight, norm_gain):
    tok_rows = queries.shape[0]
    kv_dev = keys.shape[1] // HEAD_WIDTH
    query_group_count = queries.shape[1] // keys.shape[1]
    my_index = lax.axis_index("seq")
    query_heads = queries.reshape(tok_rows, kv_dev, query_group_count, HEAD_WIDTH)
    scaled = key_head_scale / math.sqrt(HEAD_WIDTH)
    anchor_keys, anchor_values = (
        spread(keys[:KEY_BLOCK_TOKENS], "seq", 0),
        spread(values[:KEY_BLOCK_TOKENS], "seq", 0),
    )
    leading_row = retained[0, 0] * KEY_BLOCK_TOKENS
    picked_keys = lax.dynamic_slice_in_dim(keys, leading_row, KEY_BLOCK_TOKENS, 0)
    picked_values = lax.dynamic_slice_in_dim(values, leading_row, KEY_BLOCK_TOKENS, 0)
    start_carry = (
        jnp.full((tok_rows, kv_dev, query_group_count), -1e30, jnp.float32),
        jnp.zeros((tok_rows, kv_dev, query_group_count), jnp.float32),
        jnp.zeros((tok_rows, kv_dev, query_group_count, HEAD_WIDTH), jnp.float32),
    )
    anchor_mask = jnp.broadcast_to(my_index > 0, (1, KEY_BLOCK_TOKENS))
    running = attend(start_carry, query_heads, scaled, anchor_keys, anchor_values, anchor_mask)
    causal = jnp.arange(tok_rows)[:, None] >= jnp.arange(tok_rows)[None, :]
    running = attend(running, query_heads, scaled, keys, values, causal)
    piece_keys = lax.all_gather(picked_keys, "seq", axis=0, tiled=True)
    piece_values = lax.all_gather(picked_values, "seq", axis=0, tiled=True)
    owner_dev = jnp.arange(piece_keys.shape[0], dtype=jnp.int32) // (KEEP * KEY_BLOCK_TOKENS)
    running = attend(
        running, query_heads, scaled, piece_keys, piece_values, (owner_dev < my_index)[None, :]
    )
    attended = (running[2] / running[1][..., None]).reshape(tok_rows, -1).astype(jnp.bfloat16)
    product = jnp.dot(attended, out_weight, preferred_element_type=jnp.float32)
    projected = lax.psum(product.astype(jnp.bfloat16), "tp").astype(jnp.float32)
    mean_square = jnp.mean(projected * projected, -1, keepdims=True)
    width_dev = norm_gain.shape[0]
    mine = lax.dynamic_slice_in_dim(projected, lax.axis_index("tp") * width_dev, width_dev, 1)
    normed = mine / jnp.sqrt(mean_square + 1e-05) * norm_gain[None, :]
    return normed.astype(jnp.bfloat16)


def solution(mesh):
    return jax.shard_map(
        shards,
        mesh=mesh,
        in_specs=(
            P("seq", "tp"),
            P("seq", "tp"),
            P("seq", "tp"),
            P("tp"),
            P("seq", None),
            P("tp", None),
            P("tp"),
        ),
        out_specs=P("seq", "tp"),
        check_vma=False,
    )
```

profile of v0, /device:TPU:6, one launch (start us, length us, event | category | flops | bytes accessed | tf_op | source)
XLA Modules:
  0.0 878.4 jit_solution(6002863249122654919)
XLA Ops:
  7.2 1.5 slice_select_fusion.1
  8.7 1.4 constant_dynamic-slice_fusion
  10.2 0.0 all-gather.3.cloned.1.call-start
  10.2 0.7 all-gather.3.cloned.1.call-update
  10.9 0.0 all-gather.5.cloned.1.call-start
  11.0 0.7 copy.24
  11.7 0.0 all-reduce.4.cloned.1.call-start
  12.5 1.1 select_reduce_fusion
  13.7 464.7 %all-reduce.6.cloned.1.call-done = (bf16[128,128]{1,0:T(8,128)(2,1)}, bf16[128,128]{1,0:T(8,128)(2,1)}) async-done(((bf16[128,128]{1,0:T(8,128)(2,1)}, bf16[128,128]{1,0:T(8,128)(2,1)}), (bf16[128,128]{1,0:T(8,128)(2,1)}, bf16[128,128]{1,0:T(8,128)(2,1)})) %all-reduce.6.cloned.1.call-update) | async-done | bytes 65552 | tf_op jit(solution)/shard_map/psum | solution.py:15
  478.4 1.0 select_reduce_fusion.1
  479.4 116.3 %all-gather.3.cloned.1.call-done = bf16[8192,128]{1,0:T(8,128)(2,1)} async-done(((bf16[128,128]{1,0:T(8,128)(2,1)}), bf16[8192,128]{1,0:T(8,128)(2,1)}) %all-gather.3.cloned.1.call-update) | async-done | bytes 2097168 | tf_op jit(solution)/shard_map/all_gather | solution.py:65
  595.7 14.4 %fusion = (f32[256,4]{0,1:T(4,128)S(1)}, f32[8192,256,4]{1,0,2:T(8,128)}) fusion(f32[]{:T(128)} %bitcast.1, pred[8192]{0:T(1024)(128)(4,1)S(1)} %fusion.44, bf16[8192,128]{1,0:T(8,128)(2,1)} %all-gather.3.cloned.1.call-done, bf16[256,512]{1,0:T(8,128)(2,1)S(1)} %copy-done), kind=kOutput, calls=%fused_computation.4 | convolution fusion | flops 2172648448 | bytes 35926020 | tf_op jit(solution)/shard_map/chgd,khd->chgk/dot_general | solution.py:23
  610.1 0.1 bitcast_reduce_fusion.1
  610.2 0.2 fusion.24
  610.4 0.3 convolution_bitcast_fusion
  610.8 14.2 %bitcast_reduce_fusion = f32[256,4]{0,1:T(4,128)S(1)} fusion(f32[8192,256,4]{1,0,2:T(8,128)} %get-tuple-element.19, f32[256,4]{0,1:T(4,128)S(1)} %get-tuple-element.10, f32[]{:T(128)} %bitcast.1, pred[8192]{0:T(1024)(128)(4,1)S(1)} %fusion.44), kind=kLoop, calls=%fused_computation | loop fusion | flops 33553408 | bytes 33570820 | tf_op jit(solution)/shard_map/reduce_sum | solution.py:32
  625.0 87.5 %all-gather.5.cloned.1.call-done = bf16[8192,128]{0,1:T(8,128)(2,1)} async-done(((bf16[128,128]{0,1:T(8,128)(2,1)}), bf16[8192,128]{0,1:T(8,128)(2,1)}) %all-gather.5.cloned.1.call-update) | async-done | bytes 2097168 | tf_op jit(solution)/shard_map/all_gather | solution.py:66
  712.5 14.5 %fusion.12 = f32[1,128,256,4]{2,1,3,0:T(8,128)S(1)} fusion(f32[8192,256,4]{1,0,2:T(8,128)} %get-tuple-element.19, f32[256,4]{0,1:T(4,128)S(1)} %get-tuple-element.10, f32[]{:T(128)} %bitcast.1, pred[8192]{0:T(1024)(128)(4,1)S(1)} %fusion.44, bf16[8192,128]{0,1:T(8,128)(2,1)} %all-gather.5.cloned.1.call-done), kind=kOutput, calls=%fused_computation.21 | convolution fusion | flops 2181038080 | bytes 36188164 | tf_op jit(solution)/shard_map/chgk,khd->chgd/dot_general | solution.py:33
  727.0 0.3 fusion.23
  727.4 2.6 convolution_convert_fusion
  730.0 136.8 %all-reduce.4.cloned.1.call-done = bf16[256,4096]{1,0:T(8,128)(2,1)} async-done(((bf16[256,4096]{1,0:T(8,128)(2,1)}), bf16[256,4096]{1,0:T(8,128)(2,1)}) %all-reduce.4.cloned.1.call-update) | async-done | bytes 2097168 | tf_op jit(solution)/shard_map/psum | solution.py:73
  866.8 2.1 multiply_reduce_fusion
  868.9 2.1 convert_element_type.33
  871.0 0.8 multiply_convert_fusion
  (19 shorter events, 0.2 us)
Async XLA Ops:
  6.5 6.0 copy-start
  6.5 471.8 %all-reduce.6.cloned.1.call-start = ((), (), s32[]{:S(2)}) async-start(), calls=%async_computation.3 | async-start | bytes 131072 | tf_op jit(solution)/shard_map/psum | solution.py:15
  10.2 585.5 %all-gather.3.cloned.1.call-start = ((), (), s32[]{:S(2)}) async-start(), calls=%async_computation | async-start | bytes 2129920 | tf_op jit(solution)/shard_map/all_gather | solution.py:65
  10.9 701.5 %all-gather.5.cloned.1.call-start = ((), (), s32[]{:S(2)}) async-start(), calls=%async_computation.1 | async-start | bytes 2129920 | tf_op jit(solution)/shard_map/all_gather | solution.py:66
  11.7 855.1 %all-reduce.4.cloned.1.call-start = ((), (), s32[]{:S(2)}) async-start(), calls=%async_computation.2 | async-start | bytes 4194304 | tf_op jit(solution)/shard_map/psum | solution.py:73
  479.4 131.1 %copy-start.2 = (bf16[256,128]{1,0:T(8,128)(2,1)S(1)}, bf16[256,128]{1,0:T(8,128)(2,1)}, u32[]{:S(2)}) copy-start(bf16[256,128]{1,0:T(8,128)(2,1)} %param.9) | copy-start | bytes 196612
  625.0 102.1 %copy-start.4 = (bf16[128,128]{1,0:T(8,128)(2,1)S(1)}, bf16[128,128]{1,0:T(8,128)(2,1)}, u32[]{:S(2)}) copy-start(bf16[128,128]{1,0:T(8,128)(2,1)} %get-tuple-element.6) | copy-start | bytes 98308
  712.5 14.9 %copy-start.1 = (bf16[512,4096]{1,0:T(8,128)(2,1)S(1)}, bf16[512,4096]{1,0:T(8,128)(2,1)}, u32[]{:S(2)}) copy-start(bf16[512,4096]{1,0:T(8,128)(2,1)} %param.12) | copy-start | bytes 12582916
  727.0 144.0 %copy-start.3 = (f32[512]{0:T(512)S(1)}, f32[512]{0:T(512)}, u32[]{:S(2)}) copy-start(f32[512]{0:T(512)} %param.13) | copy-start | bytes 6148
Sparse Core Ops, SparseCore 0:
  10.3 467.9 all-reduce.5
  480.7 114.9 all-gather.2
  598.0 114.4 all-gather.4
  730.1 136.6 all-reduce.3
where the time goes:
time: 879 us; the launch traced here: 878 us
  waiting for transfers between devices  806 us (92%)
  matrix products  34.3 us (4%)
  other arithmetic  22.5 us (3%)
  between operations  14.6 us (2%)
    psum x1, waiting for transfers between devices, spread(): return lax.psum(kept, axis)  465 us
    psum x1, waiting for transfers between devices, shards(): projected = lax.psum(product.astype(jnp.bfloat16), 'tp').astype(jnp.float32)  137 us
    all_gather x1, waiting for transfers between devices, shards(): piece_keys = lax.all_gather(picked_keys, 'seq', axis=0, tiled=True)  116 us
    all_gather x1, waiting for transfers between devices, shards(): piece_values = lax.all_gather(picked_values, 'seq', axis=0, tiled=True)  87.5 us
  transfers between devices with their start and end apart: 4, of which 4 were waited for; matrix products, arithmetic and copies ran while one was open for 4% of the time, Pallas kernels for 0%

commit v1 on v0

v1 whole, which is shorter than its diff:
```python
import functools
import math

import jax
import jax.numpy as jnp
from jax import lax
from jax.experimental import pallas as pl
from jax.experimental.pallas import tpu as pltpu
from jax.sharding import PartitionSpec as P

HEAD = 128
BLOCK = 128
LOG2E = math.log2(math.e)
NZ, NY, NC = 4, 8, 2
NX, NH = 4, 2
HEADS = 4
TOK = 256
SLOT = 2 * BLOCK
MSG = NZ * SLOT
LOW = -1e30
F32 = jnp.float32
BF16 = jnp.bfloat16

SMEM = pl.BlockSpec(memory_space=pltpu.SMEM)
VMEM = pl.BlockSpec(memory_space=pltpu.VMEM)
M_SHAPE = jax.ShapeDtypeStruct((HEADS, TOK, HEAD), F32)
ACC_SHAPE = jax.ShapeDtypeStruct((HEADS, TOK, 2 * HEAD), F32)


def sid(z, y, c):
    return (z * NY + y % NY) * NC + c


PLACES = [(z, y, c) for z in range(NZ) for y in range(NY) for c in range(NC)]
LAST = sid(NZ - 1, NY - 1, 1)


def z_perm(k):
    pairs = [(sid(z, y, c), sid(z + k, y, c)) for z, y, c in PLACES if z + k < NZ]
    return pairs + [(LAST, sid(k - 1, NY - 1, 1))]


def y_perm(k):
    return [(sid(z, y, c), sid(z, y + k, c)) for z, y, c in PLACES]


def cross(a, b):
    return lax.dot_general(a, b, (((1,), (1,)), ((), ())), preferred_element_type=F32)


def plain(a, b):
    return lax.dot_general(a, b, (((1,), (0,)), ((), ())), preferred_element_type=F32)


def wide(a, n):
    return jnp.concatenate([a] * n, axis=1)


def seen(me, query_core, key_y):
    z, y, core = me // (NY * NC), (me // NC) % NY, me % NC
    anchor = jnp.logical_and(core == 1, key_y == NY - 1)
    first_piece = (z * NY + y) * NC + query_core == 0
    below = jnp.logical_or(key_y < y, jnp.logical_and(key_y == y, core < query_core))
    own = jnp.where(anchor, jnp.logical_not(first_piece).astype(jnp.int32), below.astype(jnp.int32))
    return [own] + [(z >= k).astype(jnp.int32) for k in range(1, NZ)]


def prepare(blocks, shown, kk, vv):
    first = jnp.int32(0)
    for j in reversed(range(len(shown))):
        first = jnp.where(shown[j] > 0, j, first)
    for j, flag in enumerate(shown):
        src = jnp.where(flag > 0, j, first)
        rows = pl.multiple_of(src * SLOT, SLOT)
        kk[pl.ds(j * BLOCK, BLOCK), :] = blocks[pl.ds(rows, BLOCK), :]
        scale = flag.astype(F32)
        v = blocks[pl.ds(j * SLOT + BLOCK, BLOCK), :].astype(F32) * scale
        vv[pl.ds(j * BLOCK, BLOCK), 0:HEAD] = v.astype(BF16)
        vv[pl.ds(j * BLOCK, BLOCK), HEAD : 2 * HEAD] = jnp.full((BLOCK, HEAD), scale, F32).astype(BF16)


def update(c, q, kk, vv, m_ref, acc_ref, h):
    s = cross(q, kk[...]) * c
    m_old = m_ref[h]
    m_new = jnp.maximum(m_old, jnp.max(s, axis=1, keepdims=True))
    alpha = jnp.exp2(m_old - m_new)
    p = jnp.exp2(s - wide(m_new, s.shape[1] // HEAD)).astype(BF16)
    acc_ref[h] = acc_ref[h] * wide(alpha, 2) + plain(p, vv[...])
    m_ref[h] = m_new


def attend_set(me, core, key_ys, c, q_ref, blocks, kk, vv, m_ref, acc_ref):
    shown = []
    for key_y in key_ys:
        shown += seen(me, core, key_y)
    total = functools.reduce(lambda a, b: a + b, shown)

    @pl.when(total > 0)
    def _():
        prepare(blocks, shown, kk, vv)
        for h in range(HEADS):
            update(c, q_ref[:, h * HEAD : (h + 1) * HEAD], kk, vv, m_ref, acc_ref, h)


def first_kernel(me_ref, c_ref, q0, q1, k_ref, v_ref, blk, m0, a0, m1, a1, blocks, kk, vv, lv):
    me = me_ref[0]
    c = c_ref[0]
    core = me % NC
    lv[:, 0:HEAD] = v_ref[...]
    lv[:, HEAD : 2 * HEAD] = jnp.ones((TOK, HEAD), BF16)
    row = lax.broadcasted_iota(jnp.int32, (TOK, TOK), 0)
    col = lax.broadcasted_iota(jnp.int32, (TOK, TOK), 1)
    for h in range(HEADS):
        s = cross(q0[:, h * HEAD : (h + 1) * HEAD], k_ref[...]) * c
        s = jnp.where(row >= col, s, LOW)
        m = jnp.broadcast_to(jnp.max(s, axis=1, keepdims=True), (TOK, HEAD))
        p = jnp.exp2(s - wide(m, TOK // HEAD)).astype(BF16)
        a0[h] = plain(p, lv[...])
        m0[h] = m
        m1[h] = jnp.full((TOK, HEAD), LOW, F32)
        a1[h] = jnp.zeros((TOK, 2 * HEAD), F32)
    blocks[...] = blk[...]
    y = (me // NC) % NY
    attend_set(me, core, [y], c, q0, blocks, kk, vv, m0, a0)
    attend_set(me, 1 - core, [y], c, q1, blocks, kk, vv, m1, a1)


def ring_kernel(step, me_ref, c_ref, q0, q1, fwd, bwd, m0i, a0i, m1i, a1i, m0, a0, m1, a1, blocks, kk, vv):
    me = me_ref[0]
    c = c_ref[0]
    core = me % NC
    y = (me // NC) % NY
    m0[...] = m0i[...]
    a0[...] = a0i[...]
    m1[...] = m1i[...]
    a1[...] = a1i[...]
    blocks[0:MSG, :] = fwd[...]
    blocks[MSG : 2 * MSG, :] = bwd[...]
    key_ys = [(y + NY - step) % NY, (y + step) % NY]
    attend_set(me, core, key_ys, c, q0, blocks, kk, vv, m0, a0)
    attend_set(me, 1 - core, key_ys, c, q1, blocks, kk, vv, m1, a1)


def last_kernel(other, me_ref, c_ref, q, blk, mi, ai, *rest):
    if other:
        out, m, a, kk, vv = rest
    else:
        m, a, kk, vv = rest
    me = me_ref[0]
    core = me % NC
    y = (me // NC) % NY
    m[...] = mi[...]
    a[...] = ai[...]
    key_ys = [(y + NY // 2) % NY]
    attend_set(me, 1 - core if other else core, key_ys, c_ref[0], q, blk, kk, vv, m, a)
    if other:
        lane = lax.broadcasted_iota(jnp.int32, (TOK, HEAD), 1)
        for h in range(HEADS):
            total = a[h][:, HEAD:]
            some = total > 0.0
            safe = jnp.where(some, total, 1.0)
            out[h, :, 0:HEAD] = (a[h][:, :HEAD] / safe).astype(BF16)
            lse = jnp.where(some, m[h] + jnp.log2(safe), LOW)
            hi = lse.astype(BF16).astype(F32)
            mid = (lse - hi).astype(BF16).astype(F32)
            low = lse - hi - mid
            parts = jnp.where(lane == 0, hi, jnp.where(lane == 1, mid, low))
            out[h, :, HEAD : 2 * HEAD] = parts.astype(BF16)


def merge_kernel(tp_ref, m, a, got, w, att, out):
    @pl.when(pl.program_id(0) == 0)
    def _():
        for h in range(HEADS):
            parts = got[h][:, HEAD:].astype(F32)
            lse = (parts[:, 0:1] + parts[:, 1:2]) + parts[:, 2:3]
            mine = m[h]
            top = jnp.maximum(mine, lse)
            w0 = jnp.exp2(mine - top)
            w1 = jnp.exp2(lse - top)
            acc = a[h][:, :HEAD] * w0 + got[h][:, :HEAD].astype(F32) * w1
            total = a[h][:, HEAD:] * w0 + w1
            att[:, h * HEAD : (h + 1) * HEAD] = (acc / total).astype(BF16)

    out[0] = plain(att[...], w[...]).astype(BF16)


def rest_kernel(tp_ref, att, w, out):
    out[0] = plain(att[...], w[...]).astype(BF16)


def params(mib=48):
    return pltpu.CompilerParams(vmem_limit_bytes=mib << 20)


def scratch(n):
    return [pltpu.VMEM((n * BLOCK, HEAD), BF16), pltpu.VMEM((n * BLOCK, 2 * HEAD), BF16)]


def cost(keys, sets):
    rows = HEADS * TOK * sets
    return pl.CostEstimate(
        flops=rows * keys * HEAD * 6, bytes_accessed=4 << 20, transcendentals=rows * keys
    )


def shards(queries, keys, values, key_head_scale, retained, out_weight, norm_gain):
    me = lax.axis_index("seq").astype(jnp.int32)
    tp = lax.axis_index("tp").astype(jnp.int32)
    core, y, z = me % NC, (me // NC) % NY, me // (NC * NY)
    hi = tp // NX
    me_s = me.reshape(1)
    tp_s = tp.reshape(1)
    c = key_head_scale * (LOG2E / math.sqrt(HEAD))

    anchor = jnp.concatenate([keys[:BLOCK], values[:BLOCK]], 0)
    anchor_far = lax.ppermute(anchor, "seq", [(0, LAST)])
    other_queries = lax.ppermute(queries, "seq", [(sid(*s), sid(s[0], s[1], 1 - s[2])) for s in PLACES])
    row = retained[0, 0] * BLOCK
    own = jnp.concatenate(
        [
            lax.dynamic_slice_in_dim(keys, row, BLOCK, 0),
            lax.dynamic_slice_in_dim(values, row, BLOCK, 0),
        ],
        0,
    )
    own = jnp.where(me == LAST, anchor_far, own)
    up = [lax.ppermute(own, "seq", z_perm(k)) for k in range(1, NZ)]
    far = jnp.where(z == 0, up[0], jnp.where(z == 1, up[1], jnp.where(z == 2, up[2], own)))
    slot = jnp.where(jnp.logical_and(y == NY - 1, core == 1), far, own)
    block = jnp.concatenate([slot] + up, 0)

    fwd = [lax.ppermute(block, "seq", y_perm(1))]
    bwd = [lax.ppermute(block, "seq", y_perm(-1))]
    for _ in range(2):
        fwd.append(lax.ppermute(fwd[-1], "seq", y_perm(1)))
        bwd.append(lax.ppermute(bwd[-1], "seq", y_perm(-1)))
    turn = [(sid(z_, y_, c_), sid(z_, y_ + (1 if c_ == 0 else -1), c_)) for z_, y_, c_ in PLACES]
    half = lax.ppermute(jnp.where(core == 0, fwd[-1], bwd[-1]), "seq", turn)

    state_shapes = [M_SHAPE, ACC_SHAPE, M_SHAPE, ACC_SHAPE]
    state = pl.pallas_call(
        first_kernel,
        out_shape=state_shapes,
        in_specs=[SMEM, SMEM] + [VMEM] * 5,
        out_specs=[VMEM] * 4,
        scratch_shapes=[pltpu.VMEM((MSG, HEAD), BF16)] + scratch(4) + [pltpu.VMEM((TOK, 2 * HEAD), BF16)],
        compiler_params=params(),
        cost_estimate=cost(640, 2),
        name="attend_own_chip",
    )(me_s, c, queries, other_queries, keys, values, block)
    for step in range(1, 4):
        state = pl.pallas_call(
            functools.partial(ring_kernel, step),
            out_shape=state_shapes,
            in_specs=[SMEM, SMEM] + [VMEM] * 8,
            out_specs=[VMEM] * 4,
            scratch_shapes=[pltpu.VMEM((2 * MSG, HEAD), BF16)] + scratch(8),
            input_output_aliases={6: 0, 7: 1, 8: 2, 9: 3},
            compiler_params=params(),
            cost_estimate=cost(1024, 2),
            name="attend_ring",
        )(me_s, c, queries, other_queries, fwd[step - 1], bwd[step - 1], *state)
    m0, a0, m1, a1 = state
    message, _, _ = pl.pallas_call(
        functools.partial(last_kernel, True),
        out_shape=[jax.ShapeDtypeStruct((HEADS, TOK, 2 * HEAD), BF16), M_SHAPE, ACC_SHAPE],
        in_specs=[SMEM, SMEM] + [VMEM] * 4,
        out_specs=[VMEM] * 3,
        scratch_shapes=scratch(4),
        input_output_aliases={4: 1, 5: 2},
        compiler_params=params(),
        cost_estimate=cost(512, 1),
        name="attend_last_other",
    )(me_s, c, other_queries, half, m1, a1)
    got = lax.ppermute(message, "seq", [(sid(*s), sid(s[0], s[1], 1 - s[2])) for s in PLACES])
    m0, a0 = pl.pallas_call(
        functools.partial(last_kernel, False),
        out_shape=[M_SHAPE, ACC_SHAPE],
        in_specs=[SMEM, SMEM] + [VMEM] * 4,
        out_specs=[VMEM] * 2,
        scratch_shapes=scratch(4),
        input_output_aliases={4: 0, 5: 1},
        compiler_params=params(),
        cost_estimate=cost(512, 1),
        name="attend_last_own",
    )(me_s, c, queries, half, m0, a0)

    wide_cols = out_weight.shape[1] // (NX * NH)

    def far_cols(i, tp_ref):
        return (0, i * NX + (tp_ref[0] + 2) % NX)

    def rest_cols(i, tp_ref):
        g = i // 2
        d = jnp.where(g == 2, 0, 1 + 2 * g)
        return (0, (i % 2) * NX + (tp_ref[0] + d) % NX)

    whole = lambda *shape: pl.BlockSpec(shape, lambda i, tp_ref: (0,) * len(shape))
    att, far_part = pl.pallas_call(
        merge_kernel,
        out_shape=[
            jax.ShapeDtypeStruct((TOK, HEADS * HEAD), BF16),
            jax.ShapeDtypeStruct((2, TOK, wide_cols), BF16),
        ],
        grid_spec=pltpu.PrefetchScalarGridSpec(
            num_scalar_prefetch=1,
            grid=(2,),
            in_specs=[
                whole(HEADS, TOK, HEAD),
                whole(HEADS, TOK, 2 * HEAD),
                whole(HEADS, TOK, 2 * HEAD),
                pl.BlockSpec((HEADS * HEAD, wide_cols), far_cols),
            ],
            out_specs=[
                whole(TOK, HEADS * HEAD),
                pl.BlockSpec((1, TOK, wide_cols), lambda i, tp_ref: (i, 0, 0)),
            ],
        ),
        compiler_params=params(),
        cost_estimate=pl.CostEstimate(flops=1 << 28, bytes_accessed=5 << 20, transcendentals=1 << 18),
        name="merge_project",
    )(tp_s, m0, a0, got, out_weight)
    right = [(i, (i // NX) * NX + (i + 1) % NX) for i in range(NX * NH)]
    left = [(i, (i // NX) * NX + (i + NX - 1) % NX) for i in range(NX * NH)]
    from_left = lax.ppermute(far_part[0], "tp", right)
    from_right = lax.ppermute(far_part[1], "tp", left)
    rest = pl.pallas_call(
        rest_kernel,
        out_shape=jax.ShapeDtypeStruct((6, TOK, wide_cols), BF16),
        grid_spec=pltpu.PrefetchScalarGridSpec(
            num_scalar_prefetch=1,
            grid=(6,),
            in_specs=[
                whole(TOK, HEADS * HEAD),
                pl.BlockSpec((HEADS * HEAD, wide_cols), rest_cols),
            ],
            out_specs=pl.BlockSpec((1, TOK, wide_cols), lambda i, tp_ref: (i, 0, 0)),
        ),
        compiler_params=params(),
        cost_estimate=pl.CostEstimate(flops=3 << 28, bytes_accessed=5 << 20, transcendentals=0),
        name="project_rest",
    )(tp_s, att, out_weight)
    to_right = jnp.stack([rest[0] + from_left, rest[1]])
    to_left = jnp.stack([rest[2], rest[3] + from_right])
    from_left = lax.ppermute(to_right, "tp", right)
    from_right = lax.ppermute(to_left, "tp", left)
    summed = rest[4:6].astype(F32) + from_left.astype(F32) + from_right.astype(F32)
    send = jnp.where(hi == 0, summed[1], summed[0]).astype(BF16)
    keep = jnp.where(hi == 0, summed[0], summed[1])
    swap = [(i, (i + NX) % (NX * NH)) for i in range(NX * NH)]
    projected = keep + lax.ppermute(send, "tp", swap).astype(F32)
    squares = jnp.sum(projected * projected, -1)
    squares = lax.psum(squares, "tp", axis_index_groups=[list(range(NX)), list(range(NX, 2 * NX))])
    squares = lax.psum(squares, "tp", axis_index_groups=[[i, i + NX] for i in range(NX)])
    mean_square = squares[:, None] / out_weight.shape[1]
    return (projected * lax.rsqrt(mean_square + 1e-05) * norm_gain[None, :]).astype(BF16)


def solution(mesh):
    return jax.shard_map(
        shards,
        mesh=mesh,
        in_specs=(
            P("seq", "tp"),
            P("seq", "tp"),
            P("seq", "tp"),
            P("tp"),
            P("seq", None),
            P("tp", None),
            P("tp"),
        ),
        out_specs=P("seq", "tp"),
        check_vma=False,
    )
```

time: 879 us -> 148 us (0.17)
  the two profiles are of different devices: /device:TPU:6 before, /device:TPU:200 now
where the time goes in v1:
time: 148 us; the launch traced here: 147 us
  starting transfers between devices  59.8 us (40%)
  waiting for transfers between devices  35.7 us (24%)
  Pallas kernels  22.8 us (15%)
  blocking collectives  19.6 us (13%)
  local copies, waits for them, and re-layouts  4.94 us (3%)
  other arithmetic  2.55 us (2%)
  between operations  1.82 us (1%)
    pallas_call x3, Pallas kernels, shards(): pl.pallas_call(functools.partial(ring_kernel, step), out_shape=state_shap...  12.4 us
    psum x1, blocking collectives, shards(): lax.psum(squares, 'tp', axis_index_groups=[list(range(NX)), list(range(NX...  10.7 us
    ppermute x1, waiting for transfers between devices, shards(): projected = keep + lax.ppermute(send, 'tp', swap).astype(F32)  9.98 us
    ppermute x2, starting transfers between devices, shards(): bwd.append(lax.ppermute(bwd[-1], 'seq', y_perm(-1)))  9.7 us
    ppermute x1, waiting for transfers between devices, shards(): from_left = lax.ppermute(to_right, 'tp', right)  9.03 us
    psum x1, blocking collectives, shards(): lax.psum(squares, 'tp', axis_index_groups=[[i, i + NX] for i in range(NX)])  8.83 us
    ppermute x1, starting transfers between devices, shards(): projected = keep + lax.ppermute(send, 'tp', swap).astype(F32)  8.22 us
    ppermute x3, waiting for transfers between devices, shards(): up = [lax.ppermute(own, 'seq', z_perm(k)) for k in range(1, NZ)]  7.81 us
  transfers between devices with their start and end apart: 18, of which 10 were waited for; matrix products, arithmetic and copies ran while one was open for 0% of the time, Pallas kernels for 13%

profile of v1, /device:TPU:200, one launch (start us, length us, event | category | flops | bytes accessed | tf_op | source)
XLA Modules:
  0.0 147.2 jit_solution(5258903179887534934)
XLA Ops:
  10.6 3.4 %collective-permute-done.3 = bf16[256,128]{1,0:T(8,128)(2,1)S(1)} collective-permute-done((bf16[256,128]{1,0:T(8,128)(2,1)S(1)}, bf16[256,128]{1,0:T(8,128)(2,1)S(1)}, u32[]{:S(2)}, u32[]{:S(2)}) %collective-permute-start.3) | collective-permute-done | bytes 65568 | tf_op jit(solution)/shard_map/ppermute | solution.py:228
  14.0 3.5 %collective-permute-start.4 = (bf16[1024,128]{1,0:T(8,128)(2,1)S(1)}, bf16[1024,128]{1,0:T(8,128)(2,1)S(1)}, u32[]{:S(2)}, u32[]{:S(2)}) collective-permute-start(bf16[1024,128]{1,0:T(8,128)(2,1)S(1)} %pad_maximum_fusion.2.blk), channel_id=1, source_target_pairs={{0,16},{8,24},{16,32},{24,40},{32,48},{40,56},{48,64},{56,72},{64,... | collective-permute-start | bytes 786440 | tf_op jit(solution)/shard_map/ppermute | solution.py:233
  17.5 4.4 %collective-permute-start.7 = (bf16[1024,128]{1,0:T(8,128)(2,1)S(1)}, bf16[1024,128]{1,0:T(8,128)(2,1)S(1)}, u32[]{:S(2)}, u32[]{:S(2)}) collective-permute-start(bf16[1024,128]{1,0:T(8,128)(2,1)S(1)} %pad_maximum_fusion.2.blk), channel_id=1, source_target_pairs={{0,112},{8,120},{16,0},{24,8},{32,16},{40,24},{48,32},{56,40},{64,... | collective-permute-start | bytes 786440 | tf_op jit(solution)/shard_map/ppermute | solution.py:234
  22.0 2.4 %collective-permute-done.4.fwd = bf16[1024,128]{1,0:T(8,128)(2,1)S(1)} collective-permute-done((bf16[1024,128]{1,0:T(8,128)(2,1)S(1)}, bf16[1024,128]{1,0:T(8,128)(2,1)S(1)}, u32[]{:S(2)}, u32[]{:S(2)}) %collective-permute-start.4) | collective-permute-done | bytes 262176 | tf_op jit(solution)/shard_map/ppermute | solution.py:233
  27.3 4.9 %collective-permute-start.8 = (bf16[1024,128]{1,0:T(8,128)(2,1)S(1)}, bf16[1024,128]{1,0:T(8,128)(2,1)S(1)}, u32[]{:S(2)}, u32[]{:S(2)}) collective-permute-start(bf16[1024,128]{1,0:T(8,128)(2,1)S(1)} %collective-permute-done.7.bwd), channel_id=1, source_target_pairs={{0,112},{8,120},{16,0},{24,8},{32,16},{40,24},{48,32},{56,40},{64,... | collective-permute-start | bytes 786440 | tf_op jit(solution)/shard_map/ppermute | solution.py:237
  32.8 5.0 %collective-permute-start.11 = (bf16[256,512]{1,0:T(8,128)(2,1)}, bf16[256,512]{1,0:T(8,128)(2,1)S(1)}, u32[]{:S(2)}, u32[]{:S(2)}) collective-permute-start(bf16[256,512]{1,0:T(8,128)(2,1)} %q.1), channel_id=1, source_target_pairs={{0,8},{8,0},{16,24},{24,16},{32,40},{40,32},{48,56},{56,48},{64,72... | collective-permute-start | bytes 786440 | tf_op jit(solution)/shard_map/ppermute | solution.py:218
  39.8 4.9 %collective-permute-start.9 = (bf16[1024,128]{1,0:T(8,128)(2,1)S(1)}, bf16[1024,128]{1,0:T(8,128)(2,1)S(1)}, u32[]{:S(2)}, u32[]{:S(2)}) collective-permute-start(bf16[1024,128]{1,0:T(8,128)(2,1)S(1)} %collective-permute-done.8.bwd), channel_id=1, source_target_pairs={{0,112},{8,120},{16,0},{24,8},{32,16},{40,24},{48,32},{56,40},{64,... | collective-permute-start | bytes 786440 | tf_op jit(solution)/shard_map/ppermute | solution.py:237
  47.9 2.8 %attend_own_chip.1 = (f32[4,256,128]{2,1,0:T(8,128)S(1)}, f32[4,256,256]{2,1,0:T(8,128)S(1)}, f32[4,256,128]{2,1,0:T(8,128)S(1)}, f32[4,256,256]{2,1,0:T(8,128)S(1)}) custom-call(s32[1]{0:T(128)} %bitcast.1.me_ref, f32[1]{0:T(128)S(6)} %mul.28.c_ref, bf16[256,512]{1,0:T(8,128)(2,1)S(1)} %copy-done.1, bf16[256,512]{1,0:T(8,128)(2,1)S(1)} %collective-permute-done.11.q1.q, ...), custom_call_target="tpu_custom_call" | custom-call | flops 1006632960 | bytes 4194304 | tf_op jit(solution)/shard_map/attend_own_chip/pallas_call | solution.py:242
  50.7 4.1 %attend_ring.3 = (f32[4,256,128]{2,1,0:T(8,128)S(1)}, f32[4,256,256]{2,1,0:T(8,128)S(1)}, f32[4,256,128]{2,1,0:T(8,128)S(1)}, f32[4,256,256]{2,1,0:T(8,128)S(1)}) custom-call(s32[1]{0:T(128)} %bitcast.1.me_ref, f32[1]{0:T(128)S(6)} %mul.28.c_ref, ...), custom_call_target="tpu_custom_call", output_to_operand_aliasing={{0}: (6, {}), {1}: (7, {}), {2}: (8, {}), {3}: (9, {})} | custom-call | flops 1610612736 | bytes 4194304 | tf_op jit(solution)/shard_map/attend_ring/pallas_call | solution.py:253
  56.8 4.1 %attend_ring.4 = (f32[4,256,128]{2,1,0:T(8,128)S(1)}, f32[4,256,256]{2,1,0:T(8,128)S(1)}, f32[4,256,128]{2,1,0:T(8,128)S(1)}, f32[4,256,256]{2,1,0:T(8,128)S(1)}) custom-call(s32[1]{0:T(128)} %bitcast.1.me_ref, f32[1]{0:T(128)S(6)} %mul.28.c_ref, ...), custom_call_target="tpu_custom_call", output_to_operand_aliasing={{0}: (6, {}), {1}: (7, {}), {2}: (8, {}), {3}: (9, {})} | custom-call | flops 1610612736 | bytes 4194304 | tf_op jit(solution)/shard_map/attend_ring/pallas_call | solution.py:253
  60.9 4.3 %attend_ring.5 = (f32[4,256,128]{2,1,0:T(8,128)S(1)}, f32[4,256,256]{2,1,0:T(8,128)S(1)}, f32[4,256,128]{2,1,0:T(8,128)S(1)}, f32[4,256,256]{2,1,0:T(8,128)S(1)}) custom-call(s32[1]{0:T(128)} %bitcast.1.me_ref, f32[1]{0:T(128)S(6)} %mul.28.c_ref, ...), custom_call_target="tpu_custom_call", output_to_operand_aliasing={{0}: (6, {}), {1}: (7, {}), {2}: (8, {}), {3}: (9, {})} | custom-call | flops 1610612736 | bytes 4194304 | tf_op jit(solution)/shard_map/attend_ring/pallas_call | solution.py:253
  66.8 4.3 %collective-permute-start.12 = (bf16[4,256,256]{2,1,0:T(8,128)(2,1)S(1)}, bf16[4,256,256]{2,1,0:T(8,128)(2,1)S(1)}, u32[]{:S(2)}, u32[]{:S(2)}) collective-permute-start(bf16[4,256,256]{2,1,0:T(8,128)(2,1)S(1)} %get-tuple-element.44), channel_id=1, source_target_pairs={{0,8},{8,0},{16,24},{24,16},{32,40},{40,32},{48,56},{56,48},{64,72... | collective-permute-start | bytes 1572872 | tf_op jit(solution)/shard_map/ppermute | solution.py:276
  72.6 2.5 %merge_project.1 = (bf16[256,512]{1,0:T(8,128)(2,1)S(1)}, bf16[2,256,512]{2,1,0:T(8,128)(2,1)S(1)}) custom-call(s32[1]{0:T(128)} %bitcast.tp_ref, f32[4,256,128]{2,1,0:T(8,128)S(1)} %get-tuple-element.40.m, f32[4,256,256]{2,1,0:T(8,128)S(1)} %get-tuple-element.41.a, bf16[4,256,256]{2,1,0:T(8,128)(2,1)S(1)} %collective-permute-done.12.got, bf16[512,4096]{1,0:T(8,128)(2,1)} %w.3), custom_call_target="tpu_custom_call" | custom-call | flops 268435456 | bytes 5242880 | tf_op jit(solution)/shard_map/merge_project/pallas_call | solution.py:300
  75.1 3.4 %collective-permute-start.13 = (bf16[256,512]{1,0:T(8,128)(2,1)S(1)}, bf16[256,512]{1,0:T(8,128)(2,1)S(1)}, u32[]{:S(2)}, u32[]{:S(2)}) collective-permute-start(bf16[256,512]{1,0:T(8,128)(2,1)S(1)} %get-tuple-element.51), channel_id=1, source_target_pairs={{0,1},{1,2},{2,3},{3,0},{4,5},{5,6},{6,7},{7,4},{8,9},{9,10},{10,1... | collective-permute-start | bytes 786440 | tf_op jit(solution)/shard_map/ppermute | solution.py:326
  78.5 3.6 %collective-permute-start.15 = (bf16[256,512]{1,0:T(8,128)(2,1)S(1)}, bf16[256,512]{1,0:T(8,128)(2,1)S(1)}, u32[]{:S(2)}, u32[]{:S(2)}) collective-permute-start(bf16[256,512]{1,0:T(8,128)(2,1)S(1)} %get-tuple-element.52), channel_id=1, source_target_pairs={{0,3},{1,0},{2,1},{3,2},{4,7},{5,4},{6,5},{7,6},{8,11},{9,8},{10,9... | collective-permute-start | bytes 786440 | tf_op jit(solution)/shard_map/ppermute | solution.py:327
  82.2 2.3 %project_rest.1 = bf16[6,256,512]{2,1,0:T(8,128)(2,1)S(1)} custom-call(s32[1]{0:T(128)} %bitcast.tp_ref, bf16[256,512]{1,0:T(8,128)(2,1)S(1)} %get-tuple-element.45.att, bf16[512,4096]{1,0:T(8,128)(2,1)S(1)} %copy-done), custom_call_target="tpu_custom_call" | custom-call | flops 805306368 | bytes 5242880 | tf_op jit(solution)/shard_map/project_rest/pallas_call | solution.py:328
  84.6 2.2 %collective-permute-done.13 = bf16[256,512]{1,0:T(8,128)(2,1)S(1)} collective-permute-done((bf16[256,512]{1,0:T(8,128)(2,1)S(1)}, bf16[256,512]{1,0:T(8,128)(2,1)S(1)}, u32[]{:S(2)}, u32[]{:S(2)}) %collective-permute-start.13) | collective-permute-done | bytes 262176 | tf_op jit(solution)/shard_map/ppermute | solution.py:326
  88.9 3.4 %collective-permute-start.14 = (bf16[2,256,512]{2,1,0:T(8,128)(2,1)S(1)}, bf16[2,256,512]{2,1,0:T(8,128)(2,1)S(1)}, u32[]{:S(2)}, u32[]{:S(2)}) collective-permute-start(bf16[2,256,512]{2,1,0:T(8,128)(2,1)S(1)} %pad_maximum_fusion), channel_id=1, source_target_pairs={{0,1},{1,2},{2,3},{3,0},{4,5},{5,6},{6,7},{7,4},{8,9},{9,10},{10,1... | collective-permute-start | bytes 1572872 | tf_op jit(solution)/shard_map/ppermute | solution.py:346
  92.3 3.7 %collective-permute-start.16 = (bf16[2,256,512]{2,1,0:T(8,128)(2,1)S(1)}, bf16[2,256,512]{2,1,0:T(8,128)(2,1)}, u32[]{:S(2)}, u32[]{:S(2)}) collective-permute-start(bf16[2,256,512]{2,1,0:T(8,128)(2,1)S(1)} %pad_maximum_fusion.1), channel_id=1, source_target_pairs={{0,3},{1,0},{2,1},{3,2},{4,7},{5,4},{6,5},{7,6},{8,11},{9,8},{10,9... | collective-permute-start | bytes 1572872 | tf_op jit(solution)/shard_map/ppermute | solution.py:347
  96.0 9.0 %collective-permute-done.14 = bf16[2,256,512]{2,1,0:T(8,128)(2,1)S(1)} collective-permute-done((bf16[2,256,512]{2,1,0:T(8,128)(2,1)S(1)}, bf16[2,256,512]{2,1,0:T(8,128)(2,1)S(1)}, u32[]{:S(2)}, u32[]{:S(2)}) %collective-permute-start.14) | collective-permute-done | bytes 524320 | tf_op jit(solution)/shard_map/ppermute | solution.py:346
  108.4 8.2 %collective-permute-start.17 = (bf16[256,512]{1,0:T(8,128)(2,1)S(1)}, bf16[256,512]{1,0:T(8,128)(2,1)S(1)}, u32[]{:S(2)}, u32[]{:S(2)}) collective-permute-start(bf16[256,512]{1,0:T(8,128)(2,1)S(1)} %fusion), channel_id=1, source_target_pairs={{0,4},{1,5},{2,6},{3,7},{4,0},{5,1},{6,2},{7,3},{8,12},{9,13},{10,... | collective-permute-start | bytes 786440 | tf_op jit(solution)/shard_map/ppermute | solution.py:352
  116.7 10.0 %collective-permute-done.17 = bf16[256,512]{1,0:T(8,128)(2,1)S(1)} collective-permute-done((bf16[256,512]{1,0:T(8,128)(2,1)S(1)}, bf16[256,512]{1,0:T(8,128)(2,1)S(1)}, u32[]{:S(2)}, u32[]{:S(2)}) %collective-permute-start.17) | collective-permute-done | bytes 262176 | tf_op jit(solution)/shard_map/ppermute | solution.py:352
  126.8 10.7 %psum.14 = f32[256]{0:T(256)S(1)} all-reduce(f32[256]{0:T(256)S(1)} %multiply_reduce_fusion), channel_id=1, replica_groups={{0,1,2,3},{4,5,6,7},{8,9,10,11},{12,13,14,15},{16,17,18,19},{20,21,22,2..., use_global_device_ids=true, to_apply=%region_1.2 | all-reduce | flops 256 | bytes 2048 | tf_op jit(solution)/shard_map/psum | solution.py:354
  137.5 8.8 %psum.15 = f32[256]{0:T(256)S(1)} all-reduce(f32[256]{0:T(256)S(1)} %psum.14), channel_id=1, replica_groups={{0,4},{1,5},{2,6},{3,7},{8,12},{9,13},{10,14},{11,15},{16,20},{17,21},{..., use_global_device_ids=true, to_apply=%region_2.3 | all-reduce | flops 256 | bytes 2048 | tf_op jit(solution)/shard_map/psum | solution.py:355
  (58 shorter events, 29.6 us)
Async XLA Ops:
  1.5 0.7 collective-permute-start
  2.2 6.2 %collective-permute-start.1 = (bf16[256,128]{1,0:T(8,128)(2,1)S(1)}, bf16[256,128]{1,0:T(8,128)(2,1)S(1)}, u32[]{:S(2)}, u32[]{:S(2)}) collective-permute-start(bf16[256,128]{1,0:T(8,128)(2,1)S(1)} %maximum_select_fusion), channel_id=1, source_target_pairs={{0,128},{8,136},{16,144},{24,152},{32,160},{40,168},{48,176},{56,1... | collective-permute-start | bytes 196616 | tf_op jit(solution)/shard_map/ppermute | solution.py:228
  3.5 7.1 %collective-permute-start.2 = (bf16[256,128]{1,0:T(8,128)(2,1)S(1)}, bf16[256,128]{1,0:T(8,128)(2,1)S(1)}, u32[]{:S(2)}, u32[]{:S(2)}) collective-permute-start(bf16[256,128]{1,0:T(8,128)(2,1)S(1)} %maximum_select_fusion), channel_id=1, source_target_pairs={{0,256},{8,264},{16,272},{24,280},{32,288},{40,296},{48,304},{56,3... | collective-permute-start | bytes 196616 | tf_op jit(solution)/shard_map/ppermute | solution.py:228
  4.8 9.2 %collective-permute-start.3 = (bf16[256,128]{1,0:T(8,128)(2,1)S(1)}, bf16[256,128]{1,0:T(8,128)(2,1)S(1)}, u32[]{:S(2)}, u32[]{:S(2)}) collective-permute-start(bf16[256,128]{1,0:T(8,128)(2,1)S(1)} %maximum_select_fusion), channel_id=1, source_target_pairs={{0,384},{8,392},{16,400},{24,408},{32,416},{40,424},{48,432},{56,4... | collective-permute-start | bytes 196616 | tf_op jit(solution)/shard_map/ppermute | solution.py:228
  14.0 10.3 %collective-permute-start.4 = (bf16[1024,128]{1,0:T(8,128)(2,1)S(1)}, bf16[1024,128]{1,0:T(8,128)(2,1)S(1)}, u32[]{:S(2)}, u32[]{:S(2)}) collective-permute-start(bf16[1024,128]{1,0:T(8,128)(2,1)S(1)} %pad_maximum_fusion.2.blk), channel_id=1, source_target_pairs={{0,16},{8,24},{16,32},{24,40},{32,48},{40,56},{48,64},{56,72},{64,... | collective-permute-start | bytes 786440 | tf_op jit(solution)/shard_map/ppermute | solution.py:233
  17.5 9.7 %collective-permute-start.7 = (bf16[1024,128]{1,0:T(8,128)(2,1)S(1)}, bf16[1024,128]{1,0:T(8,128)(2,1)S(1)}, u32[]{:S(2)}, u32[]{:S(2)}) collective-permute-start(bf16[1024,128]{1,0:T(8,128)(2,1)S(1)} %pad_maximum_fusion.2.blk), channel_id=1, source_target_pairs={{0,112},{8,120},{16,0},{24,8},{32,16},{40,24},{48,32},{56,40},{64,... | collective-permute-start | bytes 786440 | tf_op jit(solution)/shard_map/ppermute | solution.py:234
  24.4 13.5 %collective-permute-start.5 = (bf16[1024,128]{1,0:T(8,128)(2,1)S(1)}, bf16[1024,128]{1,0:T(8,128)(2,1)S(1)}, u32[]{:S(2)}, u32[]{:S(2)}) collective-permute-start(bf16[1024,128]{1,0:T(8,128)(2,1)S(1)} %collective-permute-done.4.fwd), channel_id=1, source_target_pairs={{0,16},{8,24},{16,32},{24,40},{32,48},{40,56},{48,64},{56,72},{64,... | collective-permute-start | bytes 786440 | tf_op jit(solution)/shard_map/ppermute | solution.py:236
  27.3 12.5 %collective-permute-start.8 = (bf16[1024,128]{1,0:T(8,128)(2,1)S(1)}, bf16[1024,128]{1,0:T(8,128)(2,1)S(1)}, u32[]{:S(2)}, u32[]{:S(2)}) collective-permute-start(bf16[1024,128]{1,0:T(8,128)(2,1)S(1)} %collective-permute-done.7.bwd), channel_id=1, source_target_pairs={{0,112},{8,120},{16,0},{24,8},{32,16},{40,24},{48,32},{56,40},{64,... | collective-permute-start | bytes 786440 | tf_op jit(solution)/shard_map/ppermute | solution.py:237
  32.8 12.5 %collective-permute-start.11 = (bf16[256,512]{1,0:T(8,128)(2,1)}, bf16[256,512]{1,0:T(8,128)(2,1)S(1)}, u32[]{:S(2)}, u32[]{:S(2)}) collective-permute-start(bf16[256,512]{1,0:T(8,128)(2,1)} %q.1), channel_id=1, source_target_pairs={{0,8},{8,0},{16,24},{24,16},{32,40},{40,32},{48,56},{56,48},{64,72... | collective-permute-start | bytes 786440 | tf_op jit(solution)/shard_map/ppermute | solution.py:218
  37.8 17.0 %collective-permute-start.6 = (bf16[1024,128]{1,0:T(8,128)(2,1)S(1)}, bf16[1024,128]{1,0:T(8,128)(2,1)S(1)}, u32[]{:S(2)}, u32[]{:S(2)}) collective-permute-start(bf16[1024,128]{1,0:T(8,128)(2,1)S(1)} %collective-permute-done.5.fwd), channel_id=1, source_target_pairs={{0,16},{8,24},{16,32},{24,40},{32,48},{40,56},{48,64},{56,72},{64,... | collective-permute-start | bytes 786440 | tf_op jit(solution)/shard_map/ppermute | solution.py:236
  39.8 15.1 %collective-permute-start.9 = (bf16[1024,128]{1,0:T(8,128)(2,1)S(1)}, bf16[1024,128]{1,0:T(8,128)(2,1)S(1)}, u32[]{:S(2)}, u32[]{:S(2)}) collective-permute-start(bf16[1024,128]{1,0:T(8,128)(2,1)S(1)} %collective-permute-done.8.bwd), channel_id=1, source_target_pairs={{0,112},{8,120},{16,0},{24,8},{32,16},{40,24},{48,32},{56,40},{64,... | collective-permute-start | bytes 786440 | tf_op jit(solution)/shard_map/ppermute | solution.py:237
  45.3 1.0 copy-start.1
  47.9 2.8 %copy-start.6 = (bf16[1024,128]{1,0:T(8,128)(2,1)S(1)}, bf16[1024,128]{1,0:T(8,128)(2,1)}, u32[]{:S(2)}) copy-start(bf16[1024,128]{1,0:T(8,128)(2,1)} %copy-done.5) | copy-start | bytes 786436
  47.9 2.8 %copy-start.8 = (bf16[1024,128]{1,0:T(8,128)(2,1)S(1)}, bf16[1024,128]{1,0:T(8,128)(2,1)}, u32[]{:S(2)}) copy-start(bf16[1024,128]{1,0:T(8,128)(2,1)} %copy-done.7) | copy-start | bytes 786436
  54.9 10.3 %collective-permute-start.10 = (bf16[1024,128]{1,0:T(8,128)(2,1)S(1)}, bf16[1024,128]{1,0:T(8,128)(2,1)S(1)}, u32[]{:S(2)}, u32[]{:S(2)}) collective-permute-start(bf16[1024,128]{1,0:T(8,128)(2,1)S(1)} %broadcast_select_fusion), channel_id=1, source_target_pairs={{0,16},{8,120},{16,32},{24,8},{32,48},{40,24},{48,64},{56,40},{64,... | collective-permute-start | bytes 786440 | tf_op jit(solution)/shard_map/ppermute | solution.py:239
  65.2 5.9 %copy-start.2 = (bf16[256,512]{1,0:T(8,128)(2,1)S(1)}, bf16[256,512]{1,0:T(8,128)(2,1)}, u32[]{:S(2)}) copy-start(bf16[256,512]{1,0:T(8,128)(2,1)} %q.1) | copy-start | bytes 786436
  66.8 5.8 %collective-permute-start.12 = (bf16[4,256,256]{2,1,0:T(8,128)(2,1)S(1)}, bf16[4,256,256]{2,1,0:T(8,128)(2,1)S(1)}, u32[]{:S(2)}, u32[]{:S(2)}) collective-permute-start(bf16[4,256,256]{2,1,0:T(8,128)(2,1)S(1)} %get-tuple-element.44), channel_id=1, source_target_pairs={{0,8},{8,0},{16,24},{24,16},{32,40},{40,32},{48,56},{56,48},{64,72... | collective-permute-start | bytes 1572872 | tf_op jit(solution)/shard_map/ppermute | solution.py:276
  72.6 9.6 %copy-start = (bf16[512,4096]{1,0:T(8,128)(2,1)S(1)}, bf16[512,4096]{1,0:T(8,128)(2,1)}, u32[]{:S(2)}) copy-start(bf16[512,4096]{1,0:T(8,128)(2,1)} %w.3) | copy-start | bytes 12582916
  75.1 11.7 %collective-permute-start.13 = (bf16[256,512]{1,0:T(8,128)(2,1)S(1)}, bf16[256,512]{1,0:T(8,128)(2,1)S(1)}, u32[]{:S(2)}, u32[]{:S(2)}) collective-permute-start(bf16[256,512]{1,0:T(8,128)(2,1)S(1)} %get-tuple-element.51), channel_id=1, source_target_pairs={{0,1},{1,2},{2,3},{3,0},{4,5},{5,6},{6,7},{7,4},{8,9},{9,10},{10,1... | collective-permute-start | bytes 786440 | tf_op jit(solution)/shard_map/ppermute | solution.py:326
  78.5 10.2 %collective-permute-start.15 = (bf16[256,512]{1,0:T(8,128)(2,1)S(1)}, bf16[256,512]{1,0:T(8,128)(2,1)S(1)}, u32[]{:S(2)}, u32[]{:S(2)}) collective-permute-start(bf16[256,512]{1,0:T(8,128)(2,1)S(1)} %get-tuple-element.52), channel_id=1, source_target_pairs={{0,3},{1,0},{2,1},{3,2},{4,7},{5,4},{6,5},{7,6},{8,11},{9,8},{10,9... | collective-permute-start | bytes 786440 | tf_op jit(solution)/shard_map/ppermute | solution.py:327
  88.9 16.2 %collective-permute-start.14 = (bf16[2,256,512]{2,1,0:T(8,128)(2,1)S(1)}, bf16[2,256,512]{2,1,0:T(8,128)(2,1)S(1)}, u32[]{:S(2)}, u32[]{:S(2)}) collective-permute-start(bf16[2,256,512]{2,1,0:T(8,128)(2,1)S(1)} %pad_maximum_fusion), channel_id=1, source_target_pairs={{0,1},{1,2},{2,3},{3,0},{4,5},{5,6},{6,7},{7,4},{8,9},{9,10},{10,1... | collective-permute-start | bytes 1572872 | tf_op jit(solution)/shard_map/ppermute | solution.py:346
  92.3 14.8 %collective-permute-start.16 = (bf16[2,256,512]{2,1,0:T(8,128)(2,1)S(1)}, bf16[2,256,512]{2,1,0:T(8,128)(2,1)}, u32[]{:S(2)}, u32[]{:S(2)}) collective-permute-start(bf16[2,256,512]{2,1,0:T(8,128)(2,1)S(1)} %pad_maximum_fusion.1), channel_id=1, source_target_pairs={{0,3},{1,0},{2,1},{3,2},{4,7},{5,4},{6,5},{7,6},{8,11},{9,8},{10,9... | collective-permute-start | bytes 1572872 | tf_op jit(solution)/shard_map/ppermute | solution.py:347
  108.4 38.0 %copy-start.9 = (f32[512]{0:T(512)S(1)}, f32[512]{0:T(512)}, u32[]{:S(2)}) copy-start(f32[512]{0:T(512)} %param.13) | copy-start | bytes 6148
  108.4 18.2 %collective-permute-start.17 = (bf16[256,512]{1,0:T(8,128)(2,1)S(1)}, bf16[256,512]{1,0:T(8,128)(2,1)S(1)}, u32[]{:S(2)}, u32[]{:S(2)}) collective-permute-start(bf16[256,512]{1,0:T(8,128)(2,1)S(1)} %fusion), channel_id=1, source_target_pairs={{0,4},{1,5},{2,6},{3,7},{4,0},{5,1},{6,2},{7,3},{8,12},{9,13},{10,... | collective-permute-start | bytes 786440 | tf_op jit(solution)/shard_map/ppermute | solution.py:352
  (4 other events, 3.1 us)

commit v2 on v1

--- a/solution.py
+++ b/solution.py
@@ -189,7 +189,7 @@
     out[0] = plain(att[...], w[...]).astype(BF16)
 
 
-def params(mib=48):
+def params(mib=20):
     return pltpu.CompilerParams(vmem_limit_bytes=mib << 20)
 
 
@@ -200,7 +200,7 @@
 def cost(keys, sets):
     rows = HEADS * TOK * sets
     return pl.CostEstimate(
-        flops=rows * keys * HEAD * 6, bytes_accessed=4 << 20, transcendentals=rows * keys
+        flops=rows * keys * HEAD * 20, bytes_accessed=4 << 20, transcendentals=rows * keys
     )
 
 
@@ -208,7 +208,6 @@
     me = lax.axis_index("seq").astype(jnp.int32)
     tp = lax.axis_index("tp").astype(jnp.int32)
     core, y, z = me % NC, (me // NC) % NY, me // (NC * NY)
-    hi = tp // NX
     me_s = me.reshape(1)
     tp_s = tp.reshape(1)
     c = key_head_scale * (LOG2E / math.sqrt(HEAD))
@@ -288,13 +287,17 @@
 
     wide_cols = out_weight.shape[1] // (NX * NH)
 
+    def column(tp_ref, own_half, d):
+        tp = tp_ref[0]
+        half = tp // NX if own_half else 1 - tp // NX
+        return (0, half * NX + (tp + d) % NX)
+
     def far_cols(i, tp_ref):
-        return (0, i * NX + (tp_ref[0] + 2) % NX)
-
-    def rest_cols(i, tp_ref):
-        g = i // 2
-        d = jnp.where(g == 2, 0, 1 + 2 * g)
-        return (0, (i % 2) * NX + (tp_ref[0] + d) % NX)
+        there, here = column(tp_ref, False, 2), column(tp_ref, True, 2)
+        return (0, jnp.where(i == 0, there[1], here[1]))
+
+    def rest_cols(own_half, i, tp_ref):
+        return column(tp_ref, own_half, jnp.where(i == 2, 0, 1 + 2 * i))
 
     whole = lambda *shape: pl.BlockSpec(shape, lambda i, tp_ref: (0,) * len(shape))
     att, far_part = pl.pallas_call(
@@ -318,41 +321,49 @@
             ],
         ),
         compiler_params=params(),
-        cost_estimate=pl.CostEstimate(flops=1 << 28, bytes_accessed=5 << 20, transcendentals=1 << 18),
+        cost_estimate=pl.CostEstimate(flops=1 << 31, bytes_accessed=5 << 20, transcendentals=1 << 18),
         name="merge_project",
     )(tp_s, m0, a0, got, out_weight)
     right = [(i, (i // NX) * NX + (i + 1) % NX) for i in range(NX * NH)]
     left = [(i, (i // NX) * NX + (i + NX - 1) % NX) for i in range(NX * NH)]
-    from_left = lax.ppermute(far_part[0], "tp", right)
-    from_right = lax.ppermute(far_part[1], "tp", left)
-    rest = pl.pallas_call(
-        rest_kernel,
-        out_shape=jax.ShapeDtypeStruct((6, TOK, wide_cols), BF16),
-        grid_spec=pltpu.PrefetchScalarGridSpec(
-            num_scalar_prefetch=1,
-            grid=(6,),
-            in_specs=[
-                whole(TOK, HEADS * HEAD),
-                pl.BlockSpec((HEADS * HEAD, wide_cols), rest_cols),
-            ],
-            out_specs=pl.BlockSpec((1, TOK, wide_cols), lambda i, tp_ref: (i, 0, 0)),
-        ),
-        compiler_params=params(),
-        cost_estimate=pl.CostEstimate(flops=3 << 28, bytes_accessed=5 << 20, transcendentals=0),
-        name="project_rest",
-    )(tp_s, att, out_weight)
-    to_right = jnp.stack([rest[0] + from_left, rest[1]])
-    to_left = jnp.stack([rest[2], rest[3] + from_right])
-    from_left = lax.ppermute(to_right, "tp", right)
-    from_right = lax.ppermute(to_left, "tp", left)
-    summed = rest[4:6].astype(F32) + from_left.astype(F32) + from_right.astype(F32)
-    send = jnp.where(hi == 0, summed[1], summed[0]).astype(BF16)
-    keep = jnp.where(hi == 0, summed[0], summed[1])
     swap = [(i, (i + NX) % (NX * NH)) for i in range(NX * NH)]
-    projected = keep + lax.ppermute(send, "tp", swap).astype(F32)
+    far_there = lax.ppermute(far_part[0], "tp", right)
+    far_here = lax.ppermute(far_part[1], "tp", left)
+
+    def rest(own_half):
+        return pl.pallas_call(
+            rest_kernel,
+            out_shape=jax.ShapeDtypeStruct((3, TOK, wide_cols), BF16),
+            grid_spec=pltpu.PrefetchScalarGridSpec(
+                num_scalar_prefetch=1,
+                grid=(3,),
+                in_specs=[
+                    whole(TOK, HEADS * HEAD),
+                    pl.BlockSpec((HEADS * HEAD, wide_cols), functools.partial(rest_cols, own_half)),
+                ],
+                out_specs=pl.BlockSpec((1, TOK, wide_cols), lambda i, tp_ref: (i, 0, 0)),
+            ),
+            compiler_params=params(),
+            cost_estimate=pl.CostEstimate(flops=1 << 31, bytes_accessed=2 << 20, transcendentals=0),
+            name="project_rest",
+        )(tp_s, att, out_weight)
+
+    there = rest(False)
+    there_left = lax.ppermute(there[0] + far_there, "tp", right)
+    there_right = lax.ppermute(there[1], "tp", left)
+    here = rest(True)
+    here_left = lax.ppermute(here[0], "tp", right)
+    here_right = lax.ppermute(here[1] + far_here, "tp", left)
+    there_sum = there[2].astype(F32) + there_left.astype(F32) + there_right.astype(F32)
+    crossed = lax.ppermute(there_sum.astype(BF16), "tp", swap)
+    here_sum = here[2].astype(F32) + here_left.astype(F32) + here_right.astype(F32)
+    projected = here_sum + crossed.astype(F32)
     squares = jnp.sum(projected * projected, -1)
-    squares = lax.psum(squares, "tp", axis_index_groups=[list(range(NX)), list(range(NX, 2 * NX))])
-    squares = lax.psum(squares, "tp", axis_index_groups=[[i, i + NX] for i in range(NX)])
+    near = [[i, i + 1] for i in range(0, NX * NH, 2)]
+    wrap = [[h + a, h + NX - 1 - a] for h in range(0, NX * NH, NX) for a in range(NX // 2)]
+    for groups in (near, wrap):
+        squares = jnp.sum(lax.all_gather(squares, "tp", axis_index_groups=groups), 0)
+    squares = squares + lax.ppermute(squares, "tp", swap)
     mean_square = squares[:, None] / out_weight.shape[1]
     return (projected * lax.rsqrt(mean_square + 1e-05) * norm_gain[None, :]).astype(BF16)
 

time: 148 us -> 143 us (0.966)
  the two profiles are of different devices: /device:TPU:200 before, /device:TPU:64 now
where the time goes in v2:
time: 143 us; the launch traced here: 142 us
  starting transfers between devices  81.3 us (57%)
  Pallas kernels  21.7 us (15%)
  waiting for transfers between devices  21.3 us (15%)
  blocking collectives  10.2 us (7%)
  local copies, waits for them, and re-layouts  3.86 us (3%)
  between operations  1.81 us (1%)
    pallas_call x3, Pallas kernels, shards(): pl.pallas_call(functools.partial(ring_kernel, step), out_shape=state_shap...  12.4 us
    ppermute x1, starting transfers between devices, shards(): squares = squares + lax.ppermute(squares, 'tp', swap)  11.3 us
    ppermute x1, starting transfers between devices, shards(): bwd = [lax.ppermute(block, 'seq', y_perm(-1))]  10.6 us
    ppermute x2, starting transfers between devices, shards(): bwd.append(lax.ppermute(bwd[-1], 'seq', y_perm(-1)))  10.3 us
    all_gather x2, blocking collectives, shards(): lax.all_gather(squares, 'tp', axis_index_groups=groups)  10.2 us
    ppermute x1, starting transfers between devices, shards(): crossed = lax.ppermute(there_sum.astype(BF16), 'tp', swap)  8.22 us
    ppermute x3, starting transfers between devices, shards(): up = [lax.ppermute(own, 'seq', z_perm(k)) for k in range(1, NZ)]  8.08 us
    ppermute x1, waiting for transfers between devices, shards(): crossed = lax.ppermute(there_sum.astype(BF16), 'tp', swap)  5.72 us
  transfers between devices with their start and end apart: 21, of which 8 were waited for; matrix products, arithmetic and copies ran while one was open for 0% of the time, Pallas kernels for 13%

profile of v2, /device:TPU:64, one launch (start us, length us, event | category | flops | bytes accessed | tf_op | source)
XLA Modules:
  0.0 141.7 jit_solution(8587382811455965995)
XLA Ops:
  2.2 4.3 %collective-permute-start.1 = (bf16[256,128]{1,0:T(8,128)(2,1)S(1)}, bf16[256,128]{1,0:T(8,128)(2,1)S(1)}, u32[]{:S(2)}, u32[]{:S(2)}) collective-permute-start(bf16[256,128]{1,0:T(8,128)(2,1)S(1)} %maximum_select_fusion), channel_id=1, source_target_pairs={{0,128},{8,136},{16,144},{24,152},{32,160},{40,168},{48,176},{56,1... | collective-permute-start | bytes 196616 | tf_op jit(solution)/shard_map/ppermute | solution.py:227
  6.5 3.1 %collective-permute-start.2 = (bf16[256,128]{1,0:T(8,128)(2,1)S(1)}, bf16[256,128]{1,0:T(8,128)(2,1)S(1)}, u32[]{:S(2)}, u32[]{:S(2)}) collective-permute-start(bf16[256,128]{1,0:T(8,128)(2,1)S(1)} %maximum_select_fusion), channel_id=1, source_target_pairs={{0,256},{8,264},{16,272},{24,280},{32,288},{40,296},{48,304},{56,3... | collective-permute-start | bytes 196616 | tf_op jit(solution)/shard_map/ppermute | solution.py:227
  10.3 1.9 %collective-permute-start.11 = (bf16[256,512]{1,0:T(8,128)(2,1)}, bf16[256,512]{1,0:T(8,128)(2,1)S(1)}, u32[]{:S(2)}, u32[]{:S(2)}) collective-permute-start(bf16[256,512]{1,0:T(8,128)(2,1)} %q.1), channel_id=1, source_target_pairs={{0,8},{8,0},{16,24},{24,16},{32,40},{40,32},{48,56},{56,48},{64,72... | collective-permute-start | bytes 786440 | tf_op jit(solution)/shard_map/ppermute | solution.py:217
  12.9 3.9 %collective-permute-done.1 = bf16[256,128]{1,0:T(8,128)(2,1)S(1)} collective-permute-done((bf16[256,128]{1,0:T(8,128)(2,1)S(1)}, bf16[256,128]{1,0:T(8,128)(2,1)S(1)}, u32[]{:S(2)}, u32[]{:S(2)}) %collective-permute-start.1) | collective-permute-done | bytes 65568 | tf_op jit(solution)/shard_map/ppermute | solution.py:227
  18.8 10.6 %collective-permute-start.7 = (bf16[1024,128]{1,0:T(8,128)(2,1)S(1)}, bf16[1024,128]{1,0:T(8,128)(2,1)S(1)}, u32[]{:S(2)}, u32[]{:S(2)}) collective-permute-start(bf16[1024,128]{1,0:T(8,128)(2,1)S(1)} %pad_maximum_fusion.blk), channel_id=1, source_target_pairs={{0,112},{8,120},{16,0},{24,8},{32,16},{40,24},{48,32},{56,40},{64,... | collective-permute-start | bytes 786440 | tf_op jit(solution)/shard_map/ppermute | solution.py:233
  32.1 2.8 %attend_own_chip.1 = (f32[4,256,128]{2,1,0:T(8,128)S(1)}, f32[4,256,256]{2,1,0:T(8,128)S(1)}, f32[4,256,128]{2,1,0:T(8,128)S(1)}, f32[4,256,256]{2,1,0:T(8,128)S(1)}) custom-call(s32[1]{0:T(128)} %bitcast.1.me_ref, f32[1]{0:T(128)S(6)} %mul.28.c_ref, bf16[256,512]{1,0:T(8,128)(2,1)S(1)} %copy-done.3, bf16[256,512]{1,0:T(8,128)(2,1)S(1)} %collective-permute-done.11.q1.q, ...), custom_call_target="tpu_custom_call" | custom-call | flops 3355443200 | bytes 4194304 | tf_op jit(solution)/shard_map/attend_own_chip/pallas_call | solution.py:241
  36.8 5.1 %collective-permute-start.8 = (bf16[1024,128]{1,0:T(8,128)(2,1)S(1)}, bf16[1024,128]{1,0:T(8,128)(2,1)S(1)}, u32[]{:S(2)}, u32[]{:S(2)}) collective-permute-start(bf16[1024,128]{1,0:T(8,128)(2,1)S(1)} %collective-permute-done.7.bwd), channel_id=1, source_target_pairs={{0,112},{8,120},{16,0},{24,8},{32,16},{40,24},{48,32},{56,40},{64,... | collective-permute-start | bytes 786440 | tf_op jit(solution)/shard_map/ppermute | solution.py:236
  41.9 4.1 %attend_ring.3 = (f32[4,256,128]{2,1,0:T(8,128)S(1)}, f32[4,256,256]{2,1,0:T(8,128)S(1)}, f32[4,256,128]{2,1,0:T(8,128)S(1)}, f32[4,256,256]{2,1,0:T(8,128)S(1)}) custom-call(s32[1]{0:T(128)} %bitcast.1.me_ref, f32[1]{0:T(128)S(6)} %mul.28.c_ref, ...), custom_call_target="tpu_custom_call", output_to_operand_aliasing={{0}: (6, {}), {1}: (7, {}), {2}: (8, {}), {3}: (9, {})} | custom-call | flops 5368709120 | bytes 4194304 | tf_op jit(solution)/shard_map/attend_ring/pallas_call | solution.py:252
  48.0 5.1 %collective-permute-start.9 = (bf16[1024,128]{1,0:T(8,128)(2,1)S(1)}, bf16[1024,128]{1,0:T(8,128)(2,1)S(1)}, u32[]{:S(2)}, u32[]{:S(2)}) collective-permute-start(bf16[1024,128]{1,0:T(8,128)(2,1)S(1)} %collective-permute-done.8.bwd), channel_id=1, source_target_pairs={{0,112},{8,120},{16,0},{24,8},{32,16},{40,24},{48,32},{56,40},{64,... | collective-permute-start | bytes 786440 | tf_op jit(solution)/shard_map/ppermute | solution.py:236
  53.1 4.1 %attend_ring.4 = (f32[4,256,128]{2,1,0:T(8,128)S(1)}, f32[4,256,256]{2,1,0:T(8,128)S(1)}, f32[4,256,128]{2,1,0:T(8,128)S(1)}, f32[4,256,256]{2,1,0:T(8,128)S(1)}) custom-call(s32[1]{0:T(128)} %bitcast.1.me_ref, f32[1]{0:T(128)S(6)} %mul.28.c_ref, ...), custom_call_target="tpu_custom_call", output_to_operand_aliasing={{0}: (6, {}), {1}: (7, {}), {2}: (8, {}), {3}: (9, {})} | custom-call | flops 5368709120 | bytes 4194304 | tf_op jit(solution)/shard_map/attend_ring/pallas_call | solution.py:252
  59.7 4.3 %attend_ring.5 = (f32[4,256,128]{2,1,0:T(8,128)S(1)}, f32[4,256,256]{2,1,0:T(8,128)S(1)}, f32[4,256,128]{2,1,0:T(8,128)S(1)}, f32[4,256,256]{2,1,0:T(8,128)S(1)}) custom-call(s32[1]{0:T(128)} %bitcast.1.me_ref, f32[1]{0:T(128)S(6)} %mul.28.c_ref, ...), custom_call_target="tpu_custom_call", output_to_operand_aliasing={{0}: (6, {}), {1}: (7, {}), {2}: (8, {}), {3}: (9, {})} | custom-call | flops 5368709120 | bytes 4194304 | tf_op jit(solution)/shard_map/attend_ring/pallas_call | solution.py:252
  64.0 3.7 %collective-permute-done.10.blk = bf16[1024,128]{1,0:T(8,128)(2,1)S(1)} collective-permute-done((bf16[1024,128]{1,0:T(8,128)(2,1)S(1)}, bf16[1024,128]{1,0:T(8,128)(2,1)S(1)}, u32[]{:S(2)}, u32[]{:S(2)}) %collective-permute-start.10) | collective-permute-done | bytes 262176 | tf_op jit(solution)/shard_map/ppermute | solution.py:238
  74.8 4.7 %collective-permute-start.14 = (bf16[256,512]{1,0:T(8,128)(2,1)S(1)}, bf16[256,512]{1,0:T(8,128)(2,1)S(1)}, u32[]{:S(2)}, u32[]{:S(2)}) collective-permute-start(bf16[256,512]{1,0:T(8,128)(2,1)S(1)} %get-tuple-element.47), channel_id=1, source_target_pairs={{0,3},{1,0},{2,1},{3,2},{4,7},{5,4},{6,5},{7,6},{8,11},{9,8},{10,9... | collective-permute-start | bytes 786440 | tf_op jit(solution)/shard_map/ppermute | solution.py:331
  82.6 5.1 %collective-permute-start.18 = (bf16[256,512]{1,0:T(8,128)(2,1)S(1)}, bf16[256,512]{1,0:T(8,128)(2,1)S(1)}, u32[]{:S(2)}, u32[]{:S(2)}) collective-permute-start(bf16[256,512]{1,0:T(8,128)(2,1)S(1)} %slice_bitcast_fusion), channel_id=1, source_target_pairs={{0,3},{1,0},{2,1},{3,2},{4,7},{5,4},{6,5},{7,6},{8,11},{9,8},{10,9... | collective-permute-start | bytes 786440 | tf_op jit(solution)/shard_map/ppermute | solution.py:353
  89.0 2.1 %collective-permute-done.16 = bf16[256,512]{1,0:T(8,128)(2,1)S(1)} collective-permute-done((bf16[256,512]{1,0:T(8,128)(2,1)S(1)}, bf16[256,512]{1,0:T(8,128)(2,1)S(1)}, u32[]{:S(2)}, u32[]{:S(2)}) %collective-permute-start.16) | collective-permute-done | bytes 262176 | tf_op jit(solution)/shard_map/ppermute | solution.py:330
  91.1 1.9 %collective-permute-start.17 = (bf16[256,512]{1,0:T(8,128)(2,1)S(1)}, bf16[256,512]{1,0:T(8,128)(2,1)S(1)}, u32[]{:S(2)}, u32[]{:S(2)}) collective-permute-start(bf16[256,512]{1,0:T(8,128)(2,1)S(1)} %fusion.4), channel_id=1, source_target_pairs={{0,1},{1,2},{2,3},{3,0},{4,5},{5,6},{6,7},{7,4},{8,9},{9,10},{10,1... | collective-permute-start | bytes 786440 | tf_op jit(solution)/shard_map/ppermute | solution.py:352
  93.0 1.9 %collective-permute-start.13 = (bf16[256,512]{1,0:T(8,128)(2,1)S(1)}, bf16[256,512]{1,0:T(8,128)(2,1)S(1)}, u32[]{:S(2)}, u32[]{:S(2)}) collective-permute-start(bf16[256,512]{1,0:T(8,128)(2,1)S(1)} %slice_bitcast_fusion.4), channel_id=1, source_target_pairs={{0,1},{1,2},{2,3},{3,0},{4,5},{5,6},{6,7},{7,4},{8,9},{9,10},{10,1... | collective-permute-start | bytes 786440 | tf_op jit(solution)/shard_map/ppermute | solution.py:355
  95.0 5.1 %collective-permute-start.15 = (bf16[256,512]{1,0:T(8,128)(2,1)S(1)}, bf16[256,512]{1,0:T(8,128)(2,1)S(1)}, u32[]{:S(2)}, u32[]{:S(2)}) collective-permute-start(bf16[256,512]{1,0:T(8,128)(2,1)S(1)} %fusion.5), channel_id=1, source_target_pairs={{0,3},{1,0},{2,1},{3,2},{4,7},{5,4},{6,5},{7,6},{8,11},{9,8},{10,9... | collective-permute-start | bytes 786440 | tf_op jit(solution)/shard_map/ppermute | solution.py:356
  100.1 3.3 %collective-permute-done.17 = bf16[256,512]{1,0:T(8,128)(2,1)S(1)} collective-permute-done((bf16[256,512]{1,0:T(8,128)(2,1)S(1)}, bf16[256,512]{1,0:T(8,128)(2,1)S(1)}, u32[]{:S(2)}, u32[]{:S(2)}) %collective-permute-start.17) | collective-permute-done | bytes 262176 | tf_op jit(solution)/shard_map/ppermute | solution.py:352
  103.5 8.2 %collective-permute-start.19 = (bf16[256,512]{1,0:T(8,128)(2,1)S(1)}, bf16[256,512]{1,0:T(8,128)(2,1)S(1)}, u32[]{:S(2)}, u32[]{:S(2)}) collective-permute-start(bf16[256,512]{1,0:T(8,128)(2,1)S(1)} %fusion.1), channel_id=1, source_target_pairs={{0,4},{1,5},{2,6},{3,7},{4,0},{5,1},{6,2},{7,3},{8,12},{9,13},{10,... | collective-permute-start | bytes 786440 | tf_op jit(solution)/shard_map/ppermute | solution.py:358
  111.8 5.7 %collective-permute-done.19 = bf16[256,512]{1,0:T(8,128)(2,1)S(1)} collective-permute-done((bf16[256,512]{1,0:T(8,128)(2,1)S(1)}, bf16[256,512]{1,0:T(8,128)(2,1)S(1)}, u32[]{:S(2)}, u32[]{:S(2)}) %collective-permute-start.19) | collective-permute-done | bytes 262176 | tf_op jit(solution)/shard_map/ppermute | solution.py:358
  117.7 4.7 %all-gather.2 = f32[2,1,256]{2,1,0:T(1,128)S(1)} all-gather(f32[1,1,256]{2,1,0:T(1,128)S(1)} %bitcast.35), channel_id=2, replica_groups={{0,1},{2,3},{4,5},{6,7},{8,9},{10,11},{12,13},{14,15},{16,17},{18,19},{..., dimensions={0}, use_global_device_ids=true | all-gather | bytes 3072 | tf_op jit(solution)/shard_map/all_gather | solution.py:365
  122.5 5.4 %all-gather.3 = f32[2,1,256]{2,1,0:T(1,128)S(1)} all-gather(f32[1,1,256]{2,1,0:T(1,128)S(1)} %bitcast.36), channel_id=3, replica_groups={{0,3},{1,2},{4,7},{5,6},{8,11},{9,10},{12,15},{13,14},{16,19},{17,18},{..., dimensions={0}, use_global_device_ids=true | all-gather | bytes 3072 | tf_op jit(solution)/shard_map/all_gather | solution.py:365
  127.9 11.3 %collective-permute-start.20 = (f32[256]{0:T(256)S(1)}, f32[256]{0:T(256)S(1)}, u32[]{:S(2)}, u32[]{:S(2)}) collective-permute-start(f32[256]{0:T(256)S(1)} %reduce_sum.29), channel_id=1, source_target_pairs={{0,4},{1,5},{2,6},{3,7},{4,0},{5,1},{6,2},{7,3},{8,12},{9,13},{10,... | collective-permute-start | bytes 3080 | tf_op jit(solution)/shard_map/ppermute | solution.py:366
  (58 shorter events, 27.3 us)
Async XLA Ops:
  1.5 0.7 collective-permute-start
  2.2 14.6 %collective-permute-start.1 = (bf16[256,128]{1,0:T(8,128)(2,1)S(1)}, bf16[256,128]{1,0:T(8,128)(2,1)S(1)}, u32[]{:S(2)}, u32[]{:S(2)}) collective-permute-start(bf16[256,128]{1,0:T(8,128)(2,1)S(1)} %maximum_select_fusion), channel_id=1, source_target_pairs={{0,128},{8,136},{16,144},{24,152},{32,160},{40,168},{48,176},{56,1... | collective-permute-start | bytes 196616 | tf_op jit(solution)/shard_map/ppermute | solution.py:227
  6.5 10.4 %collective-permute-start.2 = (bf16[256,128]{1,0:T(8,128)(2,1)S(1)}, bf16[256,128]{1,0:T(8,128)(2,1)S(1)}, u32[]{:S(2)}, u32[]{:S(2)}) collective-permute-start(bf16[256,128]{1,0:T(8,128)(2,1)S(1)} %maximum_select_fusion), channel_id=1, source_target_pairs={{0,256},{8,264},{16,272},{24,280},{32,288},{40,296},{48,304},{56,3... | collective-permute-start | bytes 196616 | tf_op jit(solution)/shard_map/ppermute | solution.py:227
  9.6 7.2 %collective-permute-start.3 = (bf16[256,128]{1,0:T(8,128)(2,1)S(1)}, bf16[256,128]{1,0:T(8,128)(2,1)S(1)}, u32[]{:S(2)}, u32[]{:S(2)}) collective-permute-start(bf16[256,128]{1,0:T(8,128)(2,1)S(1)} %maximum_select_fusion), channel_id=1, source_target_pairs={{0,384},{8,392},{16,400},{24,408},{32,416},{40,424},{48,432},{56,4... | collective-permute-start | bytes 196616 | tf_op jit(solution)/shard_map/ppermute | solution.py:227
  10.3 19.1 %collective-permute-start.11 = (bf16[256,512]{1,0:T(8,128)(2,1)}, bf16[256,512]{1,0:T(8,128)(2,1)S(1)}, u32[]{:S(2)}, u32[]{:S(2)}) collective-permute-start(bf16[256,512]{1,0:T(8,128)(2,1)} %q.1), channel_id=1, source_target_pairs={{0,8},{8,0},{16,24},{24,16},{32,40},{40,32},{48,56},{56,48},{64,72... | collective-permute-start | bytes 786440 | tf_op jit(solution)/shard_map/ppermute | solution.py:217
  16.9 17.9 %collective-permute-start.4 = (bf16[1024,128]{1,0:T(8,128)(2,1)S(1)}, bf16[1024,128]{1,0:T(8,128)(2,1)S(1)}, u32[]{:S(2)}, u32[]{:S(2)}) collective-permute-start(bf16[1024,128]{1,0:T(8,128)(2,1)S(1)} %pad_maximum_fusion.blk), channel_id=1, source_target_pairs={{0,16},{8,24},{16,32},{24,40},{32,48},{40,56},{48,64},{56,72},{64,... | collective-permute-start | bytes 786440 | tf_op jit(solution)/shard_map/ppermute | solution.py:232
  18.8 17.9 %collective-permute-start.7 = (bf16[1024,128]{1,0:T(8,128)(2,1)S(1)}, bf16[1024,128]{1,0:T(8,128)(2,1)S(1)}, u32[]{:S(2)}, u32[]{:S(2)}) collective-permute-start(bf16[1024,128]{1,0:T(8,128)(2,1)S(1)} %pad_maximum_fusion.blk), channel_id=1, source_target_pairs={{0,112},{8,120},{16,0},{24,8},{32,16},{40,24},{48,32},{56,40},{64,... | collective-permute-start | bytes 786440 | tf_op jit(solution)/shard_map/ppermute | solution.py:233
  34.8 11.2 %collective-permute-start.5 = (bf16[1024,128]{1,0:T(8,128)(2,1)S(1)}, bf16[1024,128]{1,0:T(8,128)(2,1)S(1)}, u32[]{:S(2)}, u32[]{:S(2)}) collective-permute-start(bf16[1024,128]{1,0:T(8,128)(2,1)S(1)} %collective-permute-done.4.fwd), channel_id=1, source_target_pairs={{0,16},{8,24},{16,32},{24,40},{32,48},{40,56},{48,64},{56,72},{64,... | collective-permute-start | bytes 786440 | tf_op jit(solution)/shard_map/ppermute | solution.py:235
  36.8 11.2 %collective-permute-start.8 = (bf16[1024,128]{1,0:T(8,128)(2,1)S(1)}, bf16[1024,128]{1,0:T(8,128)(2,1)S(1)}, u32[]{:S(2)}, u32[]{:S(2)}) collective-permute-start(bf16[1024,128]{1,0:T(8,128)(2,1)S(1)} %collective-permute-done.7.bwd), channel_id=1, source_target_pairs={{0,112},{8,120},{16,0},{24,8},{32,16},{40,24},{48,32},{56,40},{64,... | collective-permute-start | bytes 786440 | tf_op jit(solution)/shard_map/ppermute | solution.py:236
  46.0 11.2 %collective-permute-start.6 = (bf16[1024,128]{1,0:T(8,128)(2,1)S(1)}, bf16[1024,128]{1,0:T(8,128)(2,1)S(1)}, u32[]{:S(2)}, u32[]{:S(2)}) collective-permute-start(bf16[1024,128]{1,0:T(8,128)(2,1)S(1)} %collective-permute-done.5.fwd), channel_id=1, source_target_pairs={{0,16},{8,24},{16,32},{24,40},{32,48},{40,56},{48,64},{56,72},{64,... | collective-permute-start | bytes 786440 | tf_op jit(solution)/shard_map/ppermute | solution.py:235
  48.0 9.7 %collective-permute-start.9 = (bf16[1024,128]{1,0:T(8,128)(2,1)S(1)}, bf16[1024,128]{1,0:T(8,128)(2,1)S(1)}, u32[]{:S(2)}, u32[]{:S(2)}) collective-permute-start(bf16[1024,128]{1,0:T(8,128)(2,1)S(1)} %collective-permute-done.8.bwd), channel_id=1, source_target_pairs={{0,112},{8,120},{16,0},{24,8},{32,16},{40,24},{48,32},{56,40},{64,... | collective-permute-start | bytes 786440 | tf_op jit(solution)/shard_map/ppermute | solution.py:236
  57.7 9.9 %collective-permute-start.10 = (bf16[1024,128]{1,0:T(8,128)(2,1)S(1)}, bf16[1024,128]{1,0:T(8,128)(2,1)S(1)}, u32[]{:S(2)}, u32[]{:S(2)}) collective-permute-start(bf16[1024,128]{1,0:T(8,128)(2,1)S(1)} %broadcast_select_fusion), channel_id=1, source_target_pairs={{0,16},{8,120},{16,32},{24,8},{32,48},{40,24},{48,64},{56,40},{64,... | collective-permute-start | bytes 786440 | tf_op jit(solution)/shard_map/ppermute | solution.py:238
  63.9 7.3 %copy-start.4 = (bf16[256,512]{1,0:T(8,128)(2,1)S(1)}, bf16[256,512]{1,0:T(8,128)(2,1)}, u32[]{:S(2)}) copy-start(bf16[256,512]{1,0:T(8,128)(2,1)} %q.1) | copy-start | bytes 786436
  69.3 3.8 %collective-permute-start.12 = (bf16[4,256,256]{2,1,0:T(8,128)(2,1)S(1)}, bf16[4,256,256]{2,1,0:T(8,128)(2,1)S(1)}, u32[]{:S(2)}, u32[]{:S(2)}) collective-permute-start(bf16[4,256,256]{2,1,0:T(8,128)(2,1)S(1)} %get-tuple-element.44), channel_id=1, source_target_pairs={{0,8},{8,0},{16,24},{24,16},{32,40},{40,32},{48,56},{56,48},{64,72... | collective-permute-start | bytes 1572872 | tf_op jit(solution)/shard_map/ppermute | solution.py:275
  71.2 2.2 %copy-start.2 = (bf16[512,4096]{1,0:T(8,128)(2,1)S(1)}, bf16[512,4096]{1,0:T(8,128)(2,1)}, u32[]{:S(2)}) copy-start(bf16[512,4096]{1,0:T(8,128)(2,1)} %w.5) | copy-start | bytes 12582916
  74.8 20.1 %collective-permute-start.14 = (bf16[256,512]{1,0:T(8,128)(2,1)S(1)}, bf16[256,512]{1,0:T(8,128)(2,1)S(1)}, u32[]{:S(2)}, u32[]{:S(2)}) collective-permute-start(bf16[256,512]{1,0:T(8,128)(2,1)S(1)} %get-tuple-element.47), channel_id=1, source_target_pairs={{0,3},{1,0},{2,1},{3,2},{4,7},{5,4},{6,5},{7,6},{8,11},{9,8},{10,9... | collective-permute-start | bytes 786440 | tf_op jit(solution)/shard_map/ppermute | solution.py:331
  79.5 11.5 %collective-permute-start.16 = (bf16[256,512]{1,0:T(8,128)(2,1)S(1)}, bf16[256,512]{1,0:T(8,128)(2,1)S(1)}, u32[]{:S(2)}, u32[]{:S(2)}) collective-permute-start(bf16[256,512]{1,0:T(8,128)(2,1)S(1)} %get-tuple-element.48), channel_id=1, source_target_pairs={{0,1},{1,2},{2,3},{3,0},{4,5},{5,6},{6,7},{7,4},{8,9},{9,10},{10,1... | collective-permute-start | bytes 786440 | tf_op jit(solution)/shard_map/ppermute | solution.py:330
  82.6 58.2 %copy-start.5 = (f32[512]{0:T(512)S(1)}, f32[512]{0:T(512)}, u32[]{:S(2)}) copy-start(f32[512]{0:T(512)} %param.13) | copy-start | bytes 6148
  82.6 17.5 %collective-permute-start.18 = (bf16[256,512]{1,0:T(8,128)(2,1)S(1)}, bf16[256,512]{1,0:T(8,128)(2,1)S(1)}, u32[]{:S(2)}, u32[]{:S(2)}) collective-permute-start(bf16[256,512]{1,0:T(8,128)(2,1)S(1)} %slice_bitcast_fusion), channel_id=1, source_target_pairs={{0,3},{1,0},{2,1},{3,2},{4,7},{5,4},{6,5},{7,6},{8,11},{9,8},{10,9... | collective-permute-start | bytes 786440 | tf_op jit(solution)/shard_map/ppermute | solution.py:353
  91.1 12.3 %collective-permute-start.17 = (bf16[256,512]{1,0:T(8,128)(2,1)S(1)}, bf16[256,512]{1,0:T(8,128)(2,1)S(1)}, u32[]{:S(2)}, u32[]{:S(2)}) collective-permute-start(bf16[256,512]{1,0:T(8,128)(2,1)S(1)} %fusion.4), channel_id=1, source_target_pairs={{0,1},{1,2},{2,3},{3,0},{4,5},{5,6},{6,7},{7,4},{8,9},{9,10},{10,1... | collective-permute-start | bytes 786440 | tf_op jit(solution)/shard_map/ppermute | solution.py:352
  93.0 18.7 %collective-permute-start.13 = (bf16[256,512]{1,0:T(8,128)(2,1)S(1)}, bf16[256,512]{1,0:T(8,128)(2,1)S(1)}, u32[]{:S(2)}, u32[]{:S(2)}) collective-permute-start(bf16[256,512]{1,0:T(8,128)(2,1)S(1)} %slice_bitcast_fusion.4), channel_id=1, source_target_pairs={{0,1},{1,2},{2,3},{3,0},{4,5},{5,6},{6,7},{7,4},{8,9},{9,10},{10,1... | collective-permute-start | bytes 786440 | tf_op jit(solution)/shard_map/ppermute | solution.py:355
  95.0 16.8 %collective-permute-start.15 = (bf16[256,512]{1,0:T(8,128)(2,1)S(1)}, bf16[256,512]{1,0:T(8,128)(2,1)S(1)}, u32[]{:S(2)}, u32[]{:S(2)}) collective-permute-start(bf16[256,512]{1,0:T(8,128)(2,1)S(1)} %fusion.5), channel_id=1, source_target_pairs={{0,3},{1,0},{2,1},{3,2},{4,7},{5,4},{6,5},{7,6},{8,11},{9,8},{10,9... | collective-permute-start | bytes 786440 | tf_op jit(solution)/shard_map/ppermute | solution.py:356
  103.5 14.0 %collective-permute-start.19 = (bf16[256,512]{1,0:T(8,128)(2,1)S(1)}, bf16[256,512]{1,0:T(8,128)(2,1)S(1)}, u32[]{:S(2)}, u32[]{:S(2)}) collective-permute-start(bf16[256,512]{1,0:T(8,128)(2,1)S(1)} %fusion.1), channel_id=1, source_target_pairs={{0,4},{1,5},{2,6},{3,7},{4,0},{5,1},{6,2},{7,3},{8,12},{9,13},{10,... | collective-permute-start | bytes 786440 | tf_op jit(solution)/shard_map/ppermute | solution.py:358
  127.9 12.9 %collective-permute-start.20 = (f32[256]{0:T(256)S(1)}, f32[256]{0:T(256)S(1)}, u32[]{:S(2)}, u32[]{:S(2)}) collective-permute-start(f32[256]{0:T(256)S(1)} %reduce_sum.29), channel_id=1, source_target_pairs={{0,4},{1,5},{2,6},{3,7},{4,0},{5,1},{6,2},{7,3},{8,12},{9,13},{10,... | collective-permute-start | bytes 3080 | tf_op jit(solution)/shard_map/ppermute | solution.py:366
  (3 other events, 2.6 us)

commit v3 on v1

--- a/solution.py
+++ b/solution.py
@@ -32,12 +32,6 @@
 
 
 PLACES = [(z, y, c) for z in range(NZ) for y in range(NY) for c in range(NC)]
-LAST = sid(NZ - 1, NY - 1, 1)
-
-
-def z_perm(k):
-    pairs = [(sid(z, y, c), sid(z + k, y, c)) for z, y, c in PLACES if z + k < NZ]
-    return pairs + [(LAST, sid(k - 1, NY - 1, 1))]
 
 
 def y_perm(k):
@@ -58,11 +52,14 @@
 
 def seen(me, query_core, key_y):
     z, y, core = me // (NY * NC), (me // NC) % NY, me % NC
-    anchor = jnp.logical_and(core == 1, key_y == NY - 1)
+    holder_y = jnp.where(z == 0, 0, NY - 1)
+    holder_core = jnp.where(z == 0, 0, 1)
+    anchor = jnp.logical_and(core == holder_core, key_y == holder_y)
     first_piece = (z * NY + y) * NC + query_core == 0
-    below = jnp.logical_or(key_y < y, jnp.logical_and(key_y == y, core < query_core))
-    own = jnp.where(anchor, jnp.logical_not(first_piece).astype(jnp.int32), below.astype(jnp.int32))
-    return [own] + [(z >= k).astype(jnp.int32) for k in range(1, NZ)]
+    below = jnp.logical_or(key_y < y, jnp.logical_and(key_y == y, core < query_core)).astype(jnp.int32)
+    flags = [jnp.where(j == z, below, (j < z).astype(jnp.int32)) for j in range(NZ)]
+    flags[-1] = jnp.where(anchor, jnp.logical_not(first_piece).astype(jnp.int32), flags[-1])
+    return flags
 
 
 def prepare(blocks, shown, kk, vv):
@@ -102,27 +99,32 @@
             update(c, q_ref[:, h * HEAD : (h + 1) * HEAD], kk, vv, m_ref, acc_ref, h)
 
 
-def first_kernel(me_ref, c_ref, q0, q1, k_ref, v_ref, blk, m0, a0, m1, a1, blocks, kk, vv, lv):
+def local_kernel(c_ref, q, kv, m, a, lv):
+    lv[:, 0:HEAD] = kv[:, HEAD:]
+    lv[:, HEAD : 2 * HEAD] = jnp.ones((TOK, HEAD), BF16)
+    c = c_ref[0]
+    row = lax.broadcasted_iota(jnp.int32, (TOK, TOK), 0)
+    col = lax.broadcasted_iota(jnp.int32, (TOK, TOK), 1)
+    for h in range(HEADS):
+        s = cross(q[:, h * HEAD : (h + 1) * HEAD], kv[:, 0:HEAD]) * c
+        s = jnp.where(row >= col, s, LOW)
+        top = jnp.broadcast_to(jnp.max(s, axis=1, keepdims=True), (TOK, HEAD))
+        p = jnp.exp2(s - wide(top, TOK // HEAD)).astype(BF16)
+        a[h] = plain(p, lv[...])
+        m[h] = top
+
+
+def chip_kernel(me_ref, c_ref, q0, q1, blk, m0i, a0i, m0, a0, m1, a1, kk, vv):
     me = me_ref[0]
     c = c_ref[0]
     core = me % NC
-    lv[:, 0:HEAD] = v_ref[...]
-    lv[:, HEAD : 2 * HEAD] = jnp.ones((TOK, HEAD), BF16)
-    row = lax.broadcasted_iota(jnp.int32, (TOK, TOK), 0)
-    col = lax.broadcasted_iota(jnp.int32, (TOK, TOK), 1)
-    for h in range(HEADS):
-        s = cross(q0[:, h * HEAD : (h + 1) * HEAD], k_ref[...]) * c
-        s = jnp.where(row >= col, s, LOW)
-        m = jnp.broadcast_to(jnp.max(s, axis=1, keepdims=True), (TOK, HEAD))
-        p = jnp.exp2(s - wide(m, TOK // HEAD)).astype(BF16)
-        a0[h] = plain(p, lv[...])
-        m0[h] = m
-        m1[h] = jnp.full((TOK, HEAD), LOW, F32)
-        a1[h] = jnp.zeros((TOK, 2 * HEAD), F32)
-    blocks[...] = blk[...]
     y = (me // NC) % NY
-    attend_set(me, core, [y], c, q0, blocks, kk, vv, m0, a0)
-    attend_set(me, 1 - core, [y], c, q1, blocks, kk, vv, m1, a1)
+    m0[...] = m0i[...]
+    a0[...] = a0i[...]
+    m1[...] = jnp.full(m1.shape, LOW, F32)
+    a1[...] = jnp.zeros(a1.shape, F32)
+    attend_set(me, core, [y], c, q0, blk, kk, vv, m0, a0)
+    attend_set(me, 1 - core, [y], c, q1, blk, kk, vv, m1, a1)
 
 
 def ring_kernel(step, me_ref, c_ref, q0, q1, fwd, bwd, m0i, a0i, m1i, a1i, m0, a0, m1, a1, blocks, kk, vv):
@@ -185,11 +187,47 @@
     out[0] = plain(att[...], w[...]).astype(BF16)
 
 
-def rest_kernel(tp_ref, att, w, out):
+def project_kernel(tp_ref, att, w, out):
     out[0] = plain(att[...], w[...]).astype(BF16)
 
 
-def params(mib=48):
+def sum_kernel(parts, out):
+    total = parts[0].astype(F32)
+    for j in range(1, NX):
+        total += parts[j].astype(F32)
+    out[...] = total.astype(out.dtype)
+
+
+def widen_kernel(part, out):
+    out[...] = part[...].astype(F32)
+
+
+def square_kernel(parts, crossed, out, squares):
+    total = crossed[...]
+    for j in range(NX):
+        total += parts[j].astype(F32)
+    out[...] = total
+    ones = jnp.ones((8, total.shape[1]), F32)
+    sums = lax.dot_general(
+        ones,
+        total * total,
+        (((1,), (1,)), ((), ())),
+        precision=lax.Precision.HIGHEST,
+        preferred_element_type=F32,
+    )
+    for j in range(NX * NH):
+        squares[j] = sums
+
+
+def norm_kernel(features, projected, squares, gain, out):
+    total = squares[0]
+    for j in range(1, NX * NH):
+        total += squares[j]
+    scale = lax.rsqrt(jnp.transpose(total)[:, 0:1] / features + 1e-05)
+    out[...] = (projected[...] * scale * gain[...]).astype(BF16)
+
+
+def params(mib=20):
     return pltpu.CompilerParams(vmem_limit_bytes=mib << 20)
 
 
@@ -200,35 +238,36 @@
 def cost(keys, sets):
     rows = HEADS * TOK * sets
     return pl.CostEstimate(
-        flops=rows * keys * HEAD * 6, bytes_accessed=4 << 20, transcendentals=rows * keys
+        flops=rows * keys * HEAD * 20, bytes_accessed=4 << 20, transcendentals=rows * keys
     )
 
 
 def shards(queries, keys, values, key_head_scale, retained, out_weight, norm_gain):
     me = lax.axis_index("seq").astype(jnp.int32)
     tp = lax.axis_index("tp").astype(jnp.int32)
-    core, y, z = me % NC, (me // NC) % NY, me // (NC * NY)
-    hi = tp // NX
+    core, z = me % NC, me // (NC * NY)
     me_s = me.reshape(1)
     tp_s = tp.reshape(1)
     c = key_head_scale * (LOG2E / math.sqrt(HEAD))
 
+    kv = jnp.concatenate([keys, values], 1)
+    own = lax.dynamic_slice_in_dim(kv, retained[0, 0] * BLOCK, BLOCK, 0)
+    own = jnp.concatenate([own[:, :HEAD], own[:, HEAD:]], 0)
+    planes = [[sid(z_, y_, c_) for z_ in range(NZ)] for y_ in range(NY) for c_ in range(NC)]
+    stack = lax.all_to_all(
+        jnp.broadcast_to(own, (NZ, SLOT, HEAD)), "seq", 0, 0, axis_index_groups=planes
+    )
+    holders = [sid(z_, NY - 1, 1) for z_ in range(NZ)]
     anchor = jnp.concatenate([keys[:BLOCK], values[:BLOCK]], 0)
-    anchor_far = lax.ppermute(anchor, "seq", [(0, LAST)])
+    far = lax.ppermute(anchor, "seq", [(0, holders[3])])
+    anchor = jnp.where(me == holders[3], far, anchor)
+    near = lax.ppermute(anchor, "seq", [(0, holders[1]), (holders[3], holders[2])])
     other_queries = lax.ppermute(queries, "seq", [(sid(*s), sid(s[0], s[1], 1 - s[2])) for s in PLACES])
-    row = retained[0, 0] * BLOCK
-    own = jnp.concatenate(
-        [
-            lax.dynamic_slice_in_dim(keys, row, BLOCK, 0),
-            lax.dynamic_slice_in_dim(values, row, BLOCK, 0),
-        ],
-        0,
+    placed = jnp.where(jnp.logical_or(me == holders[1], me == holders[2]), near, anchor)
+    holds = jnp.where(z == 0, me == 0, me % (NY * NC) == NY * NC - 1)
+    block = jnp.concatenate(
+        [stack[: NZ - 1].reshape(MSG - SLOT, HEAD), jnp.where(holds, placed, stack[NZ - 1])], 0
     )
-    own = jnp.where(me == LAST, anchor_far, own)
-    up = [lax.ppermute(own, "seq", z_perm(k)) for k in range(1, NZ)]
-    far = jnp.where(z == 0, up[0], jnp.where(z == 1, up[1], jnp.where(z == 2, up[2], own)))
-    slot = jnp.where(jnp.logical_and(y == NY - 1, core == 1), far, own)
-    block = jnp.concatenate([slot] + up, 0)
 
     fwd = [lax.ppermute(block, "seq", y_perm(1))]
     bwd = [lax.ppermute(block, "seq", y_perm(-1))]
@@ -239,16 +278,27 @@
     half = lax.ppermute(jnp.where(core == 0, fwd[-1], bwd[-1]), "seq", turn)
 
     state_shapes = [M_SHAPE, ACC_SHAPE, M_SHAPE, ACC_SHAPE]
+    m0, a0 = pl.pallas_call(
+        local_kernel,
+        out_shape=[M_SHAPE, ACC_SHAPE],
+        in_specs=[SMEM] + [VMEM] * 2,
+        out_specs=[VMEM] * 2,
+        scratch_shapes=[pltpu.VMEM((TOK, 2 * HEAD), BF16)],
+        compiler_params=params(),
+        cost_estimate=cost(512, 1),
+        name="attend_local",
+    )(c, queries, kv)
     state = pl.pallas_call(
-        first_kernel,
+        chip_kernel,
         out_shape=state_shapes,
         in_specs=[SMEM, SMEM] + [VMEM] * 5,
         out_specs=[VMEM] * 4,
-        scratch_shapes=[pltpu.VMEM((MSG, HEAD), BF16)] + scratch(4) + [pltpu.VMEM((TOK, 2 * HEAD), BF16)],
-        compiler_params=params(),
-        cost_estimate=cost(640, 2),
+        scratch_shapes=scratch(4),
+        input_output_aliases={5: 0, 6: 1},
+        compiler_params=params(),
+        cost_estimate=cost(512, 2),
         name="attend_own_chip",
-    )(me_s, c, queries, other_queries, keys, values, block)
+    )(me_s, c, queries, other_queries, block, m0, a0)
     for step in range(1, 4):
         state = pl.pallas_call(
             functools.partial(ring_kernel, step),
@@ -288,73 +338,86 @@
 
     wide_cols = out_weight.shape[1] // (NX * NH)
 
-    def far_cols(i, tp_ref):
-        return (0, i * NX + (tp_ref[0] + 2) % NX)
-
-    def rest_cols(i, tp_ref):
-        g = i // 2
-        d = jnp.where(g == 2, 0, 1 + 2 * g)
-        return (0, (i % 2) * NX + (tp_ref[0] + d) % NX)
-
-    whole = lambda *shape: pl.BlockSpec(shape, lambda i, tp_ref: (0,) * len(shape))
-    att, far_part = pl.pallas_call(
+    def columns(own_half, j, tp_ref):
+        half = tp_ref[0] // NX
+        return (0, (half if own_half else 1 - half) * NX + j)
+
+    whole = lambda *shape: pl.BlockSpec(shape, lambda j, tp_ref: (0,) * len(shape))
+    weights = lambda own_half: pl.BlockSpec((HEADS * HEAD, wide_cols), functools.partial(columns, own_half))
+    parts = pl.BlockSpec((1, TOK, wide_cols), lambda j, tp_ref: (j, 0, 0))
+    parts_shape = jax.ShapeDtypeStruct((NX, TOK, wide_cols), BF16)
+    att, there = pl.pallas_call(
         merge_kernel,
-        out_shape=[
-            jax.ShapeDtypeStruct((TOK, HEADS * HEAD), BF16),
-            jax.ShapeDtypeStruct((2, TOK, wide_cols), BF16),
-        ],
+        out_shape=[jax.ShapeDtypeStruct((TOK, HEADS * HEAD), BF16), parts_shape],
         grid_spec=pltpu.PrefetchScalarGridSpec(
             num_scalar_prefetch=1,
-            grid=(2,),
+            grid=(NX,),
             in_specs=[
                 whole(HEADS, TOK, HEAD),
                 whole(HEADS, TOK, 2 * HEAD),
                 whole(HEADS, TOK, 2 * HEAD),
-                pl.BlockSpec((HEADS * HEAD, wide_cols), far_cols),
+                weights(False),
             ],
-            out_specs=[
-                whole(TOK, HEADS * HEAD),
-                pl.BlockSpec((1, TOK, wide_cols), lambda i, tp_ref: (i, 0, 0)),
-            ],
+            out_specs=[whole(TOK, HEADS * HEAD), parts],
         ),
         compiler_params=params(),
-        cost_estimate=pl.CostEstimate(flops=1 << 28, bytes_accessed=5 << 20, transcendentals=1 << 18),
+        cost_estimate=pl.CostEstimate(flops=1 << 31, bytes_accessed=5 << 20, transcendentals=1 << 18),
         name="merge_project",
     )(tp_s, m0, a0, got, out_weight)
-    right = [(i, (i // NX) * NX + (i + 1) % NX) for i in range(NX * NH)]
-    left = [(i, (i // NX) * NX + (i + NX - 1) % NX) for i in range(NX * NH)]
-    from_left = lax.ppermute(far_part[0], "tp", right)
-    from_right = lax.ppermute(far_part[1], "tp", left)
-    rest = pl.pallas_call(
-        rest_kernel,
-        out_shape=jax.ShapeDtypeStruct((6, TOK, wide_cols), BF16),
+    here = pl.pallas_call(
+        project_kernel,
+        out_shape=parts_shape,
         grid_spec=pltpu.PrefetchScalarGridSpec(
             num_scalar_prefetch=1,
-            grid=(6,),
-            in_specs=[
-                whole(TOK, HEADS * HEAD),
-                pl.BlockSpec((HEADS * HEAD, wide_cols), rest_cols),
-            ],
-            out_specs=pl.BlockSpec((1, TOK, wide_cols), lambda i, tp_ref: (i, 0, 0)),
+            grid=(NX,),
+            in_specs=[whole(TOK, HEADS * HEAD), weights(True)],
+            out_specs=parts,
         ),
-        compiler_params=params(),
-        cost_estimate=pl.CostEstimate(flops=3 << 28, bytes_accessed=5 << 20, transcendentals=0),
-        name="project_rest",
+        compiler_params=params(56),
+        cost_estimate=pl.CostEstimate(flops=1 << 31, bytes_accessed=2 << 20, transcendentals=0),
+        name="project_own_half",
     )(tp_s, att, out_weight)
-    to_right = jnp.stack([rest[0] + from_left, rest[1]])
-    to_left = jnp.stack([rest[2], rest[3] + from_right])
-    from_left = lax.ppermute(to_right, "tp", right)
-    from_right = lax.ppermute(to_left, "tp", left)
-    summed = rest[4:6].astype(F32) + from_left.astype(F32) + from_right.astype(F32)
-    send = jnp.where(hi == 0, summed[1], summed[0]).astype(BF16)
-    keep = jnp.where(hi == 0, summed[0], summed[1])
+    rows = [[h * NX + x for x in range(NX)] for h in range(NH)]
     swap = [(i, (i + NX) % (NX * NH)) for i in range(NX * NH)]
-    projected = keep + lax.ppermute(send, "tp", swap).astype(F32)
-    squares = jnp.sum(projected * projected, -1)
-    squares = lax.psum(squares, "tp", axis_index_groups=[list(range(NX)), list(range(NX, 2 * NX))])
-    squares = lax.psum(squares, "tp", axis_index_groups=[[i, i + NX] for i in range(NX)])
-    mean_square = squares[:, None] / out_weight.shape[1]
-    return (projected * lax.rsqrt(mean_square + 1e-05) * norm_gain[None, :]).astype(BF16)
+    there = lax.all_to_all(there, "tp", 0, 0, axis_index_groups=rows)
+    there = pl.pallas_call(
+        sum_kernel,
+        out_shape=jax.ShapeDtypeStruct((TOK, wide_cols), BF16),
+        in_specs=[VMEM],
+        out_specs=VMEM,
+        compiler_params=params(),
+        name="sum_other_half",
+    )(there)
+    crossed = pl.pallas_call(
+        widen_kernel,
+        out_shape=jax.ShapeDtypeStruct((TOK, wide_cols), F32),
+        in_specs=[VMEM],
+        out_specs=VMEM,
+        compiler_params=params(),
+        cost_estimate=pl.CostEstimate(flops=1 << 33, bytes_accessed=1 << 20, transcendentals=0),
+        name="widen_crossed",
+    )(lax.ppermute(there, "tp", swap))
+    here = lax.all_to_all(here, "tp", 0, 0, axis_index_groups=rows)
+    projected, squares = pl.pallas_call(
+        square_kernel,
+        out_shape=[
+            jax.ShapeDtypeStruct((TOK, wide_cols), F32),
+            jax.ShapeDtypeStruct((NX * NH, 8, TOK), F32),
+        ],
+        in_specs=[VMEM] * 2,
+        out_specs=[VMEM] * 2,
+        compiler_params=params(),
+        name="sum_and_square",
+    )(here, crossed)
+    squares = lax.all_to_all(squares, "tp", 0, 0)
+    return pl.pallas_call(
+        functools.partial(norm_kernel, out_weight.shape[1]),
+        out_shape=jax.ShapeDtypeStruct((TOK, wide_cols), BF16),
+        in_specs=[VMEM] * 3,
+        out_specs=VMEM,
+        compiler_params=params(),
+        name="normalize",
+    )(projected, squares, norm_gain.reshape(1, wide_cols))
 
 
 def solution(mesh):

time: 148 us -> 142 us (0.959)
  the two profiles are of different devices: /device:TPU:200 before, /device:TPU:56 now
where the time goes in v3:
time: 142 us; the launch traced here: 141 us
  starting transfers between devices  50.3 us (35%)
  blocking collectives  32.5 us (23%)
  waiting for transfers between devices  26 us (18%)
  Pallas kernels  24.8 us (17%)
  local copies, waits for them, and re-layouts  5.97 us (4%)
  between operations  1.73 us (1%)
    all_to_all x1, blocking collectives, shards(): there = lax.all_to_all(there, 'tp', 0, 0, axis_index_groups=rows)  19.8 us
    all_to_all x1, blocking collectives, shards(): squares = lax.all_to_all(squares, 'tp', 0, 0)  12.6 us
    pallas_call x3, Pallas kernels, shards(): pl.pallas_call(functools.partial(ring_kernel, step), out_shape=state_shap...  12 us
    all_to_all x1, waiting for transfers between devices, shards(): here = lax.all_to_all(here, 'tp', 0, 0, axis_index_groups=rows)  10.8 us
    ppermute x2, starting transfers between devices, shards(): fwd.append(lax.ppermute(fwd[-1], 'seq', y_perm(1)))  10.7 us
    ppermute x1, starting transfers between devices, shards(): lax.ppermute(there, 'tp', swap)  8.22 us
    ppermute x1, starting transfers between devices, shards(): fwd = [lax.ppermute(block, 'seq', y_perm(1))]  7.65 us
    all_to_all x1, starting transfers between devices, shards(): lax.all_to_all(jnp.broadcast_to(own, (NZ, SLOT, HEAD)), 'seq', 0, 0, axis...  7.26 us
  transfers between devices with their start and end apart: 14, of which 7 were waited for; matrix products, arithmetic and copies ran while one was open for 1% of the time, Pallas kernels for 14%

profile of v3, /device:TPU:56, one launch (start us, length us, event | category | flops | bytes accessed | tf_op | source)
XLA Modules:
  0.0 141.4 jit_solution(8370524673092383513)
XLA Ops:
  3.2 7.3 %all-to-all-start = ((bf16[4,256,128]{2,1,0:T(8,128)(2,1)}), bf16[4,256,128]{2,1,0:T(8,128)(2,1)S(1)}, u32[]{:S(2)}, u32[]{:S(2)}) async-start(bf16[4,256,128]{2,1,0:T(8,128)(2,1)} %broadcast_in_dim.3), calls=%async_computation | async-start | bytes 524288 | tf_op jit(solution)/shard_map/all_to_all | solution.py:257
  13.4 1.9 %collective-permute-start.9 = (bf16[256,512]{1,0:T(8,128)(2,1)}, bf16[256,512]{1,0:T(8,128)(2,1)S(1)}, u32[]{:S(2)}, u32[]{:S(2)}) collective-permute-start(bf16[256,512]{1,0:T(8,128)(2,1)} %q.3), channel_id=1, source_target_pairs={{0,8},{8,0},{16,24},{24,16},{32,40},{40,32},{48,56},{56,48},{64,72... | collective-permute-start | bytes 786440 | tf_op jit(solution)/shard_map/ppermute | solution.py:265
  16.0 3.4 %all-to-all-done = bf16[4,256,128]{2,1,0:T(8,128)(2,1)S(1)} async-done(((bf16[4,256,128]{2,1,0:T(8,128)(2,1)}), bf16[4,256,128]{2,1,0:T(8,128)(2,1)S(1)}, u32[]{:S(2)}, u32[]{:S(2)}) %all-to-all-start) | async-done | bytes 262176 | tf_op jit(solution)/shard_map/all_to_all | solution.py:257
  19.4 7.7 %collective-permute-start.2 = (bf16[1024,128]{1,0:T(8,128)(2,1)S(1)}, bf16[1024,128]{1,0:T(8,128)(2,1)S(1)}, u32[]{:S(2)}, u32[]{:S(2)}) collective-permute-start(bf16[1024,128]{1,0:T(8,128)(2,1)S(1)} %pad_maximum_fusion.blk), channel_id=1, source_target_pairs={{0,16},{8,24},{16,32},{24,40},{32,48},{40,56},{48,64},{56,72},{64,... | collective-permute-start | bytes 786440 | tf_op jit(solution)/shard_map/ppermute | solution.py:272
  27.1 1.9 %collective-permute-start.5 = (bf16[1024,128]{1,0:T(8,128)(2,1)S(1)}, bf16[1024,128]{1,0:T(8,128)(2,1)S(1)}, u32[]{:S(2)}, u32[]{:S(2)}) collective-permute-start(bf16[1024,128]{1,0:T(8,128)(2,1)S(1)} %pad_maximum_fusion.blk), channel_id=1, source_target_pairs={{0,112},{8,120},{16,0},{24,8},{32,16},{40,24},{48,32},{56,40},{64,... | collective-permute-start | bytes 786440 | tf_op jit(solution)/shard_map/ppermute | solution.py:273
  33.3 5.6 %collective-permute-start.3 = (bf16[1024,128]{1,0:T(8,128)(2,1)S(1)}, bf16[1024,128]{1,0:T(8,128)(2,1)S(1)}, u32[]{:S(2)}, u32[]{:S(2)}) collective-permute-start(bf16[1024,128]{1,0:T(8,128)(2,1)S(1)} %collective-permute-done.2.fwd), channel_id=1, source_target_pairs={{0,16},{8,24},{16,32},{24,40},{32,48},{40,56},{48,64},{56,72},{64,... | collective-permute-start | bytes 786440 | tf_op jit(solution)/shard_map/ppermute | solution.py:275
  38.9 1.9 %collective-permute-start.6 = (bf16[1024,128]{1,0:T(8,128)(2,1)S(1)}, bf16[1024,128]{1,0:T(8,128)(2,1)S(1)}, u32[]{:S(2)}, u32[]{:S(2)}) collective-permute-start(bf16[1024,128]{1,0:T(8,128)(2,1)S(1)} %collective-permute-done.5.bwd), channel_id=1, source_target_pairs={{0,112},{8,120},{16,0},{24,8},{32,16},{40,24},{48,32},{56,40},{64,... | collective-permute-start | bytes 786440 | tf_op jit(solution)/shard_map/ppermute | solution.py:276
  40.8 4.0 %attend_ring.3 = (f32[4,256,128]{2,1,0:T(8,128)S(1)}, f32[4,256,256]{2,1,0:T(8,128)S(1)}, f32[4,256,128]{2,1,0:T(8,128)S(1)}, f32[4,256,256]{2,1,0:T(8,128)S(1)}) custom-call(s32[1]{0:T(128)} %bitcast.1.me_ref, f32[1]{0:T(128)S(6)} %mul.9.c_ref, ...), custom_call_target="tpu_custom_call", output_to_operand_aliasing={{0}: (6, {}), {1}: (7, {}), {2}: (8, {}), {3}: (9, {})} | custom-call | flops 5368709120 | bytes 4194304 | tf_op jit(solution)/shard_map/attend_ring/pallas_call | solution.py:303
  44.9 5.1 %collective-permute-start.4 = (bf16[1024,128]{1,0:T(8,128)(2,1)S(1)}, bf16[1024,128]{1,0:T(8,128)(2,1)S(1)}, u32[]{:S(2)}, u32[]{:S(2)}) collective-permute-start(bf16[1024,128]{1,0:T(8,128)(2,1)S(1)} %collective-permute-done.3.fwd), channel_id=1, source_target_pairs={{0,16},{8,24},{16,32},{24,40},{32,48},{40,56},{48,64},{56,72},{64,... | collective-permute-start | bytes 786440 | tf_op jit(solution)/shard_map/ppermute | solution.py:275
  49.9 1.9 %collective-permute-start.7 = (bf16[1024,128]{1,0:T(8,128)(2,1)S(1)}, bf16[1024,128]{1,0:T(8,128)(2,1)S(1)}, u32[]{:S(2)}, u32[]{:S(2)}) collective-permute-start(bf16[1024,128]{1,0:T(8,128)(2,1)S(1)} %collective-permute-done.6.bwd), channel_id=1, source_target_pairs={{0,112},{8,120},{16,0},{24,8},{32,16},{40,24},{48,32},{56,40},{64,... | collective-permute-start | bytes 786440 | tf_op jit(solution)/shard_map/ppermute | solution.py:276
  51.9 4.0 %attend_ring.4 = (f32[4,256,128]{2,1,0:T(8,128)S(1)}, f32[4,256,256]{2,1,0:T(8,128)S(1)}, f32[4,256,128]{2,1,0:T(8,128)S(1)}, f32[4,256,256]{2,1,0:T(8,128)S(1)}) custom-call(s32[1]{0:T(128)} %bitcast.1.me_ref, f32[1]{0:T(128)S(6)} %mul.9.c_ref, ...), custom_call_target="tpu_custom_call", output_to_operand_aliasing={{0}: (6, {}), {1}: (7, {}), {2}: (8, {}), {3}: (9, {})} | custom-call | flops 5368709120 | bytes 4194304 | tf_op jit(solution)/shard_map/attend_ring/pallas_call | solution.py:303
  55.9 3.9 %collective-permute-done.7.bwd = bf16[1024,128]{1,0:T(8,128)(2,1)S(1)} collective-permute-done((bf16[1024,128]{1,0:T(8,128)(2,1)S(1)}, bf16[1024,128]{1,0:T(8,128)(2,1)S(1)}, u32[]{:S(2)}, u32[]{:S(2)}) %collective-permute-start.7) | collective-permute-done | bytes 262176 | tf_op jit(solution)/shard_map/ppermute | solution.py:276
  59.8 2.1 %collective-permute-start.8 = (bf16[1024,128]{1,0:T(8,128)(2,1)S(1)}, bf16[1024,128]{1,0:T(8,128)(2,1)S(1)}, u32[]{:S(2)}, u32[]{:S(2)}) collective-permute-start(bf16[1024,128]{1,0:T(8,128)(2,1)S(1)} %broadcast_select_fusion), channel_id=1, source_target_pairs={{0,16},{8,120},{16,32},{24,8},{32,48},{40,24},{48,64},{56,40},{64,... | collective-permute-start | bytes 786440 | tf_op jit(solution)/shard_map/ppermute | solution.py:278
  61.9 4.0 %attend_ring.5 = (f32[4,256,128]{2,1,0:T(8,128)S(1)}, f32[4,256,256]{2,1,0:T(8,128)S(1)}, f32[4,256,128]{2,1,0:T(8,128)S(1)}, f32[4,256,256]{2,1,0:T(8,128)S(1)}) custom-call(s32[1]{0:T(128)} %bitcast.1.me_ref, f32[1]{0:T(128)S(6)} %mul.9.c_ref, ...), custom_call_target="tpu_custom_call", output_to_operand_aliasing={{0}: (6, {}), {1}: (7, {}), {2}: (8, {}), {3}: (9, {})} | custom-call | flops 5368709120 | bytes 4194304 | tf_op jit(solution)/shard_map/attend_ring/pallas_call | solution.py:303
  65.9 2.2 %collective-permute-done.8.blk = bf16[1024,128]{1,0:T(8,128)(2,1)S(1)} collective-permute-done((bf16[1024,128]{1,0:T(8,128)(2,1)S(1)}, bf16[1024,128]{1,0:T(8,128)(2,1)S(1)}, u32[]{:S(2)}, u32[]{:S(2)}) %collective-permute-start.8) | collective-permute-done | bytes 262176 | tf_op jit(solution)/shard_map/ppermute | solution.py:278
  69.6 1.9 %collective-permute-start.10 = (bf16[4,256,256]{2,1,0:T(8,128)(2,1)S(1)}, bf16[4,256,256]{2,1,0:T(8,128)(2,1)S(1)}, u32[]{:S(2)}, u32[]{:S(2)}) collective-permute-start(bf16[4,256,256]{2,1,0:T(8,128)(2,1)S(1)} %get-tuple-element.50), channel_id=1, source_target_pairs={{0,8},{8,0},{16,24},{24,16},{32,40},{40,32},{48,56},{56,48},{64,72... | collective-permute-start | bytes 1572872 | tf_op jit(solution)/shard_map/ppermute | solution.py:326
  73.7 2.1 %merge_project.1 = (bf16[256,512]{1,0:T(8,128)(2,1)S(1)}, bf16[4,256,512]{2,1,0:T(8,128)(2,1)S(1)}) custom-call(s32[1]{0:T(128)} %bitcast.tp_ref, f32[4,256,128]{2,1,0:T(8,128)S(1)} %get-tuple-element.46.m, f32[4,256,256]{2,1,0:T(8,128)S(1)} %get-tuple-element.47.a, bf16[4,256,256]{2,1,0:T(8,128)(2,1)S(1)} %collective-permute-done.10.got, ...), custom_call_target="tpu_custom_call" | custom-call | flops 2147483648 | bytes 5242880 | tf_op jit(solution)/shard_map/merge_project/pallas_call | solution.py:349
  76.6 19.8 %all_to_all.20.parts = bf16[4,256,512]{2,1,0:T(8,128)(2,1)S(1)} all-to-all(bf16[4,256,512]{2,1,0:T(8,128)(2,1)S(1)} %get-tuple-element.52), channel_id=1, replica_groups={{0,1,2,3},{4,5,6,7},{8,9,10,11},{12,13,14,15},{16,17,18,19},{20,21,22,2..., dimensions={0} | all-to-all | bytes 2097152 | tf_op jit(solution)/shard_map/all_to_all | solution.py:382
  96.5 8.2 %collective-permute-start.11 = (bf16[256,512]{1,0:T(8,128)(2,1)S(1)}, bf16[256,512]{1,0:T(8,128)(2,1)S(1)}, u32[]{:S(2)}, u32[]{:S(2)}) collective-permute-start(bf16[256,512]{1,0:T(8,128)(2,1)S(1)} %sum_other_half.1), channel_id=1, source_target_pairs={{0,4},{1,5},{2,6},{3,7},{4,0},{5,1},{6,2},{7,3},{8,12},{9,13},{10,... | collective-permute-start | bytes 786440 | tf_op jit(solution)/shard_map/ppermute | solution.py:399
  104.8 4.3 %project_own_half.1 = bf16[4,256,512]{2,1,0:T(8,128)(2,1)} custom-call(s32[1]{0:T(128)} %bitcast.tp_ref, bf16[256,512]{1,0:T(8,128)(2,1)} %copy-done.4, bf16[512,4096]{1,0:T(8,128)(2,1)} %w.3), custom_call_target="tpu_custom_call" | custom-call | flops 2147483648 | bytes 2097152 | tf_op jit(solution)/shard_map/project_own_half/pallas_call | solution.py:367
  109.0 3.5 %all-to-all-start.1 = ((bf16[4,256,512]{2,1,0:T(8,128)(2,1)}), bf16[4,256,512]{2,1,0:T(8,128)(2,1)S(1)}, u32[]{:S(2)}, u32[]{:S(2)}) async-start(bf16[4,256,512]{2,1,0:T(8,128)(2,1)} %project_own_half.1), calls=%async_computation.1 | async-start | bytes 2097152 | tf_op jit(solution)/shard_map/all_to_all | solution.py:400
  112.5 3.7 %collective-permute-done.11.part = bf16[256,512]{1,0:T(8,128)(2,1)S(1)} collective-permute-done((bf16[256,512]{1,0:T(8,128)(2,1)S(1)}, bf16[256,512]{1,0:T(8,128)(2,1)S(1)}, u32[]{:S(2)}, u32[]{:S(2)}) %collective-permute-start.11) | collective-permute-done | bytes 262176 | tf_op jit(solution)/shard_map/ppermute | solution.py:399
  116.3 10.8 %all-to-all-done.1.parts = bf16[4,256,512]{2,1,0:T(8,128)(2,1)S(1)} async-done(((bf16[4,256,512]{2,1,0:T(8,128)(2,1)}), bf16[4,256,512]{2,1,0:T(8,128)(2,1)S(1)}, u32[]{:S(2)}, u32[]{:S(2)}) %all-to-all-start.1) | async-done | bytes 1048608 | tf_op jit(solution)/shard_map/all_to_all | solution.py:400
  127.8 12.6 %all_to_all.21.squares = f32[8,8,256]{2,1,0:T(8,128)S(1)} all-to-all(f32[8,8,256]{2,1,0:T(8,128)S(1)} %get-tuple-element.54), channel_id=1, replica_groups=mesh['seq'=64,'tp'=8] {'tp'}, dimensions={0} | all-to-all | bytes 131072 | tf_op jit(solution)/shard_map/all_to_all | solution.py:412
  (42 shorter events, 15.8 us)
Async XLA Ops:
  0.0 30.6 %copy-start.3 = (bf16[256,512]{1,0:T(8,128)(2,1)S(1)}, bf16[256,512]{1,0:T(8,128)(2,1)}, u32[]{:S(2)}) copy-start(bf16[256,512]{1,0:T(8,128)(2,1)} %q.3) | copy-start | bytes 786436
  3.2 16.2 %all-to-all-start = ((bf16[4,256,128]{2,1,0:T(8,128)(2,1)}), bf16[4,256,128]{2,1,0:T(8,128)(2,1)S(1)}, u32[]{:S(2)}, u32[]{:S(2)}) async-start(bf16[4,256,128]{2,1,0:T(8,128)(2,1)} %broadcast_in_dim.3), calls=%async_computation | async-start | bytes 524288 | tf_op jit(solution)/shard_map/all_to_all | solution.py:257
  12.0 0.7 collective-permute-start
  12.7 3.3 %collective-permute-start.1 = (bf16[256,128]{1,0:T(8,128)(2,1)S(1)}, bf16[256,128]{1,0:T(8,128)(2,1)S(1)}, u32[]{:S(2)}, u32[]{:S(2)}) collective-permute-start(bf16[256,128]{1,0:T(8,128)(2,1)S(1)} %broadcast_select_fusion.1), channel_id=1, source_target_pairs={{0,248},{504,376},{1,249},{505,377},{2,250},{506,378},{3,251},{507... | collective-permute-start | bytes 196616 | tf_op jit(solution)/shard_map/ppermute | solution.py:264
  13.4 17.3 %collective-permute-start.9 = (bf16[256,512]{1,0:T(8,128)(2,1)}, bf16[256,512]{1,0:T(8,128)(2,1)S(1)}, u32[]{:S(2)}, u32[]{:S(2)}) collective-permute-start(bf16[256,512]{1,0:T(8,128)(2,1)} %q.3), channel_id=1, source_target_pairs={{0,8},{8,0},{16,24},{24,16},{32,40},{40,32},{48,56},{56,48},{64,72... | collective-permute-start | bytes 786440 | tf_op jit(solution)/shard_map/ppermute | solution.py:265
  19.4 13.9 %collective-permute-start.2 = (bf16[1024,128]{1,0:T(8,128)(2,1)S(1)}, bf16[1024,128]{1,0:T(8,128)(2,1)S(1)}, u32[]{:S(2)}, u32[]{:S(2)}) collective-permute-start(bf16[1024,128]{1,0:T(8,128)(2,1)S(1)} %pad_maximum_fusion.blk), channel_id=1, source_target_pairs={{0,16},{8,24},{16,32},{24,40},{32,48},{40,56},{48,64},{56,72},{64,... | collective-permute-start | bytes 786440 | tf_op jit(solution)/shard_map/ppermute | solution.py:272
  27.1 11.8 %collective-permute-start.5 = (bf16[1024,128]{1,0:T(8,128)(2,1)S(1)}, bf16[1024,128]{1,0:T(8,128)(2,1)S(1)}, u32[]{:S(2)}, u32[]{:S(2)}) collective-permute-start(bf16[1024,128]{1,0:T(8,128)(2,1)S(1)} %pad_maximum_fusion.blk), channel_id=1, source_target_pairs={{0,112},{8,120},{16,0},{24,8},{32,16},{40,24},{48,32},{56,40},{64,... | collective-permute-start | bytes 786440 | tf_op jit(solution)/shard_map/ppermute | solution.py:273
  29.0 1.0 copy-start.2
  33.3 11.5 %collective-permute-start.3 = (bf16[1024,128]{1,0:T(8,128)(2,1)S(1)}, bf16[1024,128]{1,0:T(8,128)(2,1)S(1)}, u32[]{:S(2)}, u32[]{:S(2)}) collective-permute-start(bf16[1024,128]{1,0:T(8,128)(2,1)S(1)} %collective-permute-done.2.fwd), channel_id=1, source_target_pairs={{0,16},{8,24},{16,32},{24,40},{32,48},{40,56},{48,64},{56,72},{64,... | collective-permute-start | bytes 786440 | tf_op jit(solution)/shard_map/ppermute | solution.py:275
  38.9 11.0 %collective-permute-start.6 = (bf16[1024,128]{1,0:T(8,128)(2,1)S(1)}, bf16[1024,128]{1,0:T(8,128)(2,1)S(1)}, u32[]{:S(2)}, u32[]{:S(2)}) collective-permute-start(bf16[1024,128]{1,0:T(8,128)(2,1)S(1)} %collective-permute-done.5.bwd), channel_id=1, source_target_pairs={{0,112},{8,120},{16,0},{24,8},{32,16},{40,24},{48,32},{56,40},{64,... | collective-permute-start | bytes 786440 | tf_op jit(solution)/shard_map/ppermute | solution.py:276
  44.9 11.0 %collective-permute-start.4 = (bf16[1024,128]{1,0:T(8,128)(2,1)S(1)}, bf16[1024,128]{1,0:T(8,128)(2,1)S(1)}, u32[]{:S(2)}, u32[]{:S(2)}) collective-permute-start(bf16[1024,128]{1,0:T(8,128)(2,1)S(1)} %collective-permute-done.3.fwd), channel_id=1, source_target_pairs={{0,16},{8,24},{16,32},{24,40},{32,48},{40,56},{48,64},{56,72},{64,... | collective-permute-start | bytes 786440 | tf_op jit(solution)/shard_map/ppermute | solution.py:275
  49.9 9.9 %collective-permute-start.7 = (bf16[1024,128]{1,0:T(8,128)(2,1)S(1)}, bf16[1024,128]{1,0:T(8,128)(2,1)S(1)}, u32[]{:S(2)}, u32[]{:S(2)}) collective-permute-start(bf16[1024,128]{1,0:T(8,128)(2,1)S(1)} %collective-permute-done.6.bwd), channel_id=1, source_target_pairs={{0,112},{8,120},{16,0},{24,8},{32,16},{40,24},{48,32},{56,40},{64,... | collective-permute-start | bytes 786440 | tf_op jit(solution)/shard_map/ppermute | solution.py:276
  59.8 8.3 %collective-permute-start.8 = (bf16[1024,128]{1,0:T(8,128)(2,1)S(1)}, bf16[1024,128]{1,0:T(8,128)(2,1)S(1)}, u32[]{:S(2)}, u32[]{:S(2)}) collective-permute-start(bf16[1024,128]{1,0:T(8,128)(2,1)S(1)} %broadcast_select_fusion), channel_id=1, source_target_pairs={{0,16},{8,120},{16,32},{24,8},{32,48},{40,24},{48,64},{56,40},{64,... | collective-permute-start | bytes 786440 | tf_op jit(solution)/shard_map/ppermute | solution.py:278
  69.6 3.8 %collective-permute-start.10 = (bf16[4,256,256]{2,1,0:T(8,128)(2,1)S(1)}, bf16[4,256,256]{2,1,0:T(8,128)(2,1)S(1)}, u32[]{:S(2)}, u32[]{:S(2)}) collective-permute-start(bf16[4,256,256]{2,1,0:T(8,128)(2,1)S(1)} %get-tuple-element.50), channel_id=1, source_target_pairs={{0,8},{8,0},{16,24},{24,16},{32,40},{40,32},{48,56},{56,48},{64,72... | collective-permute-start | bytes 1572872 | tf_op jit(solution)/shard_map/ppermute | solution.py:326
  71.5 2.2 %copy-start.1 = (bf16[512,4096]{1,0:T(8,128)(2,1)S(1)}, bf16[512,4096]{1,0:T(8,128)(2,1)}, u32[]{:S(2)}) copy-start(bf16[512,4096]{1,0:T(8,128)(2,1)} %w.3) | copy-start | bytes 12582916
  75.8 0.7 copy-start.4
  96.5 19.7 %collective-permute-start.11 = (bf16[256,512]{1,0:T(8,128)(2,1)S(1)}, bf16[256,512]{1,0:T(8,128)(2,1)S(1)}, u32[]{:S(2)}, u32[]{:S(2)}) collective-permute-start(bf16[256,512]{1,0:T(8,128)(2,1)S(1)} %sum_other_half.1), channel_id=1, source_target_pairs={{0,4},{1,5},{2,6},{3,7},{4,0},{5,1},{6,2},{7,3},{8,12},{9,13},{10,... | collective-permute-start | bytes 786440 | tf_op jit(solution)/shard_map/ppermute | solution.py:399
  109.0 18.1 %all-to-all-start.1 = ((bf16[4,256,512]{2,1,0:T(8,128)(2,1)}), bf16[4,256,512]{2,1,0:T(8,128)(2,1)S(1)}, u32[]{:S(2)}, u32[]{:S(2)}) async-start(bf16[4,256,512]{2,1,0:T(8,128)(2,1)} %project_own_half.1), calls=%async_computation.1 | async-start | bytes 2097152 | tf_op jit(solution)/shard_map/all_to_all | solution.py:400
  112.5 27.9 %copy-start = (f32[512]{0:T(512)S(1)}, f32[512]{0:T(512)}, u32[]{:S(2)}) copy-start(f32[512]{0:T(512)} %param.13) | copy-start | bytes 6148

commit v4 on v3

--- a/solution.py
+++ b/solution.py
@@ -99,14 +99,14 @@
             update(c, q_ref[:, h * HEAD : (h + 1) * HEAD], kk, vv, m_ref, acc_ref, h)
 
 
-def local_kernel(c_ref, q, kv, m, a, lv):
-    lv[:, 0:HEAD] = kv[:, HEAD:]
+def local_kernel(c_ref, q, k, v, m, a, lv):
+    lv[:, 0:HEAD] = v[...]
     lv[:, HEAD : 2 * HEAD] = jnp.ones((TOK, HEAD), BF16)
     c = c_ref[0]
     row = lax.broadcasted_iota(jnp.int32, (TOK, TOK), 0)
     col = lax.broadcasted_iota(jnp.int32, (TOK, TOK), 1)
     for h in range(HEADS):
-        s = cross(q[:, h * HEAD : (h + 1) * HEAD], kv[:, 0:HEAD]) * c
+        s = cross(q[:, h * HEAD : (h + 1) * HEAD], k[...]) * c
         s = jnp.where(row >= col, s, LOW)
         top = jnp.broadcast_to(jnp.max(s, axis=1, keepdims=True), (TOK, HEAD))
         p = jnp.exp2(s - wide(top, TOK // HEAD)).astype(BF16)
@@ -187,8 +187,11 @@
     out[0] = plain(att[...], w[...]).astype(BF16)
 
 
-def project_kernel(tp_ref, att, w, out):
-    out[0] = plain(att[...], w[...]).astype(BF16)
+def project_kernel(tp_ref, att, w, *outs):
+    x, half = tp_ref[0] % NX, tp_ref[0] // NX
+    for k, out in enumerate(outs):
+        col = pl.multiple_of((half * NX + (x + k) % NX) * out.shape[1], out.shape[1])
+        out[...] = plain(att[...], w[:, pl.ds(col, out.shape[1])]).astype(BF16)
 
 
 def sum_kernel(parts, out):
@@ -198,14 +201,23 @@
     out[...] = total.astype(out.dtype)
 
 
-def widen_kernel(part, out):
-    out[...] = part[...].astype(F32)
-
-
-def square_kernel(parts, crossed, out, squares):
-    total = crossed[...]
-    for j in range(NX):
-        total += parts[j].astype(F32)
+def choose_kernel(me_ref, here, there, out):
+    last = me_ref[0] == NZ * NY * NC - 1
+
+    @pl.when(last)
+    def _():
+        out[...] = there[...]
+
+    @pl.when(jnp.logical_not(last))
+    def _():
+        out[...] = here[...]
+
+
+def square_kernel(crossed, *refs):
+    *parts, out, squares = refs
+    total = crossed[...].astype(F32)
+    for part in parts:
+        total += part[...].astype(F32)
     out[...] = total
     ones = jnp.ones((8, total.shape[1]), F32)
     sums = lax.dot_general(
@@ -250,9 +262,10 @@
     tp_s = tp.reshape(1)
     c = key_head_scale * (LOG2E / math.sqrt(HEAD))
 
-    kv = jnp.concatenate([keys, values], 1)
-    own = lax.dynamic_slice_in_dim(kv, retained[0, 0] * BLOCK, BLOCK, 0)
-    own = jnp.concatenate([own[:, :HEAD], own[:, HEAD:]], 0)
+    row = retained[0, 0] * BLOCK
+    own = jnp.concatenate(
+        [lax.dynamic_slice_in_dim(part, row, BLOCK, 0) for part in (keys, values)], 0
+    )
     planes = [[sid(z_, y_, c_) for z_ in range(NZ)] for y_ in range(NY) for c_ in range(NC)]
     stack = lax.all_to_all(
         jnp.broadcast_to(own, (NZ, SLOT, HEAD)), "seq", 0, 0, axis_index_groups=planes
@@ -260,7 +273,15 @@
     holders = [sid(z_, NY - 1, 1) for z_ in range(NZ)]
     anchor = jnp.concatenate([keys[:BLOCK], values[:BLOCK]], 0)
     far = lax.ppermute(anchor, "seq", [(0, holders[3])])
-    anchor = jnp.where(me == holders[3], far, anchor)
+    anchor = pl.pallas_call(
+        choose_kernel,
+        out_shape=jax.ShapeDtypeStruct((SLOT, HEAD), BF16),
+        in_specs=[SMEM] + [VMEM] * 2,
+        out_specs=VMEM,
+        compiler_params=params(),
+        cost_estimate=pl.CostEstimate(flops=1 << 33, bytes_accessed=1 << 17, transcendentals=0),
+        name="choose_anchor",
+    )(me_s, anchor, far)
     near = lax.ppermute(anchor, "seq", [(0, holders[1]), (holders[3], holders[2])])
     other_queries = lax.ppermute(queries, "seq", [(sid(*s), sid(s[0], s[1], 1 - s[2])) for s in PLACES])
     placed = jnp.where(jnp.logical_or(me == holders[1], me == holders[2]), near, anchor)
@@ -281,13 +302,13 @@
     m0, a0 = pl.pallas_call(
         local_kernel,
         out_shape=[M_SHAPE, ACC_SHAPE],
-        in_specs=[SMEM] + [VMEM] * 2,
+        in_specs=[SMEM] + [VMEM] * 3,
         out_specs=[VMEM] * 2,
         scratch_shapes=[pltpu.VMEM((TOK, 2 * HEAD), BF16)],
         compiler_params=params(),
         cost_estimate=cost(512, 1),
         name="attend_local",
-    )(c, queries, kv)
+    )(c, queries, keys, values)
     state = pl.pallas_call(
         chip_kernel,
         out_shape=state_shapes,
@@ -364,22 +385,22 @@
         cost_estimate=pl.CostEstimate(flops=1 << 31, bytes_accessed=5 << 20, transcendentals=1 << 18),
         name="merge_project",
     )(tp_s, m0, a0, got, out_weight)
+    rows = [[h * NX + x for x in range(NX)] for h in range(NH)]
+    swap = [(i, (i + NX) % (NX * NH)) for i in range(NX * NH)]
+    there = lax.all_to_all(there, "tp", 0, 0, axis_index_groups=rows)
     here = pl.pallas_call(
         project_kernel,
-        out_shape=parts_shape,
-        grid_spec=pltpu.PrefetchScalarGridSpec(
-            num_scalar_prefetch=1,
-            grid=(NX,),
-            in_specs=[whole(TOK, HEADS * HEAD), weights(True)],
-            out_specs=parts,
-        ),
-        compiler_params=params(56),
+        out_shape=[jax.ShapeDtypeStruct((TOK, wide_cols), BF16)] * NX,
+        in_specs=[SMEM] + [VMEM] * 2,
+        out_specs=[VMEM] * NX,
+        compiler_params=params(),
         cost_estimate=pl.CostEstimate(flops=1 << 31, bytes_accessed=2 << 20, transcendentals=0),
         name="project_own_half",
     )(tp_s, att, out_weight)
-    rows = [[h * NX + x for x in range(NX)] for h in range(NH)]
-    swap = [(i, (i + NX) % (NX * NH)) for i in range(NX * NH)]
-    there = lax.all_to_all(there, "tp", 0, 0, axis_index_groups=rows)
+    here = [here[0]] + [
+        lax.ppermute(here[k], "tp", [(i, i // NX * NX + (i + k) % NX) for i in range(NX * NH)])
+        for k in range(1, NX)
+    ]
     there = pl.pallas_call(
         sum_kernel,
         out_shape=jax.ShapeDtypeStruct((TOK, wide_cols), BF16),
@@ -388,27 +409,18 @@
         compiler_params=params(),
         name="sum_other_half",
     )(there)
-    crossed = pl.pallas_call(
-        widen_kernel,
-        out_shape=jax.ShapeDtypeStruct((TOK, wide_cols), F32),
-        in_specs=[VMEM],
-        out_specs=VMEM,
-        compiler_params=params(),
-        cost_estimate=pl.CostEstimate(flops=1 << 33, bytes_accessed=1 << 20, transcendentals=0),
-        name="widen_crossed",
-    )(lax.ppermute(there, "tp", swap))
-    here = lax.all_to_all(here, "tp", 0, 0, axis_index_groups=rows)
+    crossed = lax.ppermute(there, "tp", swap)
     projected, squares = pl.pallas_call(
         square_kernel,
         out_shape=[
             jax.ShapeDtypeStruct((TOK, wide_cols), F32),
             jax.ShapeDtypeStruct((NX * NH, 8, TOK), F32),
         ],
-        in_specs=[VMEM] * 2,
+        in_specs=[VMEM] * (NX + 1),
         out_specs=[VMEM] * 2,
         compiler_params=params(),
         name="sum_and_square",
-    )(here, crossed)
+    )(crossed, *here)
     squares = lax.all_to_all(squares, "tp", 0, 0)
     return pl.pallas_call(
         functools.partial(norm_kernel, out_weight.shape[1]),

time: 142 us -> 133 us (0.937)
  the two profiles are of different devices: /device:TPU:56 before, /device:TPU:64 now
where the time goes in v4:
time: 133 us; the launch traced here: 132 us
  starting transfers between devices  65.5 us (49%)
  Pallas kernels  23.7 us (18%)
  waiting for transfers between devices  19.5 us (15%)
  blocking collectives  17.3 us (13%)
  local copies, waits for them, and re-layouts  4.23 us (3%)
  between operations  1.69 us (1%)
    all_to_all x1, blocking collectives, shards(): squares = lax.all_to_all(squares, 'tp', 0, 0)  17.3 us
    all_to_all x1, starting transfers between devices, shards(): lax.all_to_all(jnp.broadcast_to(own, (NZ, SLOT, HEAD)), 'seq', 0, 0, axis...  12.6 us
    pallas_call x3, Pallas kernels, shards(): pl.pallas_call(functools.partial(ring_kernel, step), out_shape=state_shap...  12.2 us
    ppermute x3, starting transfers between devices, shards(): lax.ppermute(here[k], 'tp', [(i, i // NX * NX + (i + k) % NX) for i in ra...  11.9 us
    ppermute x2, starting transfers between devices, shards(): bwd.append(lax.ppermute(bwd[-1], 'seq', y_perm(-1)))  10.3 us
    ppermute x1, waiting for transfers between devices, shards(): crossed = lax.ppermute(there, 'tp', swap)  8.85 us
    ppermute x1, starting transfers between devices, shards(): crossed = lax.ppermute(there, 'tp', swap)  8.22 us
    ppermute x1, starting transfers between devices, shards(): bwd = [lax.ppermute(block, 'seq', y_perm(-1))]  5.13 us
  transfers between devices with their start and end apart: 17, of which 6 were waited for; matrix products, arithmetic and copies ran while one was open for 1% of the time, Pallas kernels for 13%

profile of v4, /device:TPU:64, one launch (start us, length us, event | category | flops | bytes accessed | tf_op | source)
XLA Modules:
  0.0 132.0 jit_solution(16667180044772286047)
XLA Ops:
  3.0 12.6 %all-to-all-start = ((bf16[4,256,128]{2,1,0:T(8,128)(2,1)}), bf16[4,256,128]{2,1,0:T(8,128)(2,1)S(1)}, u32[]{:S(2)}, u32[]{:S(2)}) async-start(bf16[4,256,128]{2,1,0:T(8,128)(2,1)} %broadcast_in_dim.3), calls=%async_computation | async-start | bytes 524288 | tf_op jit(solution)/shard_map/all_to_all | solution.py:270
  19.1 2.7 %all-to-all-done = bf16[4,256,128]{2,1,0:T(8,128)(2,1)S(1)} async-done(((bf16[4,256,128]{2,1,0:T(8,128)(2,1)}), bf16[4,256,128]{2,1,0:T(8,128)(2,1)S(1)}, u32[]{:S(2)}, u32[]{:S(2)}) %all-to-all-start) | async-done | bytes 262176 | tf_op jit(solution)/shard_map/all_to_all | solution.py:270
  21.8 1.9 %collective-permute-start.2 = (bf16[1024,128]{1,0:T(8,128)(2,1)S(1)}, bf16[1024,128]{1,0:T(8,128)(2,1)S(1)}, u32[]{:S(2)}, u32[]{:S(2)}) collective-permute-start(bf16[1024,128]{1,0:T(8,128)(2,1)S(1)} %pad_maximum_fusion.blk), channel_id=1, source_target_pairs={{0,16},{8,24},{16,32},{24,40},{32,48},{40,56},{48,64},{56,72},{64,... | collective-permute-start | bytes 786440 | tf_op jit(solution)/shard_map/ppermute | solution.py:293
  23.7 5.1 %collective-permute-start.5 = (bf16[1024,128]{1,0:T(8,128)(2,1)S(1)}, bf16[1024,128]{1,0:T(8,128)(2,1)S(1)}, u32[]{:S(2)}, u32[]{:S(2)}) collective-permute-start(bf16[1024,128]{1,0:T(8,128)(2,1)S(1)} %pad_maximum_fusion.blk), channel_id=1, source_target_pairs={{0,112},{8,120},{16,0},{24,8},{32,16},{40,24},{48,32},{56,40},{64,... | collective-permute-start | bytes 786440 | tf_op jit(solution)/shard_map/ppermute | solution.py:294
  29.6 2.4 %attend_own_chip.1 = (f32[4,256,128]{2,1,0:T(8,128)S(1)}, f32[4,256,256]{2,1,0:T(8,128)S(1)}, f32[4,256,128]{2,1,0:T(8,128)S(1)}, f32[4,256,256]{2,1,0:T(8,128)S(1)}) custom-call(s32[1]{0:T(128)} %bitcast.1.me_ref, f32[1]{0:T(128)S(6)} %mul.9.c_ref, bf16[256,512]{1,0:T(8,128)(2,1)S(1)} %copy-done.5, ...), custom_call_target="tpu_custom_call", output_to_operand_aliasing={{0}: (5, {}), {1}: (6, {})} | custom-call | flops 2684354560 | bytes 4194304 | tf_op jit(solution)/shard_map/attend_own_chip/pallas_call | solution.py:312
  32.0 1.9 %collective-permute-start.3 = (bf16[1024,128]{1,0:T(8,128)(2,1)S(1)}, bf16[1024,128]{1,0:T(8,128)(2,1)S(1)}, u32[]{:S(2)}, u32[]{:S(2)}) collective-permute-start(bf16[1024,128]{1,0:T(8,128)(2,1)S(1)} %collective-permute-done.2.fwd), channel_id=1, source_target_pairs={{0,16},{8,24},{16,32},{24,40},{32,48},{40,56},{48,64},{56,72},{64,... | collective-permute-start | bytes 786440 | tf_op jit(solution)/shard_map/ppermute | solution.py:296
  33.9 5.1 %collective-permute-start.6 = (bf16[1024,128]{1,0:T(8,128)(2,1)S(1)}, bf16[1024,128]{1,0:T(8,128)(2,1)S(1)}, u32[]{:S(2)}, u32[]{:S(2)}) collective-permute-start(bf16[1024,128]{1,0:T(8,128)(2,1)S(1)} %collective-permute-done.5.bwd), channel_id=1, source_target_pairs={{0,112},{8,120},{16,0},{24,8},{32,16},{40,24},{48,32},{56,40},{64,... | collective-permute-start | bytes 786440 | tf_op jit(solution)/shard_map/ppermute | solution.py:297
  39.1 4.1 %attend_ring.3 = (f32[4,256,128]{2,1,0:T(8,128)S(1)}, f32[4,256,256]{2,1,0:T(8,128)S(1)}, f32[4,256,128]{2,1,0:T(8,128)S(1)}, f32[4,256,256]{2,1,0:T(8,128)S(1)}) custom-call(s32[1]{0:T(128)} %bitcast.1.me_ref, f32[1]{0:T(128)S(6)} %mul.9.c_ref, ...), custom_call_target="tpu_custom_call", output_to_operand_aliasing={{0}: (6, {}), {1}: (7, {}), {2}: (8, {}), {3}: (9, {})} | custom-call | flops 5368709120 | bytes 4194304 | tf_op jit(solution)/shard_map/attend_ring/pallas_call | solution.py:324
  43.2 1.9 %collective-permute-start.4 = (bf16[1024,128]{1,0:T(8,128)(2,1)S(1)}, bf16[1024,128]{1,0:T(8,128)(2,1)S(1)}, u32[]{:S(2)}, u32[]{:S(2)}) collective-permute-start(bf16[1024,128]{1,0:T(8,128)(2,1)S(1)} %collective-permute-done.3.fwd), channel_id=1, source_target_pairs={{0,16},{8,24},{16,32},{24,40},{32,48},{40,56},{48,64},{56,72},{64,... | collective-permute-start | bytes 786440 | tf_op jit(solution)/shard_map/ppermute | solution.py:296
  45.1 5.1 %collective-permute-start.7 = (bf16[1024,128]{1,0:T(8,128)(2,1)S(1)}, bf16[1024,128]{1,0:T(8,128)(2,1)S(1)}, u32[]{:S(2)}, u32[]{:S(2)}) collective-permute-start(bf16[1024,128]{1,0:T(8,128)(2,1)S(1)} %collective-permute-done.6.bwd), channel_id=1, source_target_pairs={{0,112},{8,120},{16,0},{24,8},{32,16},{40,24},{48,32},{56,40},{64,... | collective-permute-start | bytes 786440 | tf_op jit(solution)/shard_map/ppermute | solution.py:297
  50.2 4.1 %attend_ring.4 = (f32[4,256,128]{2,1,0:T(8,128)S(1)}, f32[4,256,256]{2,1,0:T(8,128)S(1)}, f32[4,256,128]{2,1,0:T(8,128)S(1)}, f32[4,256,256]{2,1,0:T(8,128)S(1)}) custom-call(s32[1]{0:T(128)} %bitcast.1.me_ref, f32[1]{0:T(128)S(6)} %mul.9.c_ref, ...), custom_call_target="tpu_custom_call", output_to_operand_aliasing={{0}: (6, {}), {1}: (7, {}), {2}: (8, {}), {3}: (9, {})} | custom-call | flops 5368709120 | bytes 4194304 | tf_op jit(solution)/shard_map/attend_ring/pallas_call | solution.py:324
  54.4 2.1 %collective-permute-start.8 = (bf16[1024,128]{1,0:T(8,128)(2,1)S(1)}, bf16[1024,128]{1,0:T(8,128)(2,1)S(1)}, u32[]{:S(2)}, u32[]{:S(2)}) collective-permute-start(bf16[1024,128]{1,0:T(8,128)(2,1)S(1)} %broadcast_select_fusion), channel_id=1, source_target_pairs={{0,16},{8,120},{16,32},{24,8},{32,48},{40,24},{48,64},{56,40},{64,... | collective-permute-start | bytes 786440 | tf_op jit(solution)/shard_map/ppermute | solution.py:299
  56.5 4.1 %attend_ring.5 = (f32[4,256,128]{2,1,0:T(8,128)S(1)}, f32[4,256,256]{2,1,0:T(8,128)S(1)}, f32[4,256,128]{2,1,0:T(8,128)S(1)}, f32[4,256,256]{2,1,0:T(8,128)S(1)}) custom-call(s32[1]{0:T(128)} %bitcast.1.me_ref, f32[1]{0:T(128)S(6)} %mul.9.c_ref, ...), custom_call_target="tpu_custom_call", output_to_operand_aliasing={{0}: (6, {}), {1}: (7, {}), {2}: (8, {}), {3}: (9, {})} | custom-call | flops 5368709120 | bytes 4194304 | tf_op jit(solution)/shard_map/attend_ring/pallas_call | solution.py:324
  60.6 3.5 %collective-permute-done.8.blk = bf16[1024,128]{1,0:T(8,128)(2,1)S(1)} collective-permute-done((bf16[1024,128]{1,0:T(8,128)(2,1)S(1)}, bf16[1024,128]{1,0:T(8,128)(2,1)S(1)}, u32[]{:S(2)}, u32[]{:S(2)}) %collective-permute-start.8) | collective-permute-done | bytes 262176 | tf_op jit(solution)/shard_map/ppermute | solution.py:299
  69.8 3.1 %merge_project.1 = (bf16[256,512]{1,0:T(8,128)(2,1)S(1)}, bf16[4,256,512]{2,1,0:T(8,128)(2,1)}) custom-call(s32[1]{0:T(128)} %bitcast.tp_ref, f32[4,256,128]{2,1,0:T(8,128)S(1)} %get-tuple-element.50.m, f32[4,256,256]{2,1,0:T(8,128)S(1)} %get-tuple-element.51.a, bf16[4,256,256]{2,1,0:T(8,128)(2,1)S(1)} %collective-permute-done.10.got, ...), custom_call_target="tpu_custom_call" | custom-call | flops 2147483648 | bytes 5242880 | tf_op jit(solution)/shard_map/merge_project/pallas_call | solution.py:370
  72.9 4.3 %all-to-all-start.1 = ((bf16[4,256,512]{2,1,0:T(8,128)(2,1)}), bf16[4,256,512]{2,1,0:T(8,128)(2,1)S(1)}, u32[]{:S(2)}, u32[]{:S(2)}) async-start(bf16[4,256,512]{2,1,0:T(8,128)(2,1)} %get-tuple-element.55), calls=%async_computation.1 | async-start | bytes 2097152 | tf_op jit(solution)/shard_map/all_to_all | solution.py:390
  77.2 2.2 %copy-done.4 = bf16[512,4096]{1,0:T(8,128)(2,1)S(1)} copy-done((bf16[512,4096]{1,0:T(8,128)(2,1)S(1)}, bf16[512,4096]{1,0:T(8,128)(2,1)}, u32[]{:S(2)}) %copy-start.4) | copy-done | bytes 4194328
  80.1 3.9 %collective-permute-start.12 = (bf16[256,512]{1,0:T(8,128)(2,1)S(1)}, bf16[256,512]{1,0:T(8,128)(2,1)S(1)}, u32[]{:S(2)}, u32[]{:S(2)}) collective-permute-start(bf16[256,512]{1,0:T(8,128)(2,1)S(1)} %get-tuple-element.58), channel_id=1, source_target_pairs={{0,1},{1,2},{2,3},{3,0},{4,5},{5,6},{6,7},{7,4},{8,9},{9,10},{10,1... | collective-permute-start | bytes 786440 | tf_op jit(solution)/shard_map/ppermute | solution.py:401
  84.1 4.6 %collective-permute-start.13 = (bf16[256,512]{1,0:T(8,128)(2,1)S(1)}, bf16[256,512]{1,0:T(8,128)(2,1)S(1)}, u32[]{:S(2)}, u32[]{:S(2)}) collective-permute-start(bf16[256,512]{1,0:T(8,128)(2,1)S(1)} %get-tuple-element.59), channel_id=1, source_target_pairs={{0,2},{1,3},{2,0},{3,1},{4,6},{5,7},{6,4},{7,5},{8,10},{9,11},{10,... | collective-permute-start | bytes 786440 | tf_op jit(solution)/shard_map/ppermute | solution.py:401
  88.7 3.4 %collective-permute-start.14 = (bf16[256,512]{1,0:T(8,128)(2,1)S(1)}, bf16[256,512]{1,0:T(8,128)(2,1)S(1)}, u32[]{:S(2)}, u32[]{:S(2)}) collective-permute-start(bf16[256,512]{1,0:T(8,128)(2,1)S(1)} %get-tuple-element.60), channel_id=1, source_target_pairs={{0,3},{1,0},{2,1},{3,2},{4,7},{5,4},{6,5},{7,6},{8,11},{9,8},{10,9... | collective-permute-start | bytes 786440 | tf_op jit(solution)/shard_map/ppermute | solution.py:401
  93.9 8.2 %collective-permute-start.11 = (bf16[256,512]{1,0:T(8,128)(2,1)S(1)}, bf16[256,512]{1,0:T(8,128)(2,1)S(1)}, u32[]{:S(2)}, u32[]{:S(2)}) collective-permute-start(bf16[256,512]{1,0:T(8,128)(2,1)S(1)} %sum_other_half.1), channel_id=1, source_target_pairs={{0,4},{1,5},{2,6},{3,7},{4,0},{5,1},{6,2},{7,3},{8,12},{9,13},{10,... | collective-permute-start | bytes 786440 | tf_op jit(solution)/shard_map/ppermute | solution.py:412
  102.1 2.2 %collective-permute-done.13.refs_2_ = bf16[256,512]{1,0:T(8,128)(2,1)S(1)} collective-permute-done((bf16[256,512]{1,0:T(8,128)(2,1)S(1)}, bf16[256,512]{1,0:T(8,128)(2,1)S(1)}, u32[]{:S(2)}, u32[]{:S(2)}) %collective-permute-start.13) | collective-permute-done | bytes 262176 | tf_op jit(solution)/shard_map/ppermute | solution.py:401
  104.2 8.8 %collective-permute-done.11.crossed = bf16[256,512]{1,0:T(8,128)(2,1)S(1)} collective-permute-done((bf16[256,512]{1,0:T(8,128)(2,1)S(1)}, bf16[256,512]{1,0:T(8,128)(2,1)S(1)}, u32[]{:S(2)}, u32[]{:S(2)}) %collective-permute-start.11) | collective-permute-done | bytes 262176 | tf_op jit(solution)/shard_map/ppermute | solution.py:412
  113.7 17.3 %all_to_all.15.squares = f32[8,8,256]{2,1,0:T(8,128)S(1)} all-to-all(f32[8,8,256]{2,1,0:T(8,128)S(1)} %get-tuple-element.62), channel_id=1, replica_groups=mesh['seq'=64,'tp'=8] {'tp'}, dimensions={0} | all-to-all | bytes 131072 | tf_op jit(solution)/shard_map/all_to_all | solution.py:424
  (44 shorter events, 15.7 us)
Async XLA Ops:
  1.5 14.0 %collective-permute-start = (bf16[256,128]{1,0:T(8,128)(2,1)S(1)}, bf16[256,128]{1,0:T(8,128)(2,1)S(1)}, u32[]{:S(2)}, u32[]{:S(2)}) collective-permute-start(bf16[256,128]{1,0:T(8,128)(2,1)S(1)} %pad_maximum_fusion.2.here), channel_id=1, source_target_pairs={{0,504},{1,505},{2,506},{3,507},{4,508},{5,509},{6,510},{7,511}} | collective-permute-start | bytes 196616 | tf_op jit(solution)/shard_map/ppermute | solution.py:275
  3.0 18.8 %all-to-all-start = ((bf16[4,256,128]{2,1,0:T(8,128)(2,1)}), bf16[4,256,128]{2,1,0:T(8,128)(2,1)S(1)}, u32[]{:S(2)}, u32[]{:S(2)}) async-start(bf16[4,256,128]{2,1,0:T(8,128)(2,1)} %broadcast_in_dim.3), calls=%async_computation | async-start | bytes 524288 | tf_op jit(solution)/shard_map/all_to_all | solution.py:270
  15.5 1.0 copy-start.5
  15.5 13.4 %copy-start = (bf16[256,128]{1,0:T(8,128)(2,1)S(1)}, bf16[256,128]{1,0:T(8,128)(2,1)}, u32[]{:S(2)}) copy-start(bf16[256,128]{1,0:T(8,128)(2,1)} %k.1) | copy-start | bytes 196612
  15.5 13.4 %copy-start.1 = (bf16[256,128]{1,0:T(8,128)(2,1)S(1)}, bf16[256,128]{1,0:T(8,128)(2,1)}, u32[]{:S(2)}) copy-start(bf16[256,128]{1,0:T(8,128)(2,1)} %v.1) | copy-start | bytes 196612
  15.6 3.5 %collective-permute-start.1 = (bf16[256,128]{1,0:T(8,128)(2,1)S(1)}, bf16[256,128]{1,0:T(8,128)(2,1)S(1)}, u32[]{:S(2)}, u32[]{:S(2)}) collective-permute-start(bf16[256,128]{1,0:T(8,128)(2,1)S(1)} %choose_anchor.1), channel_id=1, source_target_pairs={{0,248},{504,376},{1,249},{505,377},{2,250},{506,378},{3,251},{507... | collective-permute-start | bytes 196616 | tf_op jit(solution)/shard_map/ppermute | solution.py:285
  16.5 13.1 %collective-permute-start.9 = (bf16[256,512]{1,0:T(8,128)(2,1)S(1)}, bf16[256,512]{1,0:T(8,128)(2,1)S(1)}, u32[]{:S(2)}, u32[]{:S(2)}) collective-permute-start(bf16[256,512]{1,0:T(8,128)(2,1)S(1)} %copy-done.5), channel_id=1, source_target_pairs={{0,8},{8,0},{16,24},{24,16},{32,40},{40,32},{48,56},{56,48},{64,72... | collective-permute-start | bytes 786440 | tf_op jit(solution)/shard_map/ppermute | solution.py:286
  21.8 10.2 %collective-permute-start.2 = (bf16[1024,128]{1,0:T(8,128)(2,1)S(1)}, bf16[1024,128]{1,0:T(8,128)(2,1)S(1)}, u32[]{:S(2)}, u32[]{:S(2)}) collective-permute-start(bf16[1024,128]{1,0:T(8,128)(2,1)S(1)} %pad_maximum_fusion.blk), channel_id=1, source_target_pairs={{0,16},{8,24},{16,32},{24,40},{32,48},{40,56},{48,64},{56,72},{64,... | collective-permute-start | bytes 786440 | tf_op jit(solution)/shard_map/ppermute | solution.py:293
  23.7 10.2 %collective-permute-start.5 = (bf16[1024,128]{1,0:T(8,128)(2,1)S(1)}, bf16[1024,128]{1,0:T(8,128)(2,1)S(1)}, u32[]{:S(2)}, u32[]{:S(2)}) collective-permute-start(bf16[1024,128]{1,0:T(8,128)(2,1)S(1)} %pad_maximum_fusion.blk), channel_id=1, source_target_pairs={{0,112},{8,120},{16,0},{24,8},{32,16},{40,24},{48,32},{56,40},{64,... | collective-permute-start | bytes 786440 | tf_op jit(solution)/shard_map/ppermute | solution.py:294
  32.0 11.2 %collective-permute-start.3 = (bf16[1024,128]{1,0:T(8,128)(2,1)S(1)}, bf16[1024,128]{1,0:T(8,128)(2,1)S(1)}, u32[]{:S(2)}, u32[]{:S(2)}) collective-permute-start(bf16[1024,128]{1,0:T(8,128)(2,1)S(1)} %collective-permute-done.2.fwd), channel_id=1, source_target_pairs={{0,16},{8,24},{16,32},{24,40},{32,48},{40,56},{48,64},{56,72},{64,... | collective-permute-start | bytes 786440 | tf_op jit(solution)/shard_map/ppermute | solution.py:296
  33.9 11.2 %collective-permute-start.6 = (bf16[1024,128]{1,0:T(8,128)(2,1)S(1)}, bf16[1024,128]{1,0:T(8,128)(2,1)S(1)}, u32[]{:S(2)}, u32[]{:S(2)}) collective-permute-start(bf16[1024,128]{1,0:T(8,128)(2,1)S(1)} %collective-permute-done.5.bwd), channel_id=1, source_target_pairs={{0,112},{8,120},{16,0},{24,8},{32,16},{40,24},{48,32},{56,40},{64,... | collective-permute-start | bytes 786440 | tf_op jit(solution)/shard_map/ppermute | solution.py:297
  43.2 11.2 %collective-permute-start.4 = (bf16[1024,128]{1,0:T(8,128)(2,1)S(1)}, bf16[1024,128]{1,0:T(8,128)(2,1)S(1)}, u32[]{:S(2)}, u32[]{:S(2)}) collective-permute-start(bf16[1024,128]{1,0:T(8,128)(2,1)S(1)} %collective-permute-done.3.fwd), channel_id=1, source_target_pairs={{0,16},{8,24},{16,32},{24,40},{32,48},{40,56},{48,64},{56,72},{64,... | collective-permute-start | bytes 786440 | tf_op jit(solution)/shard_map/ppermute | solution.py:296
  45.1 9.2 %collective-permute-start.7 = (bf16[1024,128]{1,0:T(8,128)(2,1)S(1)}, bf16[1024,128]{1,0:T(8,128)(2,1)S(1)}, u32[]{:S(2)}, u32[]{:S(2)}) collective-permute-start(bf16[1024,128]{1,0:T(8,128)(2,1)S(1)} %collective-permute-done.6.bwd), channel_id=1, source_target_pairs={{0,112},{8,120},{16,0},{24,8},{32,16},{40,24},{48,32},{56,40},{64,... | collective-permute-start | bytes 786440 | tf_op jit(solution)/shard_map/ppermute | solution.py:297
  54.4 9.7 %collective-permute-start.8 = (bf16[1024,128]{1,0:T(8,128)(2,1)S(1)}, bf16[1024,128]{1,0:T(8,128)(2,1)S(1)}, u32[]{:S(2)}, u32[]{:S(2)}) collective-permute-start(bf16[1024,128]{1,0:T(8,128)(2,1)S(1)} %broadcast_select_fusion), channel_id=1, source_target_pairs={{0,16},{8,120},{16,32},{24,8},{32,48},{40,24},{48,64},{56,40},{64,... | collective-permute-start | bytes 786440 | tf_op jit(solution)/shard_map/ppermute | solution.py:299
  65.7 3.8 %collective-permute-start.10 = (bf16[4,256,256]{2,1,0:T(8,128)(2,1)S(1)}, bf16[4,256,256]{2,1,0:T(8,128)(2,1)S(1)}, u32[]{:S(2)}, u32[]{:S(2)}) collective-permute-start(bf16[4,256,256]{2,1,0:T(8,128)(2,1)S(1)} %get-tuple-element.54), channel_id=1, source_target_pairs={{0,8},{8,0},{16,24},{24,16},{32,40},{40,32},{48,56},{56,48},{64,72... | collective-permute-start | bytes 1572872 | tf_op jit(solution)/shard_map/ppermute | solution.py:347
  67.6 2.2 %copy-start.3 = (bf16[512,4096]{1,0:T(8,128)(2,1)S(1)}, bf16[512,4096]{1,0:T(8,128)(2,1)}, u32[]{:S(2)}) copy-start(bf16[512,4096]{1,0:T(8,128)(2,1)} %w.3) | copy-start | bytes 12582916
  72.9 20.8 %all-to-all-start.1 = ((bf16[4,256,512]{2,1,0:T(8,128)(2,1)}), bf16[4,256,512]{2,1,0:T(8,128)(2,1)S(1)}, u32[]{:S(2)}, u32[]{:S(2)}) async-start(bf16[4,256,512]{2,1,0:T(8,128)(2,1)} %get-tuple-element.55), calls=%async_computation.1 | async-start | bytes 2097152 | tf_op jit(solution)/shard_map/all_to_all | solution.py:390
  77.2 2.2 %copy-start.4 = (bf16[512,4096]{1,0:T(8,128)(2,1)S(1)}, bf16[512,4096]{1,0:T(8,128)(2,1)}, u32[]{:S(2)}) copy-start(bf16[512,4096]{1,0:T(8,128)(2,1)} %w.3) | copy-start | bytes 12582916
  79.4 51.6 %copy-start.2 = (f32[512]{0:T(512)S(1)}, f32[512]{0:T(512)}, u32[]{:S(2)}) copy-start(f32[512]{0:T(512)} %param.13) | copy-start | bytes 6148
  80.1 22.0 %collective-permute-start.12 = (bf16[256,512]{1,0:T(8,128)(2,1)S(1)}, bf16[256,512]{1,0:T(8,128)(2,1)S(1)}, u32[]{:S(2)}, u32[]{:S(2)}) collective-permute-start(bf16[256,512]{1,0:T(8,128)(2,1)S(1)} %get-tuple-element.58), channel_id=1, source_target_pairs={{0,1},{1,2},{2,3},{3,0},{4,5},{5,6},{6,7},{7,4},{8,9},{9,10},{10,1... | collective-permute-start | bytes 786440 | tf_op jit(solution)/shard_map/ppermute | solution.py:401
  84.1 20.2 %collective-permute-start.13 = (bf16[256,512]{1,0:T(8,128)(2,1)S(1)}, bf16[256,512]{1,0:T(8,128)(2,1)S(1)}, u32[]{:S(2)}, u32[]{:S(2)}) collective-permute-start(bf16[256,512]{1,0:T(8,128)(2,1)S(1)} %get-tuple-element.59), channel_id=1, source_target_pairs={{0,2},{1,3},{2,0},{3,1},{4,6},{5,7},{6,4},{7,5},{8,10},{9,11},{10,... | collective-permute-start | bytes 786440 | tf_op jit(solution)/shard_map/ppermute | solution.py:401
  88.7 15.6 %collective-permute-start.14 = (bf16[256,512]{1,0:T(8,128)(2,1)S(1)}, bf16[256,512]{1,0:T(8,128)(2,1)S(1)}, u32[]{:S(2)}, u32[]{:S(2)}) collective-permute-start(bf16[256,512]{1,0:T(8,128)(2,1)S(1)} %get-tuple-element.60), channel_id=1, source_target_pairs={{0,3},{1,0},{2,1},{3,2},{4,7},{5,4},{6,5},{7,6},{8,11},{9,8},{10,9... | collective-permute-start | bytes 786440 | tf_op jit(solution)/shard_map/ppermute | solution.py:401
  93.9 19.2 %collective-permute-start.11 = (bf16[256,512]{1,0:T(8,128)(2,1)S(1)}, bf16[256,512]{1,0:T(8,128)(2,1)S(1)}, u32[]{:S(2)}, u32[]{:S(2)}) collective-permute-start(bf16[256,512]{1,0:T(8,128)(2,1)S(1)} %sum_other_half.1), channel_id=1, source_target_pairs={{0,4},{1,5},{2,6},{3,7},{4,0},{5,1},{6,2},{7,3},{8,12},{9,13},{10,... | collective-permute-start | bytes 786440 | tf_op jit(solution)/shard_map/ppermute | solution.py:412

commit v5 on v4

--- a/solution.py
+++ b/solution.py
@@ -76,17 +76,17 @@
         vv[pl.ds(j * BLOCK, BLOCK), HEAD : 2 * HEAD] = jnp.full((BLOCK, HEAD), scale, F32).astype(BF16)
 
 
-def update(c, q, kk, vv, m_ref, acc_ref, h):
+def update(c, q, kk, vv, old, new, h):
     s = cross(q, kk[...]) * c
-    m_old = m_ref[h]
+    m_old = old[0][h]
     m_new = jnp.maximum(m_old, jnp.max(s, axis=1, keepdims=True))
     alpha = jnp.exp2(m_old - m_new)
     p = jnp.exp2(s - wide(m_new, s.shape[1] // HEAD)).astype(BF16)
-    acc_ref[h] = acc_ref[h] * wide(alpha, 2) + plain(p, vv[...])
-    m_ref[h] = m_new
-
-
-def attend_set(me, core, key_ys, c, q_ref, blocks, kk, vv, m_ref, acc_ref):
+    new[1][h] = old[1][h] * wide(alpha, 2) + plain(p, vv[...])
+    new[0][h] = m_new
+
+
+def attend_set(me, core, key_ys, c, q_ref, blocks, kk, vv, old, new):
     shown = []
     for key_y in key_ys:
         shown += seen(me, core, key_y)
@@ -96,7 +96,14 @@
     def _():
         prepare(blocks, shown, kk, vv)
         for h in range(HEADS):
-            update(c, q_ref[:, h * HEAD : (h + 1) * HEAD], kk, vv, m_ref, acc_ref, h)
+            update(c, q_ref[:, h * HEAD : (h + 1) * HEAD], kk, vv, old, new, h)
+
+    if old is not new:
+
+        @pl.when(total == 0)
+        def _():
+            for source, target in zip(old, new):
+                target[...] = source[...]
 
 
 def local_kernel(c_ref, q, k, v, m, a, lv):
@@ -119,12 +126,11 @@
     c = c_ref[0]
     core = me % NC
     y = (me // NC) % NY
-    m0[...] = m0i[...]
-    a0[...] = a0i[...]
     m1[...] = jnp.full(m1.shape, LOW, F32)
     a1[...] = jnp.zeros(a1.shape, F32)
-    attend_set(me, core, [y], c, q0, blk, kk, vv, m0, a0)
-    attend_set(me, 1 - core, [y], c, q1, blk, kk, vv, m1, a1)
+    attend_set(me, core, [y], c, q0, blk, kk, vv, (m0i, a0i), (m0, a0))
+    start = (m1, a1)
+    attend_set(me, 1 - core, [y], c, q1, blk, kk, vv, start, start)
 
 
 def ring_kernel(step, me_ref, c_ref, q0, q1, fwd, bwd, m0i, a0i, m1i, a1i, m0, a0, m1, a1, blocks, kk, vv):
@@ -132,15 +138,11 @@
     c = c_ref[0]
     core = me % NC
     y = (me // NC) % NY
-    m0[...] = m0i[...]
-    a0[...] = a0i[...]
-    m1[...] = m1i[...]
-    a1[...] = a1i[...]
     blocks[0:MSG, :] = fwd[...]
     blocks[MSG : 2 * MSG, :] = bwd[...]
     key_ys = [(y + NY - step) % NY, (y + step) % NY]
-    attend_set(me, core, key_ys, c, q0, blocks, kk, vv, m0, a0)
-    attend_set(me, 1 - core, key_ys, c, q1, blocks, kk, vv, m1, a1)
+    attend_set(me, core, key_ys, c, q0, blocks, kk, vv, (m0i, a0i), (m0, a0))
+    attend_set(me, 1 - core, key_ys, c, q1, blocks, kk, vv, (m1i, a1i), (m1, a1))
 
 
 def last_kernel(other, me_ref, c_ref, q, blk, mi, ai, *rest):
@@ -151,10 +153,8 @@
     me = me_ref[0]
     core = me % NC
     y = (me // NC) % NY
-    m[...] = mi[...]
-    a[...] = ai[...]
     key_ys = [(y + NY // 2) % NY]
-    attend_set(me, 1 - core if other else core, key_ys, c_ref[0], q, blk, kk, vv, m, a)
+    attend_set(me, 1 - core if other else core, key_ys, c_ref[0], q, blk, kk, vv, (mi, ai), (m, a))
     if other:
         lane = lax.broadcasted_iota(jnp.int32, (TOK, HEAD), 1)
         for h in range(HEADS):
@@ -170,35 +170,44 @@
             out[h, :, HEAD : 2 * HEAD] = parts.astype(BF16)
 
 
-def merge_kernel(tp_ref, m, a, got, w, att, out):
-    @pl.when(pl.program_id(0) == 0)
-    def _():
-        for h in range(HEADS):
-            parts = got[h][:, HEAD:].astype(F32)
-            lse = (parts[:, 0:1] + parts[:, 1:2]) + parts[:, 2:3]
-            mine = m[h]
-            top = jnp.maximum(mine, lse)
-            w0 = jnp.exp2(mine - top)
-            w1 = jnp.exp2(lse - top)
-            acc = a[h][:, :HEAD] * w0 + got[h][:, :HEAD].astype(F32) * w1
-            total = a[h][:, HEAD:] * w0 + w1
-            att[:, h * HEAD : (h + 1) * HEAD] = (acc / total).astype(BF16)
-
-    out[0] = plain(att[...], w[...]).astype(BF16)
-
-
-def project_kernel(tp_ref, att, w, *outs):
+def merge_kernel(tp_ref, m, a, got, w, there, *rest):
+    *here, att = rest
+    for h in range(HEADS):
+        parts = got[h][:, HEAD:].astype(F32)
+        lse = (parts[:, 0:1] + parts[:, 1:2]) + parts[:, 2:3]
+        mine = m[h]
+        top = jnp.maximum(mine, lse)
+        w0 = jnp.exp2(mine - top)
+        w1 = jnp.exp2(lse - top)
+        acc = a[h][:, :HEAD] * w0 + got[h][:, :HEAD].astype(F32) * w1
+        total = a[h][:, HEAD:] * w0 + w1
+        att[:, h * HEAD : (h + 1) * HEAD] = (acc / total).astype(BF16)
     x, half = tp_ref[0] % NX, tp_ref[0] // NX
-    for k, out in enumerate(outs):
-        col = pl.multiple_of((half * NX + (x + k) % NX) * out.shape[1], out.shape[1])
-        out[...] = plain(att[...], w[:, pl.ds(col, out.shape[1])]).astype(BF16)
-
-
-def sum_kernel(parts, out):
+    cols = there.shape[2]
+
+    def project(half, j):
+        return plain(att[...], w[:, pl.ds(pl.multiple_of((half * NX + j) * cols, cols), cols)]).astype(BF16)
+
+    for j in range(NX):
+        there[j] = project(1 - half, j)
+    for k in range(NX):
+        here[k][...] = project(half, (x + k) % NX)
+
+
+def sum_kernel(parts, part, out, same):
     total = parts[0].astype(F32)
     for j in range(1, NX):
         total += parts[j].astype(F32)
-    out[...] = total.astype(out.dtype)
+    out[...] = total.astype(BF16)
+    same[...] = part[...]
+
+
+def add_kernel(*refs):
+    *parts, out = refs
+    total = parts[0][...].astype(F32)
+    for part in parts[1:]:
+        total += part[...].astype(F32)
+    out[...] = total
 
 
 def choose_kernel(me_ref, here, there, out):
@@ -213,11 +222,8 @@
         out[...] = here[...]
 
 
-def square_kernel(crossed, *refs):
-    *parts, out, squares = refs
-    total = crossed[...].astype(F32)
-    for part in parts:
-        total += part[...].astype(F32)
+def square_kernel(part, last, out, squares):
+    total = part[...] + last[...].astype(F32)
     out[...] = total
     ones = jnp.ones((8, total.shape[1]), F32)
     sums = lax.dot_general(
@@ -359,68 +365,59 @@
 
     wide_cols = out_weight.shape[1] // (NX * NH)
 
-    def columns(own_half, j, tp_ref):
-        half = tp_ref[0] // NX
-        return (0, (half if own_half else 1 - half) * NX + j)
-
-    whole = lambda *shape: pl.BlockSpec(shape, lambda j, tp_ref: (0,) * len(shape))
-    weights = lambda own_half: pl.BlockSpec((HEADS * HEAD, wide_cols), functools.partial(columns, own_half))
-    parts = pl.BlockSpec((1, TOK, wide_cols), lambda j, tp_ref: (j, 0, 0))
-    parts_shape = jax.ShapeDtypeStruct((NX, TOK, wide_cols), BF16)
-    att, there = pl.pallas_call(
+    block_shape = jax.ShapeDtypeStruct((TOK, wide_cols), BF16)
+    there, *here = pl.pallas_call(
         merge_kernel,
-        out_shape=[jax.ShapeDtypeStruct((TOK, HEADS * HEAD), BF16), parts_shape],
-        grid_spec=pltpu.PrefetchScalarGridSpec(
-            num_scalar_prefetch=1,
-            grid=(NX,),
-            in_specs=[
-                whole(HEADS, TOK, HEAD),
-                whole(HEADS, TOK, 2 * HEAD),
-                whole(HEADS, TOK, 2 * HEAD),
-                weights(False),
-            ],
-            out_specs=[whole(TOK, HEADS * HEAD), parts],
-        ),
-        compiler_params=params(),
-        cost_estimate=pl.CostEstimate(flops=1 << 31, bytes_accessed=5 << 20, transcendentals=1 << 18),
+        out_shape=[jax.ShapeDtypeStruct((NX, TOK, wide_cols), BF16)] + [block_shape] * NX,
+        in_specs=[SMEM] + [VMEM] * 4,
+        out_specs=[VMEM] * (NX + 1),
+        scratch_shapes=[pltpu.VMEM((TOK, HEADS * HEAD), BF16)],
+        compiler_params=params(),
+        cost_estimate=pl.CostEstimate(flops=1 << 32, bytes_accessed=8 << 20, transcendentals=1 << 18),
         name="merge_project",
     )(tp_s, m0, a0, got, out_weight)
     rows = [[h * NX + x for x in range(NX)] for h in range(NH)]
     swap = [(i, (i + NX) % (NX * NH)) for i in range(NX * NH)]
+
+    def turn_x(part, k):
+        return lax.ppermute(part, "tp", [(i, i // NX * NX + (i + k) % NX) for i in range(NX * NH)])
+
     there = lax.all_to_all(there, "tp", 0, 0, axis_index_groups=rows)
-    here = pl.pallas_call(
-        project_kernel,
-        out_shape=[jax.ShapeDtypeStruct((TOK, wide_cols), BF16)] * NX,
-        in_specs=[SMEM] + [VMEM] * 2,
-        out_specs=[VMEM] * NX,
-        compiler_params=params(),
-        cost_estimate=pl.CostEstimate(flops=1 << 31, bytes_accessed=2 << 20, transcendentals=0),
-        name="project_own_half",
-    )(tp_s, att, out_weight)
-    here = [here[0]] + [
-        lax.ppermute(here[k], "tp", [(i, i // NX * NX + (i + k) % NX) for i in range(NX * NH)])
-        for k in range(1, NX)
-    ]
-    there = pl.pallas_call(
+    second, first = turn_x(here[2], 2), turn_x(here[1], 1)
+    there, third = pl.pallas_call(
         sum_kernel,
-        out_shape=jax.ShapeDtypeStruct((TOK, wide_cols), BF16),
-        in_specs=[VMEM],
-        out_specs=VMEM,
+        out_shape=[block_shape] * 2,
+        in_specs=[VMEM] * 2,
+        out_specs=[VMEM] * 2,
         compiler_params=params(),
         name="sum_other_half",
-    )(there)
-    crossed = lax.ppermute(there, "tp", swap)
+    )(there, here[3])
+
+    def add(flops, *parts):
+        return pl.pallas_call(
+            add_kernel,
+            out_shape=jax.ShapeDtypeStruct((TOK, wide_cols), F32),
+            in_specs=[VMEM] * len(parts),
+            out_specs=VMEM,
+            compiler_params=params(),
+            cost_estimate=pl.CostEstimate(flops=flops, bytes_accessed=1 << 20, transcendentals=0),
+            name="add_parts",
+        )(*parts)
+
+    third = turn_x(third, 3)
+    part = add(1 << 31, here[0], first, second)
+    part = add(1 << 30, part, lax.ppermute(there, "tp", swap))
     projected, squares = pl.pallas_call(
         square_kernel,
         out_shape=[
             jax.ShapeDtypeStruct((TOK, wide_cols), F32),
             jax.ShapeDtypeStruct((NX * NH, 8, TOK), F32),
         ],
-        in_specs=[VMEM] * (NX + 1),
+        in_specs=[VMEM] * 2,
         out_specs=[VMEM] * 2,
         compiler_params=params(),
         name="sum_and_square",
-    )(crossed, *here)
+    )(part, third)
     squares = lax.all_to_all(squares, "tp", 0, 0)
     return pl.pallas_call(
         functools.partial(norm_kernel, out_weight.shape[1]),

time: 133 us -> 134 us (level)
  waiting for transfers between devices: 19.5 us -> 21.2 us
    all_to_all x1, waiting for transfers between devices: 1.68 us -> 8 us  [shards(): there = lax.all_to_all(there, 'tp', 0, 0, axis_index_groups=rows)]
    ppermute x4, waiting for transfers between devices: 11 us -> 6.91 us  [the longest x1 6.9 us: shards(): part = add(1 << 30, part, lax.ppermute(there, 'tp', swap))]
    pallas_call x3 -> x4, Pallas kernels: 3.98 us -> 2.78 us  [the longest x1 2.5 us: shards(): pl.pallas_call(merge_kernel, out_shape=[jax.ShapeDtypeStruct((NX, TOK, wi...]
  transfers between devices with their start and end apart: 17 -> 17, of which waited for: 6 -> 5; matrix products, arithmetic and copies ran while one was open for 1% -> 1% of each run, Pallas kernels for 13% -> 14%
where the time goes in v5:
time: 134 us; the launch traced here: 133 us
  starting transfers between devices  65 us (49%)
  Pallas kernels  23.8 us (18%)
  waiting for transfers between devices  21.2 us (16%)
  blocking collectives  17.3 us (13%)
  local copies, waits for them, and re-layouts  3.69 us (3%)
  between operations  1.72 us (1%)
    all_to_all x1, blocking collectives, shards(): squares = lax.all_to_all(squares, 'tp', 0, 0)  17.3 us
    pallas_call x3, Pallas kernels, shards(): pl.pallas_call(functools.partial(ring_kernel, step), out_shape=state_shap...  13.4 us
    all_to_all x1, starting transfers between devices, shards(): lax.all_to_all(jnp.broadcast_to(own, (NZ, SLOT, HEAD)), 'seq', 0, 0, axis...  12.6 us
    ppermute x3, starting transfers between devices, turn_x(): lax.ppermute(part, 'tp', [(i, i // NX * NX + (i + k) % NX) for i in range...  11.5 us
    ppermute x2, starting transfers between devices, shards(): bwd.append(lax.ppermute(bwd[-1], 'seq', y_perm(-1)))  10.3 us
    ppermute x1, starting transfers between devices, shards(): part = add(1 << 30, part, lax.ppermute(there, 'tp', swap))  8.23 us
    all_to_all x1, waiting for transfers between devices, shards(): there = lax.all_to_all(there, 'tp', 0, 0, axis_index_groups=rows)  8 us
    ppermute x1, waiting for transfers between devices, shards(): part = add(1 << 30, part, lax.ppermute(there, 'tp', swap))  6.9 us
  transfers between devices with their start and end apart: 17, of which 5 were waited for; matrix products, arithmetic and copies ran while one was open for 1% of the time, Pallas kernels for 14%

profile of v5, /device:TPU:64, one launch (start us, length us, event | category | flops | bytes accessed | tf_op | source)
XLA Modules:
  0.0 132.9 jit_solution(3498915022287390041)
XLA Ops:
  3.0 12.6 %all-to-all-start = ((bf16[4,256,128]{2,1,0:T(8,128)(2,1)}), bf16[4,256,128]{2,1,0:T(8,128)(2,1)S(1)}, u32[]{:S(2)}, u32[]{:S(2)}) async-start(bf16[4,256,128]{2,1,0:T(8,128)(2,1)} %broadcast_in_dim.3), calls=%async_computation | async-start | bytes 524288 | tf_op jit(solution)/shard_map/all_to_all | solution.py:276
  19.1 2.7 %all-to-all-done = bf16[4,256,128]{2,1,0:T(8,128)(2,1)S(1)} async-done(((bf16[4,256,128]{2,1,0:T(8,128)(2,1)}), bf16[4,256,128]{2,1,0:T(8,128)(2,1)S(1)}, u32[]{:S(2)}, u32[]{:S(2)}) %all-to-all-start) | async-done | bytes 262176 | tf_op jit(solution)/shard_map/all_to_all | solution.py:276
  21.8 1.9 %collective-permute-start.2 = (bf16[1024,128]{1,0:T(8,128)(2,1)S(1)}, bf16[1024,128]{1,0:T(8,128)(2,1)S(1)}, u32[]{:S(2)}, u32[]{:S(2)}) collective-permute-start(bf16[1024,128]{1,0:T(8,128)(2,1)S(1)} %pad_maximum_fusion.blk), channel_id=1, source_target_pairs={{0,16},{8,24},{16,32},{24,40},{32,48},{40,56},{48,64},{56,72},{64,... | collective-permute-start | bytes 786440 | tf_op jit(solution)/shard_map/ppermute | solution.py:299
  23.8 5.1 %collective-permute-start.5 = (bf16[1024,128]{1,0:T(8,128)(2,1)S(1)}, bf16[1024,128]{1,0:T(8,128)(2,1)S(1)}, u32[]{:S(2)}, u32[]{:S(2)}) collective-permute-start(bf16[1024,128]{1,0:T(8,128)(2,1)S(1)} %pad_maximum_fusion.blk), channel_id=1, source_target_pairs={{0,112},{8,120},{16,0},{24,8},{32,16},{40,24},{48,32},{56,40},{64,... | collective-permute-start | bytes 786440 | tf_op jit(solution)/shard_map/ppermute | solution.py:300
  29.6 2.5 %attend_own_chip.1 = (f32[4,256,128]{2,1,0:T(8,128)S(1)}, f32[4,256,256]{2,1,0:T(8,128)S(1)}, f32[4,256,128]{2,1,0:T(8,128)S(1)}, f32[4,256,256]{2,1,0:T(8,128)S(1)}) custom-call(s32[1]{0:T(128)} %bitcast.1.me_ref, f32[1]{0:T(128)S(6)} %mul.9.c_ref, bf16[256,512]{1,0:T(8,128)(2,1)S(1)} %copy-done.4, ...), custom_call_target="tpu_custom_call", output_to_operand_aliasing={{0}: (5, {}), {1}: (6, {})} | custom-call | flops 2684354560 | bytes 4194304 | tf_op jit(solution)/shard_map/attend_own_chip/pallas_call | solution.py:318
  32.1 1.9 %collective-permute-start.3 = (bf16[1024,128]{1,0:T(8,128)(2,1)S(1)}, bf16[1024,128]{1,0:T(8,128)(2,1)S(1)}, u32[]{:S(2)}, u32[]{:S(2)}) collective-permute-start(bf16[1024,128]{1,0:T(8,128)(2,1)S(1)} %collective-permute-done.2.fwd), channel_id=1, source_target_pairs={{0,16},{8,24},{16,32},{24,40},{32,48},{40,56},{48,64},{56,72},{64,... | collective-permute-start | bytes 786440 | tf_op jit(solution)/shard_map/ppermute | solution.py:302
  34.1 5.1 %collective-permute-start.6 = (bf16[1024,128]{1,0:T(8,128)(2,1)S(1)}, bf16[1024,128]{1,0:T(8,128)(2,1)S(1)}, u32[]{:S(2)}, u32[]{:S(2)}) collective-permute-start(bf16[1024,128]{1,0:T(8,128)(2,1)S(1)} %collective-permute-done.5.bwd), channel_id=1, source_target_pairs={{0,112},{8,120},{16,0},{24,8},{32,16},{40,24},{48,32},{56,40},{64,... | collective-permute-start | bytes 786440 | tf_op jit(solution)/shard_map/ppermute | solution.py:303
  39.2 4.4 %attend_ring.3 = (f32[4,256,128]{2,1,0:T(8,128)S(1)}, f32[4,256,256]{2,1,0:T(8,128)S(1)}, f32[4,256,128]{2,1,0:T(8,128)S(1)}, f32[4,256,256]{2,1,0:T(8,128)S(1)}) custom-call(s32[1]{0:T(128)} %bitcast.1.me_ref, f32[1]{0:T(128)S(6)} %mul.9.c_ref, ...), custom_call_target="tpu_custom_call", output_to_operand_aliasing={{0}: (6, {}), {1}: (7, {}), {2}: (8, {}), {3}: (9, {})} | custom-call | flops 5368709120 | bytes 4194304 | tf_op jit(solution)/shard_map/attend_ring/pallas_call | solution.py:330
  43.6 1.9 %collective-permute-start.4 = (bf16[1024,128]{1,0:T(8,128)(2,1)S(1)}, bf16[1024,128]{1,0:T(8,128)(2,1)S(1)}, u32[]{:S(2)}, u32[]{:S(2)}) collective-permute-start(bf16[1024,128]{1,0:T(8,128)(2,1)S(1)} %collective-permute-done.3.fwd), channel_id=1, source_target_pairs={{0,16},{8,24},{16,32},{24,40},{32,48},{40,56},{48,64},{56,72},{64,... | collective-permute-start | bytes 786440 | tf_op jit(solution)/shard_map/ppermute | solution.py:302
  45.6 5.1 %collective-permute-start.7 = (bf16[1024,128]{1,0:T(8,128)(2,1)S(1)}, bf16[1024,128]{1,0:T(8,128)(2,1)S(1)}, u32[]{:S(2)}, u32[]{:S(2)}) collective-permute-start(bf16[1024,128]{1,0:T(8,128)(2,1)S(1)} %collective-permute-done.6.bwd), channel_id=1, source_target_pairs={{0,112},{8,120},{16,0},{24,8},{32,16},{40,24},{48,32},{56,40},{64,... | collective-permute-start | bytes 786440 | tf_op jit(solution)/shard_map/ppermute | solution.py:303
  50.7 4.6 %attend_ring.4 = (f32[4,256,128]{2,1,0:T(8,128)S(1)}, f32[4,256,256]{2,1,0:T(8,128)S(1)}, f32[4,256,128]{2,1,0:T(8,128)S(1)}, f32[4,256,256]{2,1,0:T(8,128)S(1)}) custom-call(s32[1]{0:T(128)} %bitcast.1.me_ref, f32[1]{0:T(128)S(6)} %mul.9.c_ref, ...), custom_call_target="tpu_custom_call", output_to_operand_aliasing={{0}: (6, {}), {1}: (7, {}), {2}: (8, {}), {3}: (9, {})} | custom-call | flops 5368709120 | bytes 4194304 | tf_op jit(solution)/shard_map/attend_ring/pallas_call | solution.py:330
  55.4 1.9 %collective-permute-start.8 = (bf16[1024,128]{1,0:T(8,128)(2,1)S(1)}, bf16[1024,128]{1,0:T(8,128)(2,1)S(1)}, u32[]{:S(2)}, u32[]{:S(2)}) collective-permute-start(bf16[1024,128]{1,0:T(8,128)(2,1)S(1)} %broadcast_select_fusion), channel_id=1, source_target_pairs={{0,16},{8,120},{16,32},{24,8},{32,48},{40,24},{48,64},{56,40},{64,... | collective-permute-start | bytes 786440 | tf_op jit(solution)/shard_map/ppermute | solution.py:305
  57.3 4.4 %attend_ring.5 = (f32[4,256,128]{2,1,0:T(8,128)S(1)}, f32[4,256,256]{2,1,0:T(8,128)S(1)}, f32[4,256,128]{2,1,0:T(8,128)S(1)}, f32[4,256,256]{2,1,0:T(8,128)S(1)}) custom-call(s32[1]{0:T(128)} %bitcast.1.me_ref, f32[1]{0:T(128)S(6)} %mul.9.c_ref, ...), custom_call_target="tpu_custom_call", output_to_operand_aliasing={{0}: (6, {}), {1}: (7, {}), {2}: (8, {}), {3}: (9, {})} | custom-call | flops 5368709120 | bytes 4194304 | tf_op jit(solution)/shard_map/attend_ring/pallas_call | solution.py:330
  61.7 3.1 %collective-permute-done.8.blk = bf16[1024,128]{1,0:T(8,128)(2,1)S(1)} collective-permute-done((bf16[1024,128]{1,0:T(8,128)(2,1)S(1)}, bf16[1024,128]{1,0:T(8,128)(2,1)S(1)}, u32[]{:S(2)}, u32[]{:S(2)}) %collective-permute-start.8) | collective-permute-done | bytes 262176 | tf_op jit(solution)/shard_map/ppermute | solution.py:305
  66.5 1.9 %collective-permute-start.10 = (bf16[4,256,256]{2,1,0:T(8,128)(2,1)S(1)}, bf16[4,256,256]{2,1,0:T(8,128)(2,1)S(1)}, u32[]{:S(2)}, u32[]{:S(2)}) collective-permute-start(bf16[4,256,256]{2,1,0:T(8,128)(2,1)S(1)} %get-tuple-element.55), channel_id=1, source_target_pairs={{0,8},{8,0},{16,24},{24,16},{32,40},{40,32},{48,56},{56,48},{64,72... | collective-permute-start | bytes 1572872 | tf_op jit(solution)/shard_map/ppermute | solution.py:353
  70.6 2.5 %merge_project.1 = (bf16[4,256,512]{2,1,0:T(8,128)(2,1)}, bf16[256,512]{1,0:T(8,128)(2,1)S(1)}, bf16[256,512]{1,0:T(8,128)(2,1)S(1)}, bf16[256,512]{1,0:T(8,128)(2,1)S(1)}, bf16[256,512]{1,0:T(8,128)(2,1)S(1)}) custom-call(s32[1]{0:T(128)} %bitcast.tp_ref, f32[4,256,128]{2,1,0:T(8,128)S(1)} %get-tuple-element.51.m, f32[4,256,256]{2,1,0:T(8,128)S(1)} %get-tuple-element.52.a, ...), custom_call_target="tpu_custom_call" | custom-call | flops 4294967296 | bytes 8388608 | tf_op jit(solution)/shard_map/merge_project/pallas_call | solution.py:369
  73.8 4.3 %all-to-all-start.1 = ((bf16[4,256,512]{2,1,0:T(8,128)(2,1)}), bf16[4,256,512]{2,1,0:T(8,128)(2,1)S(1)}, u32[]{:S(2)}, u32[]{:S(2)}) async-start(bf16[4,256,512]{2,1,0:T(8,128)(2,1)} %get-tuple-element.59), calls=%async_computation.1 | async-start | bytes 2097152 | tf_op jit(solution)/shard_map/all_to_all | solution.py:385
  78.1 3.9 %collective-permute-start.11 = (bf16[256,512]{1,0:T(8,128)(2,1)S(1)}, bf16[256,512]{1,0:T(8,128)(2,1)S(1)}, u32[]{:S(2)}, u32[]{:S(2)}) collective-permute-start(bf16[256,512]{1,0:T(8,128)(2,1)S(1)} %get-tuple-element.57), channel_id=1, source_target_pairs={{0,1},{1,2},{2,3},{3,0},{4,5},{5,6},{6,7},{7,4},{8,9},{9,10},{10,1... | collective-permute-start | bytes 786440 | tf_op jit(solution)/shard_map/ppermute | solution.py:383
  82.0 4.6 %collective-permute-start.12 = (bf16[256,512]{1,0:T(8,128)(2,1)S(1)}, bf16[256,512]{1,0:T(8,128)(2,1)S(1)}, u32[]{:S(2)}, u32[]{:S(2)}) collective-permute-start(bf16[256,512]{1,0:T(8,128)(2,1)S(1)} %get-tuple-element.58), channel_id=1, source_target_pairs={{0,2},{1,3},{2,0},{3,1},{4,6},{5,7},{6,4},{7,5},{8,10},{9,11},{10,... | collective-permute-start | bytes 786440 | tf_op jit(solution)/shard_map/ppermute | solution.py:383
  86.6 8.0 %all-to-all-done.1.parts = bf16[4,256,512]{2,1,0:T(8,128)(2,1)S(1)} async-done(((bf16[4,256,512]{2,1,0:T(8,128)(2,1)}), bf16[4,256,512]{2,1,0:T(8,128)(2,1)S(1)}, u32[]{:S(2)}, u32[]{:S(2)}) %all-to-all-start.1) | async-done | bytes 1048608 | tf_op jit(solution)/shard_map/all_to_all | solution.py:385
  94.7 8.2 %collective-permute-start.13 = (bf16[256,512]{1,0:T(8,128)(2,1)S(1)}, bf16[256,512]{1,0:T(8,128)(2,1)S(1)}, u32[]{:S(2)}, u32[]{:S(2)}) collective-permute-start(bf16[256,512]{1,0:T(8,128)(2,1)S(1)} %get-tuple-element.61), channel_id=1, source_target_pairs={{0,4},{1,5},{2,6},{3,7},{4,0},{5,1},{6,2},{7,3},{8,12},{9,13},{10,... | collective-permute-start | bytes 786440 | tf_op jit(solution)/shard_map/ppermute | solution.py:409
  103.0 3.0 %collective-permute-start.14 = (bf16[256,512]{1,0:T(8,128)(2,1)S(1)}, bf16[256,512]{1,0:T(8,128)(2,1)S(1)}, u32[]{:S(2)}, u32[]{:S(2)}) collective-permute-start(bf16[256,512]{1,0:T(8,128)(2,1)S(1)} %get-tuple-element.62), channel_id=1, source_target_pairs={{0,3},{1,0},{2,1},{3,2},{4,7},{5,4},{6,5},{7,6},{8,11},{9,8},{10,9... | collective-permute-start | bytes 786440 | tf_op jit(solution)/shard_map/ppermute | solution.py:383
  107.1 6.9 %collective-permute-done.13.refs_1_ = bf16[256,512]{1,0:T(8,128)(2,1)S(1)} collective-permute-done((bf16[256,512]{1,0:T(8,128)(2,1)S(1)}, bf16[256,512]{1,0:T(8,128)(2,1)S(1)}, u32[]{:S(2)}, u32[]{:S(2)}) %collective-permute-start.13) | collective-permute-done | bytes 262176 | tf_op jit(solution)/shard_map/ppermute | solution.py:409
  114.6 17.3 %all_to_all.15.squares = f32[8,8,256]{2,1,0:T(8,128)S(1)} all-to-all(f32[8,8,256]{2,1,0:T(8,128)S(1)} %get-tuple-element.64), channel_id=1, replica_groups=mesh['seq'=64,'tp'=8] {'tp'}, dimensions={0} | all-to-all | bytes 131072 | tf_op jit(solution)/shard_map/all_to_all | solution.py:421
  (47 shorter events, 13.1 us)
Async XLA Ops:
  1.5 14.0 %collective-permute-start = (bf16[256,128]{1,0:T(8,128)(2,1)S(1)}, bf16[256,128]{1,0:T(8,128)(2,1)S(1)}, u32[]{:S(2)}, u32[]{:S(2)}) collective-permute-start(bf16[256,128]{1,0:T(8,128)(2,1)S(1)} %pad_maximum_fusion.2.here), channel_id=1, source_target_pairs={{0,504},{1,505},{2,506},{3,507},{4,508},{5,509},{6,510},{7,511}} | collective-permute-start | bytes 196616 | tf_op jit(solution)/shard_map/ppermute | solution.py:281
  3.0 18.8 %all-to-all-start = ((bf16[4,256,128]{2,1,0:T(8,128)(2,1)}), bf16[4,256,128]{2,1,0:T(8,128)(2,1)S(1)}, u32[]{:S(2)}, u32[]{:S(2)}) async-start(bf16[4,256,128]{2,1,0:T(8,128)(2,1)} %broadcast_in_dim.3), calls=%async_computation | async-start | bytes 524288 | tf_op jit(solution)/shard_map/all_to_all | solution.py:276
  15.6 1.0 copy-start.4
  15.6 13.4 %copy-start = (bf16[256,128]{1,0:T(8,128)(2,1)S(1)}, bf16[256,128]{1,0:T(8,128)(2,1)}, u32[]{:S(2)}) copy-start(bf16[256,128]{1,0:T(8,128)(2,1)} %k.1) | copy-start | bytes 196612
  15.6 13.4 %copy-start.1 = (bf16[256,128]{1,0:T(8,128)(2,1)S(1)}, bf16[256,128]{1,0:T(8,128)(2,1)}, u32[]{:S(2)}) copy-start(bf16[256,128]{1,0:T(8,128)(2,1)} %v.1) | copy-start | bytes 196612
  15.6 3.5 %collective-permute-start.1 = (bf16[256,128]{1,0:T(8,128)(2,1)S(1)}, bf16[256,128]{1,0:T(8,128)(2,1)S(1)}, u32[]{:S(2)}, u32[]{:S(2)}) collective-permute-start(bf16[256,128]{1,0:T(8,128)(2,1)S(1)} %choose_anchor.1), channel_id=1, source_target_pairs={{0,248},{504,376},{1,249},{505,377},{2,250},{506,378},{3,251},{507... | collective-permute-start | bytes 196616 | tf_op jit(solution)/shard_map/ppermute | solution.py:291
  16.5 13.1 %collective-permute-start.9 = (bf16[256,512]{1,0:T(8,128)(2,1)S(1)}, bf16[256,512]{1,0:T(8,128)(2,1)S(1)}, u32[]{:S(2)}, u32[]{:S(2)}) collective-permute-start(bf16[256,512]{1,0:T(8,128)(2,1)S(1)} %copy-done.4), channel_id=1, source_target_pairs={{0,8},{8,0},{16,24},{24,16},{32,40},{40,32},{48,56},{56,48},{64,72... | collective-permute-start | bytes 786440 | tf_op jit(solution)/shard_map/ppermute | solution.py:292
  21.8 10.3 %collective-permute-start.2 = (bf16[1024,128]{1,0:T(8,128)(2,1)S(1)}, bf16[1024,128]{1,0:T(8,128)(2,1)S(1)}, u32[]{:S(2)}, u32[]{:S(2)}) collective-permute-start(bf16[1024,128]{1,0:T(8,128)(2,1)S(1)} %pad_maximum_fusion.blk), channel_id=1, source_target_pairs={{0,16},{8,24},{16,32},{24,40},{32,48},{40,56},{48,64},{56,72},{64,... | collective-permute-start | bytes 786440 | tf_op jit(solution)/shard_map/ppermute | solution.py:299
  23.8 10.3 %collective-permute-start.5 = (bf16[1024,128]{1,0:T(8,128)(2,1)S(1)}, bf16[1024,128]{1,0:T(8,128)(2,1)S(1)}, u32[]{:S(2)}, u32[]{:S(2)}) collective-permute-start(bf16[1024,128]{1,0:T(8,128)(2,1)S(1)} %pad_maximum_fusion.blk), channel_id=1, source_target_pairs={{0,112},{8,120},{16,0},{24,8},{32,16},{40,24},{48,32},{56,40},{64,... | collective-permute-start | bytes 786440 | tf_op jit(solution)/shard_map/ppermute | solution.py:300
  32.1 11.5 %collective-permute-start.3 = (bf16[1024,128]{1,0:T(8,128)(2,1)S(1)}, bf16[1024,128]{1,0:T(8,128)(2,1)S(1)}, u32[]{:S(2)}, u32[]{:S(2)}) collective-permute-start(bf16[1024,128]{1,0:T(8,128)(2,1)S(1)} %collective-permute-done.2.fwd), channel_id=1, source_target_pairs={{0,16},{8,24},{16,32},{24,40},{32,48},{40,56},{48,64},{56,72},{64,... | collective-permute-start | bytes 786440 | tf_op jit(solution)/shard_map/ppermute | solution.py:302
  34.1 11.5 %collective-permute-start.6 = (bf16[1024,128]{1,0:T(8,128)(2,1)S(1)}, bf16[1024,128]{1,0:T(8,128)(2,1)S(1)}, u32[]{:S(2)}, u32[]{:S(2)}) collective-permute-start(bf16[1024,128]{1,0:T(8,128)(2,1)S(1)} %collective-permute-done.5.bwd), channel_id=1, source_target_pairs={{0,112},{8,120},{16,0},{24,8},{32,16},{40,24},{48,32},{56,40},{64,... | collective-permute-start | bytes 786440 | tf_op jit(solution)/shard_map/ppermute | solution.py:303
  43.6 11.7 %collective-permute-start.4 = (bf16[1024,128]{1,0:T(8,128)(2,1)S(1)}, bf16[1024,128]{1,0:T(8,128)(2,1)S(1)}, u32[]{:S(2)}, u32[]{:S(2)}) collective-permute-start(bf16[1024,128]{1,0:T(8,128)(2,1)S(1)} %collective-permute-done.3.fwd), channel_id=1, source_target_pairs={{0,16},{8,24},{16,32},{24,40},{32,48},{40,56},{48,64},{56,72},{64,... | collective-permute-start | bytes 786440 | tf_op jit(solution)/shard_map/ppermute | solution.py:302
  45.6 9.8 %collective-permute-start.7 = (bf16[1024,128]{1,0:T(8,128)(2,1)S(1)}, bf16[1024,128]{1,0:T(8,128)(2,1)S(1)}, u32[]{:S(2)}, u32[]{:S(2)}) collective-permute-start(bf16[1024,128]{1,0:T(8,128)(2,1)S(1)} %collective-permute-done.6.bwd), channel_id=1, source_target_pairs={{0,112},{8,120},{16,0},{24,8},{32,16},{40,24},{48,32},{56,40},{64,... | collective-permute-start | bytes 786440 | tf_op jit(solution)/shard_map/ppermute | solution.py:303
  55.4 9.5 %collective-permute-start.8 = (bf16[1024,128]{1,0:T(8,128)(2,1)S(1)}, bf16[1024,128]{1,0:T(8,128)(2,1)S(1)}, u32[]{:S(2)}, u32[]{:S(2)}) collective-permute-start(bf16[1024,128]{1,0:T(8,128)(2,1)S(1)} %broadcast_select_fusion), channel_id=1, source_target_pairs={{0,16},{8,120},{16,32},{24,8},{32,48},{40,24},{48,64},{56,40},{64,... | collective-permute-start | bytes 786440 | tf_op jit(solution)/shard_map/ppermute | solution.py:305
  66.5 3.8 %collective-permute-start.10 = (bf16[4,256,256]{2,1,0:T(8,128)(2,1)S(1)}, bf16[4,256,256]{2,1,0:T(8,128)(2,1)S(1)}, u32[]{:S(2)}, u32[]{:S(2)}) collective-permute-start(bf16[4,256,256]{2,1,0:T(8,128)(2,1)S(1)} %get-tuple-element.55), channel_id=1, source_target_pairs={{0,8},{8,0},{16,24},{24,16},{32,40},{40,32},{48,56},{56,48},{64,72... | collective-permute-start | bytes 1572872 | tf_op jit(solution)/shard_map/ppermute | solution.py:353
  68.4 2.2 %copy-start.3 = (bf16[512,4096]{1,0:T(8,128)(2,1)S(1)}, bf16[512,4096]{1,0:T(8,128)(2,1)}, u32[]{:S(2)}) copy-start(bf16[512,4096]{1,0:T(8,128)(2,1)} %w.1) | copy-start | bytes 12582916
  73.1 0.7 copy-start.5
  73.8 20.8 %all-to-all-start.1 = ((bf16[4,256,512]{2,1,0:T(8,128)(2,1)}), bf16[4,256,512]{2,1,0:T(8,128)(2,1)S(1)}, u32[]{:S(2)}, u32[]{:S(2)}) async-start(bf16[4,256,512]{2,1,0:T(8,128)(2,1)} %get-tuple-element.59), calls=%async_computation.1 | async-start | bytes 2097152 | tf_op jit(solution)/shard_map/all_to_all | solution.py:385
  78.1 27.9 %collective-permute-start.11 = (bf16[256,512]{1,0:T(8,128)(2,1)S(1)}, bf16[256,512]{1,0:T(8,128)(2,1)S(1)}, u32[]{:S(2)}, u32[]{:S(2)}) collective-permute-start(bf16[256,512]{1,0:T(8,128)(2,1)S(1)} %get-tuple-element.57), channel_id=1, source_target_pairs={{0,1},{1,2},{2,3},{3,0},{4,5},{5,6},{6,7},{7,4},{8,9},{9,10},{10,1... | collective-permute-start | bytes 786440 | tf_op jit(solution)/shard_map/ppermute | solution.py:383
  82.0 24.0 %collective-permute-start.12 = (bf16[256,512]{1,0:T(8,128)(2,1)S(1)}, bf16[256,512]{1,0:T(8,128)(2,1)S(1)}, u32[]{:S(2)}, u32[]{:S(2)}) collective-permute-start(bf16[256,512]{1,0:T(8,128)(2,1)S(1)} %get-tuple-element.58), channel_id=1, source_target_pairs={{0,2},{1,3},{2,0},{3,1},{4,6},{5,7},{6,4},{7,5},{8,10},{9,11},{10,... | collective-permute-start | bytes 786440 | tf_op jit(solution)/shard_map/ppermute | solution.py:383
  94.7 19.2 %collective-permute-start.13 = (bf16[256,512]{1,0:T(8,128)(2,1)S(1)}, bf16[256,512]{1,0:T(8,128)(2,1)S(1)}, u32[]{:S(2)}, u32[]{:S(2)}) collective-permute-start(bf16[256,512]{1,0:T(8,128)(2,1)S(1)} %get-tuple-element.61), channel_id=1, source_target_pairs={{0,4},{1,5},{2,6},{3,7},{4,0},{5,1},{6,2},{7,3},{8,12},{9,13},{10,... | collective-permute-start | bytes 786440 | tf_op jit(solution)/shard_map/ppermute | solution.py:409
  103.0 11.1 %collective-permute-start.14 = (bf16[256,512]{1,0:T(8,128)(2,1)S(1)}, bf16[256,512]{1,0:T(8,128)(2,1)S(1)}, u32[]{:S(2)}, u32[]{:S(2)}) collective-permute-start(bf16[256,512]{1,0:T(8,128)(2,1)S(1)} %get-tuple-element.62), channel_id=1, source_target_pairs={{0,3},{1,0},{2,1},{3,2},{4,7},{5,4},{6,5},{7,6},{8,11},{9,8},{10,9... | collective-permute-start | bytes 786440 | tf_op jit(solution)/shard_map/ppermute | solution.py:383
  106.0 1.0 copy-start.6
  107.1 24.8 %copy-start.2 = (f32[512]{0:T(512)S(1)}, f32[512]{0:T(512)}, u32[]{:S(2)}) copy-start(f32[512]{0:T(512)} %param.13) | copy-start | bytes 6148

commit v6 on v4

--- a/solution.py
+++ b/solution.py
@@ -170,35 +170,47 @@
             out[h, :, HEAD : 2 * HEAD] = parts.astype(BF16)
 
 
-def merge_kernel(tp_ref, m, a, got, w, att, out):
-    @pl.when(pl.program_id(0) == 0)
-    def _():
-        for h in range(HEADS):
-            parts = got[h][:, HEAD:].astype(F32)
-            lse = (parts[:, 0:1] + parts[:, 1:2]) + parts[:, 2:3]
-            mine = m[h]
-            top = jnp.maximum(mine, lse)
-            w0 = jnp.exp2(mine - top)
-            w1 = jnp.exp2(lse - top)
-            acc = a[h][:, :HEAD] * w0 + got[h][:, :HEAD].astype(F32) * w1
-            total = a[h][:, HEAD:] * w0 + w1
-            att[:, h * HEAD : (h + 1) * HEAD] = (acc / total).astype(BF16)
-
-    out[0] = plain(att[...], w[...]).astype(BF16)
-
-
-def project_kernel(tp_ref, att, w, *outs):
+def project(att, w, half, j, cols):
+    return plain(att[...], w[:, pl.ds(pl.multiple_of((half * NX + j) * cols, cols), cols)]).astype(BF16)
+
+
+def merge_kernel(tp_ref, m, a, got, w, att, there):
+    for h in range(HEADS):
+        parts = got[h][:, HEAD:].astype(F32)
+        lse = (parts[:, 0:1] + parts[:, 1:2]) + parts[:, 2:3]
+        mine = m[h]
+        top = jnp.maximum(mine, lse)
+        w0 = jnp.exp2(mine - top)
+        w1 = jnp.exp2(lse - top)
+        acc = a[h][:, :HEAD] * w0 + got[h][:, :HEAD].astype(F32) * w1
+        total = a[h][:, HEAD:] * w0 + w1
+        att[:, h * HEAD : (h + 1) * HEAD] = (acc / total).astype(BF16)
+    for j in range(NX):
+        there[j] = project(att, w, 1 - tp_ref[0] // NX, j, there.shape[2])
+
+
+def own_kernel(tp_ref, att, w, *outs):
     x, half = tp_ref[0] % NX, tp_ref[0] // NX
     for k, out in enumerate(outs):
-        col = pl.multiple_of((half * NX + (x + k) % NX) * out.shape[1], out.shape[1])
-        out[...] = plain(att[...], w[:, pl.ds(col, out.shape[1])]).astype(BF16)
-
-
-def sum_kernel(parts, out):
+        out[...] = project(att, w, half, (x + k) % NX, out.shape[1])
+
+
+def sum_kernel(parts, *refs):
     total = parts[0].astype(F32)
     for j in range(1, NX):
         total += parts[j].astype(F32)
-    out[...] = total.astype(out.dtype)
+    out, *same = refs[NX - 1 :]
+    out[...] = total.astype(BF16)
+    for source, target in zip(refs, same):
+        target[...] = source[...]
+
+
+def add_kernel(*refs):
+    *parts, out = refs
+    total = parts[0][...].astype(F32)
+    for part in parts[1:]:
+        total += part[...].astype(F32)
+    out[...] = total
 
 
 def choose_kernel(me_ref, here, there, out):
@@ -213,11 +225,11 @@
         out[...] = here[...]
 
 
-def square_kernel(crossed, *refs):
+def square_kernel(part, *refs):
     *parts, out, squares = refs
-    total = crossed[...].astype(F32)
-    for part in parts:
-        total += part[...].astype(F32)
+    total = part[...]
+    for other in parts:
+        total += other[...].astype(F32)
     out[...] = total
     ones = jnp.ones((8, total.shape[1]), F32)
     sums = lax.dot_general(
@@ -359,68 +371,63 @@
 
     wide_cols = out_weight.shape[1] // (NX * NH)
 
-    def columns(own_half, j, tp_ref):
-        half = tp_ref[0] // NX
-        return (0, (half if own_half else 1 - half) * NX + j)
-
-    whole = lambda *shape: pl.BlockSpec(shape, lambda j, tp_ref: (0,) * len(shape))
-    weights = lambda own_half: pl.BlockSpec((HEADS * HEAD, wide_cols), functools.partial(columns, own_half))
-    parts = pl.BlockSpec((1, TOK, wide_cols), lambda j, tp_ref: (j, 0, 0))
-    parts_shape = jax.ShapeDtypeStruct((NX, TOK, wide_cols), BF16)
+    block_shape = jax.ShapeDtypeStruct((TOK, wide_cols), BF16)
     att, there = pl.pallas_call(
         merge_kernel,
-        out_shape=[jax.ShapeDtypeStruct((TOK, HEADS * HEAD), BF16), parts_shape],
-        grid_spec=pltpu.PrefetchScalarGridSpec(
-            num_scalar_prefetch=1,
-            grid=(NX,),
-            in_specs=[
-                whole(HEADS, TOK, HEAD),
-                whole(HEADS, TOK, 2 * HEAD),
-                whole(HEADS, TOK, 2 * HEAD),
-                weights(False),
-            ],
-            out_specs=[whole(TOK, HEADS * HEAD), parts],
-        ),
-        compiler_params=params(),
-        cost_estimate=pl.CostEstimate(flops=1 << 31, bytes_accessed=5 << 20, transcendentals=1 << 18),
+        out_shape=[
+            jax.ShapeDtypeStruct((TOK, HEADS * HEAD), BF16),
+            jax.ShapeDtypeStruct((NX, TOK, wide_cols), BF16),
+        ],
+        in_specs=[SMEM] + [VMEM] * 4,
+        out_specs=[VMEM] * 2,
+        compiler_params=params(),
+        cost_estimate=pl.CostEstimate(flops=1 << 31, bytes_accessed=8 << 20, transcendentals=1 << 18),
         name="merge_project",
     )(tp_s, m0, a0, got, out_weight)
     rows = [[h * NX + x for x in range(NX)] for h in range(NH)]
     swap = [(i, (i + NX) % (NX * NH)) for i in range(NX * NH)]
     there = lax.all_to_all(there, "tp", 0, 0, axis_index_groups=rows)
     here = pl.pallas_call(
-        project_kernel,
-        out_shape=[jax.ShapeDtypeStruct((TOK, wide_cols), BF16)] * NX,
+        own_kernel,
+        out_shape=[block_shape] * NX,
         in_specs=[SMEM] + [VMEM] * 2,
         out_specs=[VMEM] * NX,
         compiler_params=params(),
         cost_estimate=pl.CostEstimate(flops=1 << 31, bytes_accessed=2 << 20, transcendentals=0),
         name="project_own_half",
     )(tp_s, att, out_weight)
-    here = [here[0]] + [
-        lax.ppermute(here[k], "tp", [(i, i // NX * NX + (i + k) % NX) for i in range(NX * NH)])
-        for k in range(1, NX)
+    there, *parts = pl.pallas_call(
+        sum_kernel,
+        out_shape=[block_shape] * NX,
+        in_specs=[VMEM] * NX,
+        out_specs=[VMEM] * NX,
+        compiler_params=params(),
+        name="sum_other_half",
+    )(there, *here[1:])
+    parts = [
+        lax.ppermute(part, "tp", [(i, i // NX * NX + (i + k) % NX) for i in range(NX * NH)])
+        for k, part in enumerate(parts, 1)
     ]
-    there = pl.pallas_call(
-        sum_kernel,
-        out_shape=jax.ShapeDtypeStruct((TOK, wide_cols), BF16),
-        in_specs=[VMEM],
+    part = pl.pallas_call(
+        add_kernel,
+        out_shape=jax.ShapeDtypeStruct((TOK, wide_cols), F32),
+        in_specs=[VMEM] * 2,
         out_specs=VMEM,
         compiler_params=params(),
-        name="sum_other_half",
-    )(there)
-    crossed = lax.ppermute(there, "tp", swap)
+        cost_estimate=pl.CostEstimate(flops=1 << 33, bytes_accessed=1 << 20, transcendentals=0),
+        name="add_crossed",
+    )(here[0], lax.ppermute(there, "tp", swap))
     projected, squares = pl.pallas_call(
         square_kernel,
         out_shape=[
             jax.ShapeDtypeStruct((TOK, wide_cols), F32),
             jax.ShapeDtypeStruct((NX * NH, 8, TOK), F32),
         ],
-        in_specs=[VMEM] * (NX + 1),
+        in_specs=[VMEM] * NX,
         out_specs=[VMEM] * 2,
         compiler_params=params(),
         name="sum_and_square",
-    )(crossed, *here)
+    )(part, *parts)
     squares = lax.all_to_all(squares, "tp", 0, 0)
     return pl.pallas_call(
         functools.partial(norm_kernel, out_weight.shape[1]),

time: 133 us -> 135 us (1.015)
  waiting for transfers between devices: 19.5 us -> 29.2 us
  blocking collectives: 17.3 us -> 14 us
  starting transfers between devices: 65.5 us -> 62.7 us
    all_to_all x1, waiting for transfers between devices: 1.68 us -> 12.8 us  [shards(): there = lax.all_to_all(there, 'tp', 0, 0, axis_index_groups=rows)]
    all_to_all x1, blocking collectives: 17.3 us -> 14 us  [shards(): squares = lax.all_to_all(squares, 'tp', 0, 0)]
    ppermute x4, starting transfers between devices: 20.1 us -> 17.2 us  [the longest x3 8.97 us: shards(): lax.ppermute(part, 'tp', [(i, i // NX * NX + (i + k) % NX) for i in range...]
    ppermute x4, waiting for transfers between devices: 11 us -> 9.52 us  [the longest x3 6.79 us: shards(): lax.ppermute(part, 'tp', [(i, i // NX * NX + (i + k) % NX) for i in range...]
  transfers between devices with their start and end apart: 17 -> 17, of which waited for: 6 -> 7; matrix products, arithmetic and copies ran while one was open for 1% -> 1% of each run, Pallas kernels for 13% -> 13%
where the time goes in v6:
time: 135 us; the launch traced here: 134 us
  starting transfers between devices  62.7 us (46%)
  waiting for transfers between devices  29.2 us (22%)
  Pallas kernels  22.7 us (17%)
  blocking collectives  14 us (10%)
  local copies, waits for them, and re-layouts  4.2 us (3%)
  between operations  1.69 us (1%)
    all_to_all x1, blocking collectives, shards(): squares = lax.all_to_all(squares, 'tp', 0, 0)  14 us
    all_to_all x1, waiting for transfers between devices, shards(): there = lax.all_to_all(there, 'tp', 0, 0, axis_index_groups=rows)  12.8 us
    all_to_all x1, starting transfers between devices, shards(): lax.all_to_all(jnp.broadcast_to(own, (NZ, SLOT, HEAD)), 'seq', 0, 0, axis...  12.6 us
    pallas_call x3, Pallas kernels, shards(): pl.pallas_call(functools.partial(ring_kernel, step), out_shape=state_shap...  12.2 us
    ppermute x2, starting transfers between devices, shards(): bwd.append(lax.ppermute(bwd[-1], 'seq', y_perm(-1)))  10.3 us
    ppermute x3, starting transfers between devices, shards(): lax.ppermute(part, 'tp', [(i, i // NX * NX + (i + k) % NX) for i in range...  8.97 us
    ppermute x1, starting transfers between devices, shards(): lax.ppermute(there, 'tp', swap)  8.22 us
    ppermute x3, waiting for transfers between devices, shards(): lax.ppermute(part, 'tp', [(i, i // NX * NX + (i + k) % NX) for i in range...  6.79 us
  transfers between devices with their start and end apart: 17, of which 7 were waited for; matrix products, arithmetic and copies ran while one was open for 1% of the time, Pallas kernels for 13%

profile of v6, /device:TPU:64, one launch (start us, length us, event | category | flops | bytes accessed | tf_op | source)
XLA Modules:
  0.0 134.5 jit_solution(18224977471432263355)
XLA Ops:
  2.9 12.6 %all-to-all-start = ((bf16[4,256,128]{2,1,0:T(8,128)(2,1)}), bf16[4,256,128]{2,1,0:T(8,128)(2,1)S(1)}, u32[]{:S(2)}, u32[]{:S(2)}) async-start(bf16[4,256,128]{2,1,0:T(8,128)(2,1)} %broadcast_in_dim.3), calls=%async_computation | async-start | bytes 524288 | tf_op jit(solution)/shard_map/all_to_all | solution.py:282
  19.1 2.7 %all-to-all-done = bf16[4,256,128]{2,1,0:T(8,128)(2,1)S(1)} async-done(((bf16[4,256,128]{2,1,0:T(8,128)(2,1)}), bf16[4,256,128]{2,1,0:T(8,128)(2,1)S(1)}, u32[]{:S(2)}, u32[]{:S(2)}) %all-to-all-start) | async-done | bytes 262176 | tf_op jit(solution)/shard_map/all_to_all | solution.py:282
  23.8 5.1 %collective-permute-start.5 = (bf16[1024,128]{1,0:T(8,128)(2,1)S(1)}, bf16[1024,128]{1,0:T(8,128)(2,1)S(1)}, u32[]{:S(2)}, u32[]{:S(2)}) collective-permute-start(bf16[1024,128]{1,0:T(8,128)(2,1)S(1)} %pad_maximum_fusion.blk), channel_id=1, source_target_pairs={{0,112},{8,120},{16,0},{24,8},{32,16},{40,24},{48,32},{56,40},{64,... | collective-permute-start | bytes 786440 | tf_op jit(solution)/shard_map/ppermute | solution.py:306
  29.6 2.4 %attend_own_chip.1 = (f32[4,256,128]{2,1,0:T(8,128)S(1)}, f32[4,256,256]{2,1,0:T(8,128)S(1)}, f32[4,256,128]{2,1,0:T(8,128)S(1)}, f32[4,256,256]{2,1,0:T(8,128)S(1)}) custom-call(s32[1]{0:T(128)} %bitcast.1.me_ref, f32[1]{0:T(128)S(6)} %mul.9.c_ref, bf16[256,512]{1,0:T(8,128)(2,1)S(1)} %copy-done.5, ...), custom_call_target="tpu_custom_call", output_to_operand_aliasing={{0}: (5, {}), {1}: (6, {})} | custom-call | flops 2684354560 | bytes 4194304 | tf_op jit(solution)/shard_map/attend_own_chip/pallas_call | solution.py:324
  34.0 5.1 %collective-permute-start.6 = (bf16[1024,128]{1,0:T(8,128)(2,1)S(1)}, bf16[1024,128]{1,0:T(8,128)(2,1)S(1)}, u32[]{:S(2)}, u32[]{:S(2)}) collective-permute-start(bf16[1024,128]{1,0:T(8,128)(2,1)S(1)} %collective-permute-done.5.bwd), channel_id=1, source_target_pairs={{0,112},{8,120},{16,0},{24,8},{32,16},{40,24},{48,32},{56,40},{64,... | collective-permute-start | bytes 786440 | tf_op jit(solution)/shard_map/ppermute | solution.py:309
  39.1 4.1 %attend_ring.3 = (f32[4,256,128]{2,1,0:T(8,128)S(1)}, f32[4,256,256]{2,1,0:T(8,128)S(1)}, f32[4,256,128]{2,1,0:T(8,128)S(1)}, f32[4,256,256]{2,1,0:T(8,128)S(1)}) custom-call(s32[1]{0:T(128)} %bitcast.1.me_ref, f32[1]{0:T(128)S(6)} %mul.9.c_ref, ...), custom_call_target="tpu_custom_call", output_to_operand_aliasing={{0}: (6, {}), {1}: (7, {}), {2}: (8, {}), {3}: (9, {})} | custom-call | flops 5368709120 | bytes 4194304 | tf_op jit(solution)/shard_map/attend_ring/pallas_call | solution.py:336
  43.2 1.9 %collective-permute-start.4 = (bf16[1024,128]{1,0:T(8,128)(2,1)S(1)}, bf16[1024,128]{1,0:T(8,128)(2,1)S(1)}, u32[]{:S(2)}, u32[]{:S(2)}) collective-permute-start(bf16[1024,128]{1,0:T(8,128)(2,1)S(1)} %collective-permute-done.3.fwd), channel_id=1, source_target_pairs={{0,16},{8,24},{16,32},{24,40},{32,48},{40,56},{48,64},{56,72},{64,... | collective-permute-start | bytes 786440 | tf_op jit(solution)/shard_map/ppermute | solution.py:308
  45.1 5.1 %collective-permute-start.7 = (bf16[1024,128]{1,0:T(8,128)(2,1)S(1)}, bf16[1024,128]{1,0:T(8,128)(2,1)S(1)}, u32[]{:S(2)}, u32[]{:S(2)}) collective-permute-start(bf16[1024,128]{1,0:T(8,128)(2,1)S(1)} %collective-permute-done.6.bwd), channel_id=1, source_target_pairs={{0,112},{8,120},{16,0},{24,8},{32,16},{40,24},{48,32},{56,40},{64,... | collective-permute-start | bytes 786440 | tf_op jit(solution)/shard_map/ppermute | solution.py:309
  50.3 4.1 %attend_ring.4 = (f32[4,256,128]{2,1,0:T(8,128)S(1)}, f32[4,256,256]{2,1,0:T(8,128)S(1)}, f32[4,256,128]{2,1,0:T(8,128)S(1)}, f32[4,256,256]{2,1,0:T(8,128)S(1)}) custom-call(s32[1]{0:T(128)} %bitcast.1.me_ref, f32[1]{0:T(128)S(6)} %mul.9.c_ref, ...), custom_call_target="tpu_custom_call", output_to_operand_aliasing={{0}: (6, {}), {1}: (7, {}), {2}: (8, {}), {3}: (9, {})} | custom-call | flops 5368709120 | bytes 4194304 | tf_op jit(solution)/shard_map/attend_ring/pallas_call | solution.py:336
  54.4 2.1 %collective-permute-start.8 = (bf16[1024,128]{1,0:T(8,128)(2,1)S(1)}, bf16[1024,128]{1,0:T(8,128)(2,1)S(1)}, u32[]{:S(2)}, u32[]{:S(2)}) collective-permute-start(bf16[1024,128]{1,0:T(8,128)(2,1)S(1)} %broadcast_select_fusion), channel_id=1, source_target_pairs={{0,16},{8,120},{16,32},{24,8},{32,48},{40,24},{48,64},{56,40},{64,... | collective-permute-start | bytes 786440 | tf_op jit(solution)/shard_map/ppermute | solution.py:311
  56.5 4.1 %attend_ring.5 = (f32[4,256,128]{2,1,0:T(8,128)S(1)}, f32[4,256,256]{2,1,0:T(8,128)S(1)}, f32[4,256,128]{2,1,0:T(8,128)S(1)}, f32[4,256,256]{2,1,0:T(8,128)S(1)}) custom-call(s32[1]{0:T(128)} %bitcast.1.me_ref, f32[1]{0:T(128)S(6)} %mul.9.c_ref, ...), custom_call_target="tpu_custom_call", output_to_operand_aliasing={{0}: (6, {}), {1}: (7, {}), {2}: (8, {}), {3}: (9, {})} | custom-call | flops 5368709120 | bytes 4194304 | tf_op jit(solution)/shard_map/attend_ring/pallas_call | solution.py:336
  60.6 3.5 %collective-permute-done.8.blk = bf16[1024,128]{1,0:T(8,128)(2,1)S(1)} collective-permute-done((bf16[1024,128]{1,0:T(8,128)(2,1)S(1)}, bf16[1024,128]{1,0:T(8,128)(2,1)S(1)}, u32[]{:S(2)}, u32[]{:S(2)}) %collective-permute-start.8) | collective-permute-done | bytes 262176 | tf_op jit(solution)/shard_map/ppermute | solution.py:311
  69.8 2.1 %merge_project.1 = (bf16[256,512]{1,0:T(8,128)(2,1)S(1)}, bf16[4,256,512]{2,1,0:T(8,128)(2,1)}) custom-call(s32[1]{0:T(128)} %bitcast.tp_ref, f32[4,256,128]{2,1,0:T(8,128)S(1)} %get-tuple-element.54.m, f32[4,256,256]{2,1,0:T(8,128)S(1)} %get-tuple-element.55.a, bf16[4,256,256]{2,1,0:T(8,128)(2,1)S(1)} %collective-permute-done.10.got, ...), custom_call_target="tpu_custom_call" | custom-call | flops 2147483648 | bytes 8388608 | tf_op jit(solution)/shard_map/merge_project/pallas_call | solution.py:375
  71.9 4.3 %all-to-all-start.1 = ((bf16[4,256,512]{2,1,0:T(8,128)(2,1)}), bf16[4,256,512]{2,1,0:T(8,128)(2,1)S(1)}, u32[]{:S(2)}, u32[]{:S(2)}) async-start(bf16[4,256,512]{2,1,0:T(8,128)(2,1)} %get-tuple-element.61), calls=%async_computation.1 | async-start | bytes 2097152 | tf_op jit(solution)/shard_map/all_to_all | solution.py:389
  76.2 2.2 %copy-done.4 = bf16[512,4096]{1,0:T(8,128)(2,1)S(1)} copy-done((bf16[512,4096]{1,0:T(8,128)(2,1)S(1)}, bf16[512,4096]{1,0:T(8,128)(2,1)}, u32[]{:S(2)}) %copy-start.4) | copy-done | bytes 4194328
  79.1 12.8 %all-to-all-done.1.parts = bf16[4,256,512]{2,1,0:T(8,128)(2,1)S(1)} async-done(((bf16[4,256,512]{2,1,0:T(8,128)(2,1)}), bf16[4,256,512]{2,1,0:T(8,128)(2,1)S(1)}, u32[]{:S(2)}, u32[]{:S(2)}) %all-to-all-start.1) | async-done | bytes 1048608 | tf_op jit(solution)/shard_map/all_to_all | solution.py:389
  92.1 8.2 %collective-permute-start.11 = (bf16[256,512]{1,0:T(8,128)(2,1)S(1)}, bf16[256,512]{1,0:T(8,128)(2,1)S(1)}, u32[]{:S(2)}, u32[]{:S(2)}) collective-permute-start(bf16[256,512]{1,0:T(8,128)(2,1)S(1)} %get-tuple-element.65), channel_id=1, source_target_pairs={{0,4},{1,5},{2,6},{3,7},{4,0},{5,1},{6,2},{7,3},{8,12},{9,13},{10,... | collective-permute-start | bytes 786440 | tf_op jit(solution)/shard_map/ppermute | solution.py:419
  100.3 2.5 %collective-permute-start.12 = (bf16[256,512]{1,0:T(8,128)(2,1)S(1)}, bf16[256,512]{1,0:T(8,128)(2,1)S(1)}, u32[]{:S(2)}, u32[]{:S(2)}) collective-permute-start(bf16[256,512]{1,0:T(8,128)(2,1)S(1)} %get-tuple-element.66), channel_id=1, source_target_pairs={{0,1},{1,2},{2,3},{3,0},{4,5},{5,6},{6,7},{7,4},{8,9},{9,10},{10,1... | collective-permute-start | bytes 786440 | tf_op jit(solution)/shard_map/ppermute | solution.py:408
  102.8 4.0 %collective-permute-start.13 = (bf16[256,512]{1,0:T(8,128)(2,1)S(1)}, bf16[256,512]{1,0:T(8,128)(2,1)S(1)}, u32[]{:S(2)}, u32[]{:S(2)}) collective-permute-start(bf16[256,512]{1,0:T(8,128)(2,1)S(1)} %get-tuple-element.67), channel_id=1, source_target_pairs={{0,2},{1,3},{2,0},{3,1},{4,6},{5,7},{6,4},{7,5},{8,10},{9,11},{10,... | collective-permute-start | bytes 786440 | tf_op jit(solution)/shard_map/ppermute | solution.py:408
  106.8 2.5 %collective-permute-start.14 = (bf16[256,512]{1,0:T(8,128)(2,1)S(1)}, bf16[256,512]{1,0:T(8,128)(2,1)S(1)}, u32[]{:S(2)}, u32[]{:S(2)}) collective-permute-start(bf16[256,512]{1,0:T(8,128)(2,1)S(1)} %get-tuple-element.68), channel_id=1, source_target_pairs={{0,3},{1,0},{2,1},{3,2},{4,7},{5,4},{6,5},{7,6},{8,11},{9,8},{10,9... | collective-permute-start | bytes 786440 | tf_op jit(solution)/shard_map/ppermute | solution.py:408
  109.3 2.7 %collective-permute-done.11.refs_1_ = bf16[256,512]{1,0:T(8,128)(2,1)S(1)} collective-permute-done((bf16[256,512]{1,0:T(8,128)(2,1)S(1)}, bf16[256,512]{1,0:T(8,128)(2,1)S(1)}, u32[]{:S(2)}, u32[]{:S(2)}) %collective-permute-start.11) | collective-permute-done | bytes 262176 | tf_op jit(solution)/shard_map/ppermute | solution.py:419
  112.1 4.3 %collective-permute-done.12.refs_0_ = bf16[256,512]{1,0:T(8,128)(2,1)S(1)} collective-permute-done((bf16[256,512]{1,0:T(8,128)(2,1)S(1)}, bf16[256,512]{1,0:T(8,128)(2,1)S(1)}, u32[]{:S(2)}, u32[]{:S(2)}) %collective-permute-start.12) | collective-permute-done | bytes 262176 | tf_op jit(solution)/shard_map/ppermute | solution.py:408
  116.4 2.5 %collective-permute-done.14.refs_2_ = bf16[256,512]{1,0:T(8,128)(2,1)S(1)} collective-permute-done((bf16[256,512]{1,0:T(8,128)(2,1)S(1)}, bf16[256,512]{1,0:T(8,128)(2,1)S(1)}, u32[]{:S(2)}, u32[]{:S(2)}) %collective-permute-start.14) | collective-permute-done | bytes 262176 | tf_op jit(solution)/shard_map/ppermute | solution.py:408
  119.5 14.0 %all_to_all.15.squares = f32[8,8,256]{2,1,0:T(8,128)S(1)} all-to-all(f32[8,8,256]{2,1,0:T(8,128)S(1)} %get-tuple-element.70), channel_id=1, replica_groups=mesh['seq'=64,'tp'=8] {'tp'}, dimensions={0} | all-to-all | bytes 131072 | tf_op jit(solution)/shard_map/all_to_all | solution.py:431
  (45 shorter events, 17.8 us)
Async XLA Ops:
  1.5 14.1 %collective-permute-start = (bf16[256,128]{1,0:T(8,128)(2,1)S(1)}, bf16[256,128]{1,0:T(8,128)(2,1)S(1)}, u32[]{:S(2)}, u32[]{:S(2)}) collective-permute-start(bf16[256,128]{1,0:T(8,128)(2,1)S(1)} %pad_maximum_fusion.2.here), channel_id=1, source_target_pairs={{0,504},{1,505},{2,506},{3,507},{4,508},{5,509},{6,510},{7,511}} | collective-permute-start | bytes 196616 | tf_op jit(solution)/shard_map/ppermute | solution.py:287
  2.9 18.9 %all-to-all-start = ((bf16[4,256,128]{2,1,0:T(8,128)(2,1)}), bf16[4,256,128]{2,1,0:T(8,128)(2,1)S(1)}, u32[]{:S(2)}, u32[]{:S(2)}) async-start(bf16[4,256,128]{2,1,0:T(8,128)(2,1)} %broadcast_in_dim.3), calls=%async_computation | async-start | bytes 524288 | tf_op jit(solution)/shard_map/all_to_all | solution.py:282
  15.6 1.0 copy-start.5
  15.6 13.4 %copy-start = (bf16[256,128]{1,0:T(8,128)(2,1)S(1)}, bf16[256,128]{1,0:T(8,128)(2,1)}, u32[]{:S(2)}) copy-start(bf16[256,128]{1,0:T(8,128)(2,1)} %k.1) | copy-start | bytes 196612
  15.6 13.4 %copy-start.1 = (bf16[256,128]{1,0:T(8,128)(2,1)S(1)}, bf16[256,128]{1,0:T(8,128)(2,1)}, u32[]{:S(2)}) copy-start(bf16[256,128]{1,0:T(8,128)(2,1)} %v.1) | copy-start | bytes 196612
  15.6 3.5 %collective-permute-start.1 = (bf16[256,128]{1,0:T(8,128)(2,1)S(1)}, bf16[256,128]{1,0:T(8,128)(2,1)S(1)}, u32[]{:S(2)}, u32[]{:S(2)}) collective-permute-start(bf16[256,128]{1,0:T(8,128)(2,1)S(1)} %choose_anchor.1), channel_id=1, source_target_pairs={{0,248},{504,376},{1,249},{505,377},{2,250},{506,378},{3,251},{507... | collective-permute-start | bytes 196616 | tf_op jit(solution)/shard_map/ppermute | solution.py:297
  16.5 13.1 %collective-permute-start.9 = (bf16[256,512]{1,0:T(8,128)(2,1)S(1)}, bf16[256,512]{1,0:T(8,128)(2,1)S(1)}, u32[]{:S(2)}, u32[]{:S(2)}) collective-permute-start(bf16[256,512]{1,0:T(8,128)(2,1)S(1)} %copy-done.5), channel_id=1, source_target_pairs={{0,8},{8,0},{16,24},{24,16},{32,40},{40,32},{48,56},{56,48},{64,72... | collective-permute-start | bytes 786440 | tf_op jit(solution)/shard_map/ppermute | solution.py:298
  21.8 10.2 %collective-permute-start.2 = (bf16[1024,128]{1,0:T(8,128)(2,1)S(1)}, bf16[1024,128]{1,0:T(8,128)(2,1)S(1)}, u32[]{:S(2)}, u32[]{:S(2)}) collective-permute-start(bf16[1024,128]{1,0:T(8,128)(2,1)S(1)} %pad_maximum_fusion.blk), channel_id=1, source_target_pairs={{0,16},{8,24},{16,32},{24,40},{32,48},{40,56},{48,64},{56,72},{64,... | collective-permute-start | bytes 786440 | tf_op jit(solution)/shard_map/ppermute | solution.py:305
  23.8 10.2 %collective-permute-start.5 = (bf16[1024,128]{1,0:T(8,128)(2,1)S(1)}, bf16[1024,128]{1,0:T(8,128)(2,1)S(1)}, u32[]{:S(2)}, u32[]{:S(2)}) collective-permute-start(bf16[1024,128]{1,0:T(8,128)(2,1)S(1)} %pad_maximum_fusion.blk), channel_id=1, source_target_pairs={{0,112},{8,120},{16,0},{24,8},{32,16},{40,24},{48,32},{56,40},{64,... | collective-permute-start | bytes 786440 | tf_op jit(solution)/shard_map/ppermute | solution.py:306
  32.0 11.2 %collective-permute-start.3 = (bf16[1024,128]{1,0:T(8,128)(2,1)S(1)}, bf16[1024,128]{1,0:T(8,128)(2,1)S(1)}, u32[]{:S(2)}, u32[]{:S(2)}) collective-permute-start(bf16[1024,128]{1,0:T(8,128)(2,1)S(1)} %collective-permute-done.2.fwd), channel_id=1, source_target_pairs={{0,16},{8,24},{16,32},{24,40},{32,48},{40,56},{48,64},{56,72},{64,... | collective-permute-start | bytes 786440 | tf_op jit(solution)/shard_map/ppermute | solution.py:308
  34.0 11.2 %collective-permute-start.6 = (bf16[1024,128]{1,0:T(8,128)(2,1)S(1)}, bf16[1024,128]{1,0:T(8,128)(2,1)S(1)}, u32[]{:S(2)}, u32[]{:S(2)}) collective-permute-start(bf16[1024,128]{1,0:T(8,128)(2,1)S(1)} %collective-permute-done.5.bwd), channel_id=1, source_target_pairs={{0,112},{8,120},{16,0},{24,8},{32,16},{40,24},{48,32},{56,40},{64,... | collective-permute-start | bytes 786440 | tf_op jit(solution)/shard_map/ppermute | solution.py:309
  43.2 11.2 %collective-permute-start.4 = (bf16[1024,128]{1,0:T(8,128)(2,1)S(1)}, bf16[1024,128]{1,0:T(8,128)(2,1)S(1)}, u32[]{:S(2)}, u32[]{:S(2)}) collective-permute-start(bf16[1024,128]{1,0:T(8,128)(2,1)S(1)} %collective-permute-done.3.fwd), channel_id=1, source_target_pairs={{0,16},{8,24},{16,32},{24,40},{32,48},{40,56},{48,64},{56,72},{64,... | collective-permute-start | bytes 786440 | tf_op jit(solution)/shard_map/ppermute | solution.py:308
  45.1 9.2 %collective-permute-start.7 = (bf16[1024,128]{1,0:T(8,128)(2,1)S(1)}, bf16[1024,128]{1,0:T(8,128)(2,1)S(1)}, u32[]{:S(2)}, u32[]{:S(2)}) collective-permute-start(bf16[1024,128]{1,0:T(8,128)(2,1)S(1)} %collective-permute-done.6.bwd), channel_id=1, source_target_pairs={{0,112},{8,120},{16,0},{24,8},{32,16},{40,24},{48,32},{56,40},{64,... | collective-permute-start | bytes 786440 | tf_op jit(solution)/shard_map/ppermute | solution.py:309
  54.4 9.7 %collective-permute-start.8 = (bf16[1024,128]{1,0:T(8,128)(2,1)S(1)}, bf16[1024,128]{1,0:T(8,128)(2,1)S(1)}, u32[]{:S(2)}, u32[]{:S(2)}) collective-permute-start(bf16[1024,128]{1,0:T(8,128)(2,1)S(1)} %broadcast_select_fusion), channel_id=1, source_target_pairs={{0,16},{8,120},{16,32},{24,8},{32,48},{40,24},{48,64},{56,40},{64,... | collective-permute-start | bytes 786440 | tf_op jit(solution)/shard_map/ppermute | solution.py:311
  65.7 3.8 %collective-permute-start.10 = (bf16[4,256,256]{2,1,0:T(8,128)(2,1)S(1)}, bf16[4,256,256]{2,1,0:T(8,128)(2,1)S(1)}, u32[]{:S(2)}, u32[]{:S(2)}) collective-permute-start(bf16[4,256,256]{2,1,0:T(8,128)(2,1)S(1)} %get-tuple-element.58), channel_id=1, source_target_pairs={{0,8},{8,0},{16,24},{24,16},{32,40},{40,32},{48,56},{56,48},{64,72... | collective-permute-start | bytes 1572872 | tf_op jit(solution)/shard_map/ppermute | solution.py:359
  67.6 2.2 %copy-start.3 = (bf16[512,4096]{1,0:T(8,128)(2,1)S(1)}, bf16[512,4096]{1,0:T(8,128)(2,1)}, u32[]{:S(2)}) copy-start(bf16[512,4096]{1,0:T(8,128)(2,1)} %w.3) | copy-start | bytes 12582916
  71.9 20.1 %all-to-all-start.1 = ((bf16[4,256,512]{2,1,0:T(8,128)(2,1)}), bf16[4,256,512]{2,1,0:T(8,128)(2,1)S(1)}, u32[]{:S(2)}, u32[]{:S(2)}) async-start(bf16[4,256,512]{2,1,0:T(8,128)(2,1)} %get-tuple-element.61), calls=%async_computation.1 | async-start | bytes 2097152 | tf_op jit(solution)/shard_map/all_to_all | solution.py:389
  76.2 2.2 %copy-start.4 = (bf16[512,4096]{1,0:T(8,128)(2,1)S(1)}, bf16[512,4096]{1,0:T(8,128)(2,1)}, u32[]{:S(2)}) copy-start(bf16[512,4096]{1,0:T(8,128)(2,1)} %w.3) | copy-start | bytes 12582916
  92.1 20.0 %collective-permute-start.11 = (bf16[256,512]{1,0:T(8,128)(2,1)S(1)}, bf16[256,512]{1,0:T(8,128)(2,1)S(1)}, u32[]{:S(2)}, u32[]{:S(2)}) collective-permute-start(bf16[256,512]{1,0:T(8,128)(2,1)S(1)} %get-tuple-element.65), channel_id=1, source_target_pairs={{0,4},{1,5},{2,6},{3,7},{4,0},{5,1},{6,2},{7,3},{8,12},{9,13},{10,... | collective-permute-start | bytes 786440 | tf_op jit(solution)/shard_map/ppermute | solution.py:419
  100.3 16.0 %collective-permute-start.12 = (bf16[256,512]{1,0:T(8,128)(2,1)S(1)}, bf16[256,512]{1,0:T(8,128)(2,1)S(1)}, u32[]{:S(2)}, u32[]{:S(2)}) collective-permute-start(bf16[256,512]{1,0:T(8,128)(2,1)S(1)} %get-tuple-element.66), channel_id=1, source_target_pairs={{0,1},{1,2},{2,3},{3,0},{4,5},{5,6},{6,7},{7,4},{8,9},{9,10},{10,1... | collective-permute-start | bytes 786440 | tf_op jit(solution)/shard_map/ppermute | solution.py:408
  102.8 13.6 %collective-permute-start.13 = (bf16[256,512]{1,0:T(8,128)(2,1)S(1)}, bf16[256,512]{1,0:T(8,128)(2,1)S(1)}, u32[]{:S(2)}, u32[]{:S(2)}) collective-permute-start(bf16[256,512]{1,0:T(8,128)(2,1)S(1)} %get-tuple-element.67), channel_id=1, source_target_pairs={{0,2},{1,3},{2,0},{3,1},{4,6},{5,7},{6,4},{7,5},{8,10},{9,11},{10,... | collective-permute-start | bytes 786440 | tf_op jit(solution)/shard_map/ppermute | solution.py:408
  106.8 12.1 %collective-permute-start.14 = (bf16[256,512]{1,0:T(8,128)(2,1)S(1)}, bf16[256,512]{1,0:T(8,128)(2,1)S(1)}, u32[]{:S(2)}, u32[]{:S(2)}) collective-permute-start(bf16[256,512]{1,0:T(8,128)(2,1)S(1)} %get-tuple-element.68), channel_id=1, source_target_pairs={{0,3},{1,0},{2,1},{3,2},{4,7},{5,4},{6,5},{7,6},{8,11},{9,8},{10,9... | collective-permute-start | bytes 786440 | tf_op jit(solution)/shard_map/ppermute | solution.py:408
  112.0 21.4 %copy-start.2 = (f32[512]{0:T(512)S(1)}, f32[512]{0:T(512)}, u32[]{:S(2)}) copy-start(f32[512]{0:T(512)} %param.13) | copy-start | bytes 6148

commit v7 on v6

--- a/solution.py
+++ b/solution.py
@@ -76,27 +76,54 @@
         vv[pl.ds(j * BLOCK, BLOCK), HEAD : 2 * HEAD] = jnp.full((BLOCK, HEAD), scale, F32).astype(BF16)
 
 
-def update(c, q, kk, vv, m_ref, acc_ref, h):
-    s = cross(q, kk[...]) * c
-    m_old = m_ref[h]
-    m_new = jnp.maximum(m_old, jnp.max(s, axis=1, keepdims=True))
-    alpha = jnp.exp2(m_old - m_new)
-    p = jnp.exp2(s - wide(m_new, s.shape[1] // HEAD)).astype(BF16)
-    acc_ref[h] = acc_ref[h] * wide(alpha, 2) + plain(p, vv[...])
-    m_ref[h] = m_new
-
-
-def attend_set(me, core, key_ys, c, q_ref, blocks, kk, vv, m_ref, acc_ref):
+def attend_heads(c, q_ref, kk, vv, m_ref, acc_ref):
+    def scores(h):
+        return cross(q_ref[:, h * HEAD : (h + 1) * HEAD], kk[...])
+
+    s = scores(0)
+    for h in range(HEADS):
+        later = scores(h + 1) if h + 1 < HEADS else None
+        s = s * c
+        m_old = m_ref[h]
+        m_new = jnp.maximum(m_old, jnp.max(s, axis=1, keepdims=True))
+        alpha = jnp.exp2(m_old - m_new)
+        p = jnp.exp2(s - wide(m_new, s.shape[1] // HEAD)).astype(BF16)
+        m_ref[h] = m_new
+        acc_ref[h] = acc_ref[h] * wide(alpha, 2) + plain(p, vv[...])
+        s = later
+
+
+def shown_slots(me, core, key_ys):
     shown = []
     for key_y in key_ys:
         shown += seen(me, core, key_y)
-    total = functools.reduce(lambda a, b: a + b, shown)
+    return shown, functools.reduce(lambda a, b: a + b, shown)
+
+
+def attend_set(me, core, key_ys, c, q_ref, blocks, kk, vv, m_ref, acc_ref):
+    shown, total = shown_slots(me, core, key_ys)
 
     @pl.when(total > 0)
     def _():
         prepare(blocks, shown, kk, vv)
-        for h in range(HEADS):
-            update(c, q_ref[:, h * HEAD : (h + 1) * HEAD], kk, vv, m_ref, acc_ref, h)
+        attend_heads(c, q_ref, kk, vv, m_ref, acc_ref)
+
+
+def attend_both(me, key_ys, c, sets, blocks, kk, vv):
+    core = me % NC
+    for i, (q_ref, m_ref, acc_ref) in enumerate(sets):
+        shown, total = shown_slots(me, 1 - core if i else core, key_ys)
+        fresh = total > 0
+        if i:
+            fresh = jnp.logical_and(fresh, me // NC == 0)
+
+        @pl.when(fresh)
+        def _():
+            prepare(blocks, shown, kk, vv)
+
+        @pl.when(total > 0)
+        def _():
+            attend_heads(c, q_ref, kk, vv, m_ref, acc_ref)
 
 
 def local_kernel(c_ref, q, k, v, m, a, lv):
@@ -130,7 +157,6 @@
 def ring_kernel(step, me_ref, c_ref, q0, q1, fwd, bwd, m0i, a0i, m1i, a1i, m0, a0, m1, a1, blocks, kk, vv):
     me = me_ref[0]
     c = c_ref[0]
-    core = me % NC
     y = (me // NC) % NY
     m0[...] = m0i[...]
     a0[...] = a0i[...]
@@ -139,8 +165,7 @@
     blocks[0:MSG, :] = fwd[...]
     blocks[MSG : 2 * MSG, :] = bwd[...]
     key_ys = [(y + NY - step) % NY, (y + step) % NY]
-    attend_set(me, core, key_ys, c, q0, blocks, kk, vv, m0, a0)
-    attend_set(me, 1 - core, key_ys, c, q1, blocks, kk, vv, m1, a1)
+    attend_both(me, key_ys, c, ((q0, m0, a0), (q1, m1, a1)), blocks, kk, vv)
 
 
 def last_kernel(other, me_ref, c_ref, q, blk, mi, ai, *rest):
@@ -195,41 +220,30 @@
         out[...] = project(att, w, half, (x + k) % NX, out.shape[1])
 
 
-def sum_kernel(parts, *refs):
+def sum_kernel(parts, out):
     total = parts[0].astype(F32)
     for j in range(1, NX):
         total += parts[j].astype(F32)
-    out, *same = refs[NX - 1 :]
     out[...] = total.astype(BF16)
-    for source, target in zip(refs, same):
-        target[...] = source[...]
-
-
-def add_kernel(*refs):
-    *parts, out = refs
+
+
+def choose_kernel(me_ref, here, there, out):
+    last = me_ref[0] == NZ * NY * NC - 1
+
+    @pl.when(last)
+    def _():
+        out[...] = there[...]
+
+    @pl.when(jnp.logical_not(last))
+    def _():
+        out[...] = here[...]
+
+
+def square_kernel(*refs):
+    *parts, out, squares = refs
     total = parts[0][...].astype(F32)
     for part in parts[1:]:
         total += part[...].astype(F32)
-    out[...] = total
-
-
-def choose_kernel(me_ref, here, there, out):
-    last = me_ref[0] == NZ * NY * NC - 1
-
-    @pl.when(last)
-    def _():
-        out[...] = there[...]
-
-    @pl.when(jnp.logical_not(last))
-    def _():
-        out[...] = here[...]
-
-
-def square_kernel(part, *refs):
-    *parts, out, squares = refs
-    total = part[...]
-    for other in parts:
-        total += other[...].astype(F32)
     out[...] = total
     ones = jnp.ones((8, total.shape[1]), F32)
     sums = lax.dot_general(
@@ -396,38 +410,30 @@
         cost_estimate=pl.CostEstimate(flops=1 << 31, bytes_accessed=2 << 20, transcendentals=0),
         name="project_own_half",
     )(tp_s, att, out_weight)
-    there, *parts = pl.pallas_call(
+    parts = [here[0]] + [
+        lax.ppermute(here[k], "tp", [(i, i // NX * NX + (i + k) % NX) for i in range(NX * NH)])
+        for k in range(1, NX)
+    ]
+    there = pl.pallas_call(
         sum_kernel,
-        out_shape=[block_shape] * NX,
-        in_specs=[VMEM] * NX,
-        out_specs=[VMEM] * NX,
+        out_shape=block_shape,
+        in_specs=[VMEM],
+        out_specs=VMEM,
         compiler_params=params(),
         name="sum_other_half",
-    )(there, *here[1:])
-    parts = [
-        lax.ppermute(part, "tp", [(i, i // NX * NX + (i + k) % NX) for i in range(NX * NH)])
-        for k, part in enumerate(parts, 1)
-    ]
-    part = pl.pallas_call(
-        add_kernel,
-        out_shape=jax.ShapeDtypeStruct((TOK, wide_cols), F32),
-        in_specs=[VMEM] * 2,
-        out_specs=VMEM,
-        compiler_params=params(),
-        cost_estimate=pl.CostEstimate(flops=1 << 33, bytes_accessed=1 << 20, transcendentals=0),
-        name="add_crossed",
-    )(here[0], lax.ppermute(there, "tp", swap))
+    )(there)
+    parts.append(lax.ppermute(there, "tp", swap))
     projected, squares = pl.pallas_call(
         square_kernel,
         out_shape=[
             jax.ShapeDtypeStruct((TOK, wide_cols), F32),
             jax.ShapeDtypeStruct((NX * NH, 8, TOK), F32),
         ],
-        in_specs=[VMEM] * NX,
+        in_specs=[VMEM] * (NX + 1),
         out_specs=[VMEM] * 2,
         compiler_params=params(),
         name="sum_and_square",
-    )(part, *parts)
+    )(*parts)
     squares = lax.all_to_all(squares, "tp", 0, 0)
     return pl.pallas_call(
         functools.partial(norm_kernel, out_weight.shape[1]),

time: 135 us -> 131 us (0.970)
  waiting for transfers between devices: 29.2 us -> 20.4 us
  blocking collectives: 14 us -> 17.3 us
  starting transfers between devices: 62.7 us -> 65.4 us
  Pallas kernels: 22.7 us -> 21.3 us
    all_to_all x1, waiting for transfers between devices: 12.8 us -> 1.69 us  [shards(): there = lax.all_to_all(there, 'tp', 0, 0, axis_index_groups=rows)]
    all_to_all x1, blocking collectives: 14 us -> 17.3 us  [shards(): squares = lax.all_to_all(squares, 'tp', 0, 0)]
    ppermute x4, starting transfers between devices: 17.2 us -> 20.1 us  [the longest x3 11.9 us: shards(): lax.ppermute(here[k], 'tp', [(i, i // NX * NX + (i + k) % NX) for i in ra...]
    ppermute x4, waiting for transfers between devices: 9.52 us -> 11 us  [the longest x1 8.85 us: shards(): parts.append(lax.ppermute(there, 'tp', swap))]
  transfers between devices with their start and end apart: 17 -> 17, of which waited for: 7 -> 7; matrix products, arithmetic and copies ran while one was open for 1% -> 1% of each run, Pallas kernels for 13% -> 12%
where the time goes in v7:
time: 131 us; the launch traced here: 130 us
  starting transfers between devices  65.4 us (50%)
  Pallas kernels  21.3 us (16%)
  waiting for transfers between devices  20.4 us (16%)
  blocking collectives  17.3 us (13%)
  local copies, waits for them, and re-layouts  4.2 us (3%)
  between operations  1.68 us (1%)
    all_to_all x1, blocking collectives, shards(): squares = lax.all_to_all(squares, 'tp', 0, 0)  17.3 us
    all_to_all x1, starting transfers between devices, shards(): lax.all_to_all(jnp.broadcast_to(own, (NZ, SLOT, HEAD)), 'seq', 0, 0, axis...  12.6 us
    ppermute x3, starting transfers between devices, shards(): lax.ppermute(here[k], 'tp', [(i, i // NX * NX + (i + k) % NX) for i in ra...  11.9 us
    pallas_call x3, Pallas kernels, shards(): pl.pallas_call(functools.partial(ring_kernel, step), out_shape=state_shap...  11.2 us
    ppermute x2, starting transfers between devices, shards(): bwd.append(lax.ppermute(bwd[-1], 'seq', y_perm(-1)))  10.3 us
    ppermute x1, waiting for transfers between devices, shards(): parts.append(lax.ppermute(there, 'tp', swap))  8.85 us
    ppermute x1, starting transfers between devices, shards(): parts.append(lax.ppermute(there, 'tp', swap))  8.22 us
    ppermute x1, starting transfers between devices, shards(): bwd = [lax.ppermute(block, 'seq', y_perm(-1))]  5.13 us
  transfers between devices with their start and end apart: 17, of which 7 were waited for; matrix products, arithmetic and copies ran while one was open for 1% of the time, Pallas kernels for 12%

profile of v7, /device:TPU:64, one launch (start us, length us, event | category | flops | bytes accessed | tf_op | source)
XLA Modules:
  0.0 130.3 jit_solution(17455042944419228717)
XLA Ops:
  2.9 12.6 %all-to-all-start = ((bf16[4,256,128]{2,1,0:T(8,128)(2,1)}), bf16[4,256,128]{2,1,0:T(8,128)(2,1)S(1)}, u32[]{:S(2)}, u32[]{:S(2)}) async-start(bf16[4,256,128]{2,1,0:T(8,128)(2,1)} %broadcast_in_dim.3), calls=%async_computation | async-start | bytes 524288 | tf_op jit(solution)/shard_map/all_to_all | solution.py:296
  19.1 2.7 %all-to-all-done = bf16[4,256,128]{2,1,0:T(8,128)(2,1)S(1)} async-done(((bf16[4,256,128]{2,1,0:T(8,128)(2,1)}), bf16[4,256,128]{2,1,0:T(8,128)(2,1)S(1)}, u32[]{:S(2)}, u32[]{:S(2)}) %all-to-all-start) | async-done | bytes 262176 | tf_op jit(solution)/shard_map/all_to_all | solution.py:296
  21.8 1.9 %collective-permute-start.2 = (bf16[1024,128]{1,0:T(8,128)(2,1)S(1)}, bf16[1024,128]{1,0:T(8,128)(2,1)S(1)}, u32[]{:S(2)}, u32[]{:S(2)}) collective-permute-start(bf16[1024,128]{1,0:T(8,128)(2,1)S(1)} %pad_maximum_fusion.blk), channel_id=1, source_target_pairs={{0,16},{8,24},{16,32},{24,40},{32,48},{40,56},{48,64},{56,72},{64,... | collective-permute-start | bytes 786440 | tf_op jit(solution)/shard_map/ppermute | solution.py:319
  23.8 5.1 %collective-permute-start.5 = (bf16[1024,128]{1,0:T(8,128)(2,1)S(1)}, bf16[1024,128]{1,0:T(8,128)(2,1)S(1)}, u32[]{:S(2)}, u32[]{:S(2)}) collective-permute-start(bf16[1024,128]{1,0:T(8,128)(2,1)S(1)} %pad_maximum_fusion.blk), channel_id=1, source_target_pairs={{0,112},{8,120},{16,0},{24,8},{32,16},{40,24},{48,32},{56,40},{64,... | collective-permute-start | bytes 786440 | tf_op jit(solution)/shard_map/ppermute | solution.py:320
  29.6 2.2 %attend_own_chip.1 = (f32[4,256,128]{2,1,0:T(8,128)S(1)}, f32[4,256,256]{2,1,0:T(8,128)S(1)}, f32[4,256,128]{2,1,0:T(8,128)S(1)}, f32[4,256,256]{2,1,0:T(8,128)S(1)}) custom-call(s32[1]{0:T(128)} %bitcast.1.me_ref, f32[1]{0:T(128)S(6)} %mul.9.c_ref, bf16[256,512]{1,0:T(8,128)(2,1)S(1)} %copy-done.5, ...), custom_call_target="tpu_custom_call", output_to_operand_aliasing={{0}: (5, {}), {1}: (6, {})} | custom-call | flops 2684354560 | bytes 4194304 | tf_op jit(solution)/shard_map/attend_own_chip/pallas_call | solution.py:338
  31.8 1.9 %collective-permute-start.3 = (bf16[1024,128]{1,0:T(8,128)(2,1)S(1)}, bf16[1024,128]{1,0:T(8,128)(2,1)S(1)}, u32[]{:S(2)}, u32[]{:S(2)}) collective-permute-start(bf16[1024,128]{1,0:T(8,128)(2,1)S(1)} %collective-permute-done.2.fwd), channel_id=1, source_target_pairs={{0,16},{8,24},{16,32},{24,40},{32,48},{40,56},{48,64},{56,72},{64,... | collective-permute-start | bytes 786440 | tf_op jit(solution)/shard_map/ppermute | solution.py:322
  33.8 5.1 %collective-permute-start.6 = (bf16[1024,128]{1,0:T(8,128)(2,1)S(1)}, bf16[1024,128]{1,0:T(8,128)(2,1)S(1)}, u32[]{:S(2)}, u32[]{:S(2)}) collective-permute-start(bf16[1024,128]{1,0:T(8,128)(2,1)S(1)} %collective-permute-done.5.bwd), channel_id=1, source_target_pairs={{0,112},{8,120},{16,0},{24,8},{32,16},{40,24},{48,32},{56,40},{64,... | collective-permute-start | bytes 786440 | tf_op jit(solution)/shard_map/ppermute | solution.py:323
  38.9 3.7 %attend_ring.3 = (f32[4,256,128]{2,1,0:T(8,128)S(1)}, f32[4,256,256]{2,1,0:T(8,128)S(1)}, f32[4,256,128]{2,1,0:T(8,128)S(1)}, f32[4,256,256]{2,1,0:T(8,128)S(1)}) custom-call(s32[1]{0:T(128)} %bitcast.1.me_ref, f32[1]{0:T(128)S(6)} %mul.9.c_ref, ...), custom_call_target="tpu_custom_call", output_to_operand_aliasing={{0}: (6, {}), {1}: (7, {}), {2}: (8, {}), {3}: (9, {})} | custom-call | flops 5368709120 | bytes 4194304 | tf_op jit(solution)/shard_map/attend_ring/pallas_call | solution.py:350
  44.5 5.1 %collective-permute-start.7 = (bf16[1024,128]{1,0:T(8,128)(2,1)S(1)}, bf16[1024,128]{1,0:T(8,128)(2,1)S(1)}, u32[]{:S(2)}, u32[]{:S(2)}) collective-permute-start(bf16[1024,128]{1,0:T(8,128)(2,1)S(1)} %collective-permute-done.6.bwd), channel_id=1, source_target_pairs={{0,112},{8,120},{16,0},{24,8},{32,16},{40,24},{48,32},{56,40},{64,... | collective-permute-start | bytes 786440 | tf_op jit(solution)/shard_map/ppermute | solution.py:323
  49.7 3.7 %attend_ring.4 = (f32[4,256,128]{2,1,0:T(8,128)S(1)}, f32[4,256,256]{2,1,0:T(8,128)S(1)}, f32[4,256,128]{2,1,0:T(8,128)S(1)}, f32[4,256,256]{2,1,0:T(8,128)S(1)}) custom-call(s32[1]{0:T(128)} %bitcast.1.me_ref, f32[1]{0:T(128)S(6)} %mul.9.c_ref, ...), custom_call_target="tpu_custom_call", output_to_operand_aliasing={{0}: (6, {}), {1}: (7, {}), {2}: (8, {}), {3}: (9, {})} | custom-call | flops 5368709120 | bytes 4194304 | tf_op jit(solution)/shard_map/attend_ring/pallas_call | solution.py:350
  53.6 1.9 %collective-permute-start.8 = (bf16[1024,128]{1,0:T(8,128)(2,1)S(1)}, bf16[1024,128]{1,0:T(8,128)(2,1)S(1)}, u32[]{:S(2)}, u32[]{:S(2)}) collective-permute-start(bf16[1024,128]{1,0:T(8,128)(2,1)S(1)} %broadcast_select_fusion), channel_id=1, source_target_pairs={{0,16},{8,120},{16,32},{24,8},{32,48},{40,24},{48,64},{56,40},{64,... | collective-permute-start | bytes 786440 | tf_op jit(solution)/shard_map/ppermute | solution.py:325
  55.5 3.9 %attend_ring.5 = (f32[4,256,128]{2,1,0:T(8,128)S(1)}, f32[4,256,256]{2,1,0:T(8,128)S(1)}, f32[4,256,128]{2,1,0:T(8,128)S(1)}, f32[4,256,256]{2,1,0:T(8,128)S(1)}) custom-call(s32[1]{0:T(128)} %bitcast.1.me_ref, f32[1]{0:T(128)S(6)} %mul.9.c_ref, ...), custom_call_target="tpu_custom_call", output_to_operand_aliasing={{0}: (6, {}), {1}: (7, {}), {2}: (8, {}), {3}: (9, {})} | custom-call | flops 5368709120 | bytes 4194304 | tf_op jit(solution)/shard_map/attend_ring/pallas_call | solution.py:350
  59.4 4.1 %collective-permute-done.8.blk = bf16[1024,128]{1,0:T(8,128)(2,1)S(1)} collective-permute-done((bf16[1024,128]{1,0:T(8,128)(2,1)S(1)}, bf16[1024,128]{1,0:T(8,128)(2,1)S(1)}, u32[]{:S(2)}, u32[]{:S(2)}) %collective-permute-start.8) | collective-permute-done | bytes 262176 | tf_op jit(solution)/shard_map/ppermute | solution.py:325
  65.0 1.9 %collective-permute-start.10 = (bf16[4,256,256]{2,1,0:T(8,128)(2,1)S(1)}, bf16[4,256,256]{2,1,0:T(8,128)(2,1)S(1)}, u32[]{:S(2)}, u32[]{:S(2)}) collective-permute-start(bf16[4,256,256]{2,1,0:T(8,128)(2,1)S(1)} %get-tuple-element.54), channel_id=1, source_target_pairs={{0,8},{8,0},{16,24},{24,16},{32,40},{40,32},{48,56},{56,48},{64,72... | collective-permute-start | bytes 1572872 | tf_op jit(solution)/shard_map/ppermute | solution.py:373
  69.1 2.1 %merge_project.1 = (bf16[256,512]{1,0:T(8,128)(2,1)S(1)}, bf16[4,256,512]{2,1,0:T(8,128)(2,1)}) custom-call(s32[1]{0:T(128)} %bitcast.tp_ref, f32[4,256,128]{2,1,0:T(8,128)S(1)} %get-tuple-element.50.m, f32[4,256,256]{2,1,0:T(8,128)S(1)} %get-tuple-element.51.a, bf16[4,256,256]{2,1,0:T(8,128)(2,1)S(1)} %collective-permute-done.10.got, ...), custom_call_target="tpu_custom_call" | custom-call | flops 2147483648 | bytes 8388608 | tf_op jit(solution)/shard_map/merge_project/pallas_call | solution.py:389
  71.2 4.3 %all-to-all-start.1 = ((bf16[4,256,512]{2,1,0:T(8,128)(2,1)}), bf16[4,256,512]{2,1,0:T(8,128)(2,1)S(1)}, u32[]{:S(2)}, u32[]{:S(2)}) async-start(bf16[4,256,512]{2,1,0:T(8,128)(2,1)} %get-tuple-element.60), calls=%async_computation.1 | async-start | bytes 2097152 | tf_op jit(solution)/shard_map/all_to_all | solution.py:403
  75.5 2.2 %copy-done.4 = bf16[512,4096]{1,0:T(8,128)(2,1)S(1)} copy-done((bf16[512,4096]{1,0:T(8,128)(2,1)S(1)}, bf16[512,4096]{1,0:T(8,128)(2,1)}, u32[]{:S(2)}) %copy-start.4) | copy-done | bytes 4194328
  78.4 3.9 %collective-permute-start.11 = (bf16[256,512]{1,0:T(8,128)(2,1)S(1)}, bf16[256,512]{1,0:T(8,128)(2,1)S(1)}, u32[]{:S(2)}, u32[]{:S(2)}) collective-permute-start(bf16[256,512]{1,0:T(8,128)(2,1)S(1)} %get-tuple-element.57), channel_id=1, source_target_pairs={{0,1},{1,2},{2,3},{3,0},{4,5},{5,6},{6,7},{7,4},{8,9},{9,10},{10,1... | collective-permute-start | bytes 786440 | tf_op jit(solution)/shard_map/ppermute | solution.py:414
  82.4 4.6 %collective-permute-start.12 = (bf16[256,512]{1,0:T(8,128)(2,1)S(1)}, bf16[256,512]{1,0:T(8,128)(2,1)S(1)}, u32[]{:S(2)}, u32[]{:S(2)}) collective-permute-start(bf16[256,512]{1,0:T(8,128)(2,1)S(1)} %get-tuple-element.58), channel_id=1, source_target_pairs={{0,2},{1,3},{2,0},{3,1},{4,6},{5,7},{6,4},{7,5},{8,10},{9,11},{10,... | collective-permute-start | bytes 786440 | tf_op jit(solution)/shard_map/ppermute | solution.py:414
  87.0 3.4 %collective-permute-start.13 = (bf16[256,512]{1,0:T(8,128)(2,1)S(1)}, bf16[256,512]{1,0:T(8,128)(2,1)S(1)}, u32[]{:S(2)}, u32[]{:S(2)}) collective-permute-start(bf16[256,512]{1,0:T(8,128)(2,1)S(1)} %get-tuple-element.59), channel_id=1, source_target_pairs={{0,3},{1,0},{2,1},{3,2},{4,7},{5,4},{6,5},{7,6},{8,11},{9,8},{10,9... | collective-permute-start | bytes 786440 | tf_op jit(solution)/shard_map/ppermute | solution.py:414
  92.2 8.2 %collective-permute-start.14 = (bf16[256,512]{1,0:T(8,128)(2,1)S(1)}, bf16[256,512]{1,0:T(8,128)(2,1)S(1)}, u32[]{:S(2)}, u32[]{:S(2)}) collective-permute-start(bf16[256,512]{1,0:T(8,128)(2,1)S(1)} %sum_other_half.1), channel_id=1, source_target_pairs={{0,4},{1,5},{2,6},{3,7},{4,0},{5,1},{6,2},{7,3},{8,12},{9,13},{10,... | collective-permute-start | bytes 786440 | tf_op jit(solution)/shard_map/ppermute | solution.py:425
  100.4 2.2 %collective-permute-done.12.refs_2_ = bf16[256,512]{1,0:T(8,128)(2,1)S(1)} collective-permute-done((bf16[256,512]{1,0:T(8,128)(2,1)S(1)}, bf16[256,512]{1,0:T(8,128)(2,1)S(1)}, u32[]{:S(2)}, u32[]{:S(2)}) %collective-permute-start.12) | collective-permute-done | bytes 262176 | tf_op jit(solution)/shard_map/ppermute | solution.py:414
  102.5 8.8 %collective-permute-done.14.refs_4_ = bf16[256,512]{1,0:T(8,128)(2,1)S(1)} collective-permute-done((bf16[256,512]{1,0:T(8,128)(2,1)S(1)}, bf16[256,512]{1,0:T(8,128)(2,1)S(1)}, u32[]{:S(2)}, u32[]{:S(2)}) %collective-permute-start.14) | collective-permute-done | bytes 262176 | tf_op jit(solution)/shard_map/ppermute | solution.py:425
  112.0 17.3 %all_to_all.15.squares = f32[8,8,256]{2,1,0:T(8,128)S(1)} all-to-all(f32[8,8,256]{2,1,0:T(8,128)S(1)} %get-tuple-element.62), channel_id=1, replica_groups=mesh['seq'=64,'tp'=8] {'tp'}, dimensions={0} | all-to-all | bytes 131072 | tf_op jit(solution)/shard_map/all_to_all | solution.py:437
  (44 shorter events, 15.7 us)
Async XLA Ops:
  1.5 14.1 %collective-permute-start = (bf16[256,128]{1,0:T(8,128)(2,1)S(1)}, bf16[256,128]{1,0:T(8,128)(2,1)S(1)}, u32[]{:S(2)}, u32[]{:S(2)}) collective-permute-start(bf16[256,128]{1,0:T(8,128)(2,1)S(1)} %pad_maximum_fusion.2.here), channel_id=1, source_target_pairs={{0,504},{1,505},{2,506},{3,507},{4,508},{5,509},{6,510},{7,511}} | collective-permute-start | bytes 196616 | tf_op jit(solution)/shard_map/ppermute | solution.py:301
  2.9 18.9 %all-to-all-start = ((bf16[4,256,128]{2,1,0:T(8,128)(2,1)}), bf16[4,256,128]{2,1,0:T(8,128)(2,1)S(1)}, u32[]{:S(2)}, u32[]{:S(2)}) async-start(bf16[4,256,128]{2,1,0:T(8,128)(2,1)} %broadcast_in_dim.3), calls=%async_computation | async-start | bytes 524288 | tf_op jit(solution)/shard_map/all_to_all | solution.py:296
  15.6 1.0 copy-start.5
  15.6 13.4 %copy-start = (bf16[256,128]{1,0:T(8,128)(2,1)S(1)}, bf16[256,128]{1,0:T(8,128)(2,1)}, u32[]{:S(2)}) copy-start(bf16[256,128]{1,0:T(8,128)(2,1)} %k.1) | copy-start | bytes 196612
  15.6 13.4 %copy-start.1 = (bf16[256,128]{1,0:T(8,128)(2,1)S(1)}, bf16[256,128]{1,0:T(8,128)(2,1)}, u32[]{:S(2)}) copy-start(bf16[256,128]{1,0:T(8,128)(2,1)} %v.1) | copy-start | bytes 196612
  15.6 3.5 %collective-permute-start.1 = (bf16[256,128]{1,0:T(8,128)(2,1)S(1)}, bf16[256,128]{1,0:T(8,128)(2,1)S(1)}, u32[]{:S(2)}, u32[]{:S(2)}) collective-permute-start(bf16[256,128]{1,0:T(8,128)(2,1)S(1)} %choose_anchor.1), channel_id=1, source_target_pairs={{0,248},{504,376},{1,249},{505,377},{2,250},{506,378},{3,251},{507... | collective-permute-start | bytes 196616 | tf_op jit(solution)/shard_map/ppermute | solution.py:311
  16.5 13.1 %collective-permute-start.9 = (bf16[256,512]{1,0:T(8,128)(2,1)S(1)}, bf16[256,512]{1,0:T(8,128)(2,1)S(1)}, u32[]{:S(2)}, u32[]{:S(2)}) collective-permute-start(bf16[256,512]{1,0:T(8,128)(2,1)S(1)} %copy-done.5), channel_id=1, source_target_pairs={{0,8},{8,0},{16,24},{24,16},{32,40},{40,32},{48,56},{56,48},{64,72... | collective-permute-start | bytes 786440 | tf_op jit(solution)/shard_map/ppermute | solution.py:312
  21.8 10.0 %collective-permute-start.2 = (bf16[1024,128]{1,0:T(8,128)(2,1)S(1)}, bf16[1024,128]{1,0:T(8,128)(2,1)S(1)}, u32[]{:S(2)}, u32[]{:S(2)}) collective-permute-start(bf16[1024,128]{1,0:T(8,128)(2,1)S(1)} %pad_maximum_fusion.blk), channel_id=1, source_target_pairs={{0,16},{8,24},{16,32},{24,40},{32,48},{40,56},{48,64},{56,72},{64,... | collective-permute-start | bytes 786440 | tf_op jit(solution)/shard_map/ppermute | solution.py:319
  23.8 10.0 %collective-permute-start.5 = (bf16[1024,128]{1,0:T(8,128)(2,1)S(1)}, bf16[1024,128]{1,0:T(8,128)(2,1)S(1)}, u32[]{:S(2)}, u32[]{:S(2)}) collective-permute-start(bf16[1024,128]{1,0:T(8,128)(2,1)S(1)} %pad_maximum_fusion.blk), channel_id=1, source_target_pairs={{0,112},{8,120},{16,0},{24,8},{32,16},{40,24},{48,32},{56,40},{64,... | collective-permute-start | bytes 786440 | tf_op jit(solution)/shard_map/ppermute | solution.py:320
  31.8 10.8 %collective-permute-start.3 = (bf16[1024,128]{1,0:T(8,128)(2,1)S(1)}, bf16[1024,128]{1,0:T(8,128)(2,1)S(1)}, u32[]{:S(2)}, u32[]{:S(2)}) collective-permute-start(bf16[1024,128]{1,0:T(8,128)(2,1)S(1)} %collective-permute-done.2.fwd), channel_id=1, source_target_pairs={{0,16},{8,24},{16,32},{24,40},{32,48},{40,56},{48,64},{56,72},{64,... | collective-permute-start | bytes 786440 | tf_op jit(solution)/shard_map/ppermute | solution.py:322
  33.8 10.8 %collective-permute-start.6 = (bf16[1024,128]{1,0:T(8,128)(2,1)S(1)}, bf16[1024,128]{1,0:T(8,128)(2,1)S(1)}, u32[]{:S(2)}, u32[]{:S(2)}) collective-permute-start(bf16[1024,128]{1,0:T(8,128)(2,1)S(1)} %collective-permute-done.5.bwd), channel_id=1, source_target_pairs={{0,112},{8,120},{16,0},{24,8},{32,16},{40,24},{48,32},{56,40},{64,... | collective-permute-start | bytes 786440 | tf_op jit(solution)/shard_map/ppermute | solution.py:323
  42.6 10.8 %collective-permute-start.4 = (bf16[1024,128]{1,0:T(8,128)(2,1)S(1)}, bf16[1024,128]{1,0:T(8,128)(2,1)S(1)}, u32[]{:S(2)}, u32[]{:S(2)}) collective-permute-start(bf16[1024,128]{1,0:T(8,128)(2,1)S(1)} %collective-permute-done.3.fwd), channel_id=1, source_target_pairs={{0,16},{8,24},{16,32},{24,40},{32,48},{40,56},{48,64},{56,72},{64,... | collective-permute-start | bytes 786440 | tf_op jit(solution)/shard_map/ppermute | solution.py:322
  44.5 9.0 %collective-permute-start.7 = (bf16[1024,128]{1,0:T(8,128)(2,1)S(1)}, bf16[1024,128]{1,0:T(8,128)(2,1)S(1)}, u32[]{:S(2)}, u32[]{:S(2)}) collective-permute-start(bf16[1024,128]{1,0:T(8,128)(2,1)S(1)} %collective-permute-done.6.bwd), channel_id=1, source_target_pairs={{0,112},{8,120},{16,0},{24,8},{32,16},{40,24},{48,32},{56,40},{64,... | collective-permute-start | bytes 786440 | tf_op jit(solution)/shard_map/ppermute | solution.py:323
  53.6 9.9 %collective-permute-start.8 = (bf16[1024,128]{1,0:T(8,128)(2,1)S(1)}, bf16[1024,128]{1,0:T(8,128)(2,1)S(1)}, u32[]{:S(2)}, u32[]{:S(2)}) collective-permute-start(bf16[1024,128]{1,0:T(8,128)(2,1)S(1)} %broadcast_select_fusion), channel_id=1, source_target_pairs={{0,16},{8,120},{16,32},{24,8},{32,48},{40,24},{48,64},{56,40},{64,... | collective-permute-start | bytes 786440 | tf_op jit(solution)/shard_map/ppermute | solution.py:325
  65.0 3.8 %collective-permute-start.10 = (bf16[4,256,256]{2,1,0:T(8,128)(2,1)S(1)}, bf16[4,256,256]{2,1,0:T(8,128)(2,1)S(1)}, u32[]{:S(2)}, u32[]{:S(2)}) collective-permute-start(bf16[4,256,256]{2,1,0:T(8,128)(2,1)S(1)} %get-tuple-element.54), channel_id=1, source_target_pairs={{0,8},{8,0},{16,24},{24,16},{32,40},{40,32},{48,56},{56,48},{64,72... | collective-permute-start | bytes 1572872 | tf_op jit(solution)/shard_map/ppermute | solution.py:373
  66.9 2.2 %copy-start.3 = (bf16[512,4096]{1,0:T(8,128)(2,1)S(1)}, bf16[512,4096]{1,0:T(8,128)(2,1)}, u32[]{:S(2)}) copy-start(bf16[512,4096]{1,0:T(8,128)(2,1)} %w.3) | copy-start | bytes 12582916
  71.2 20.8 %all-to-all-start.1 = ((bf16[4,256,512]{2,1,0:T(8,128)(2,1)}), bf16[4,256,512]{2,1,0:T(8,128)(2,1)S(1)}, u32[]{:S(2)}, u32[]{:S(2)}) async-start(bf16[4,256,512]{2,1,0:T(8,128)(2,1)} %get-tuple-element.60), calls=%async_computation.1 | async-start | bytes 2097152 | tf_op jit(solution)/shard_map/all_to_all | solution.py:403
  75.5 2.2 %copy-start.4 = (bf16[512,4096]{1,0:T(8,128)(2,1)S(1)}, bf16[512,4096]{1,0:T(8,128)(2,1)}, u32[]{:S(2)}) copy-start(bf16[512,4096]{1,0:T(8,128)(2,1)} %w.3) | copy-start | bytes 12582916
  77.7 51.6 %copy-start.2 = (f32[512]{0:T(512)S(1)}, f32[512]{0:T(512)}, u32[]{:S(2)}) copy-start(f32[512]{0:T(512)} %param.13) | copy-start | bytes 6148
  78.4 21.9 %collective-permute-start.11 = (bf16[256,512]{1,0:T(8,128)(2,1)S(1)}, bf16[256,512]{1,0:T(8,128)(2,1)S(1)}, u32[]{:S(2)}, u32[]{:S(2)}) collective-permute-start(bf16[256,512]{1,0:T(8,128)(2,1)S(1)} %get-tuple-element.57), channel_id=1, source_target_pairs={{0,1},{1,2},{2,3},{3,0},{4,5},{5,6},{6,7},{7,4},{8,9},{9,10},{10,1... | collective-permute-start | bytes 786440 | tf_op jit(solution)/shard_map/ppermute | solution.py:414
  82.4 20.2 %collective-permute-start.12 = (bf16[256,512]{1,0:T(8,128)(2,1)S(1)}, bf16[256,512]{1,0:T(8,128)(2,1)S(1)}, u32[]{:S(2)}, u32[]{:S(2)}) collective-permute-start(bf16[256,512]{1,0:T(8,128)(2,1)S(1)} %get-tuple-element.58), channel_id=1, source_target_pairs={{0,2},{1,3},{2,0},{3,1},{4,6},{5,7},{6,4},{7,5},{8,10},{9,11},{10,... | collective-permute-start | bytes 786440 | tf_op jit(solution)/shard_map/ppermute | solution.py:414
  87.0 15.6 %collective-permute-start.13 = (bf16[256,512]{1,0:T(8,128)(2,1)S(1)}, bf16[256,512]{1,0:T(8,128)(2,1)S(1)}, u32[]{:S(2)}, u32[]{:S(2)}) collective-permute-start(bf16[256,512]{1,0:T(8,128)(2,1)S(1)} %get-tuple-element.59), channel_id=1, source_target_pairs={{0,3},{1,0},{2,1},{3,2},{4,7},{5,4},{6,5},{7,6},{8,11},{9,8},{10,9... | collective-permute-start | bytes 786440 | tf_op jit(solution)/shard_map/ppermute | solution.py:414
  92.2 19.2 %collective-permute-start.14 = (bf16[256,512]{1,0:T(8,128)(2,1)S(1)}, bf16[256,512]{1,0:T(8,128)(2,1)S(1)}, u32[]{:S(2)}, u32[]{:S(2)}) collective-permute-start(bf16[256,512]{1,0:T(8,128)(2,1)S(1)} %sum_other_half.1), channel_id=1, source_target_pairs={{0,4},{1,5},{2,6},{3,7},{4,0},{5,1},{6,2},{7,3},{8,12},{9,13},{10,... | collective-permute-start | bytes 786440 | tf_op jit(solution)/shard_map/ppermute | solution.py:425

commit v8 on v7

--- a/solution.py
+++ b/solution.py
@@ -283,7 +283,7 @@
 def shards(queries, keys, values, key_head_scale, retained, out_weight, norm_gain):
     me = lax.axis_index("seq").astype(jnp.int32)
     tp = lax.axis_index("tp").astype(jnp.int32)
-    core, z = me % NC, me // (NC * NY)
+    z = me // (NC * NY)
     me_s = me.reshape(1)
     tp_s = tp.reshape(1)
     c = key_head_scale * (LOG2E / math.sqrt(HEAD))
@@ -299,6 +299,7 @@
     holders = [sid(z_, NY - 1, 1) for z_ in range(NZ)]
     anchor = jnp.concatenate([keys[:BLOCK], values[:BLOCK]], 0)
     far = lax.ppermute(anchor, "seq", [(0, holders[3])])
+    other_queries = lax.ppermute(queries, "seq", [(sid(*s), sid(s[0], s[1], 1 - s[2])) for s in PLACES])
     anchor = pl.pallas_call(
         choose_kernel,
         out_shape=jax.ShapeDtypeStruct((SLOT, HEAD), BF16),
@@ -309,7 +310,6 @@
         name="choose_anchor",
     )(me_s, anchor, far)
     near = lax.ppermute(anchor, "seq", [(0, holders[1]), (holders[3], holders[2])])
-    other_queries = lax.ppermute(queries, "seq", [(sid(*s), sid(s[0], s[1], 1 - s[2])) for s in PLACES])
     placed = jnp.where(jnp.logical_or(me == holders[1], me == holders[2]), near, anchor)
     holds = jnp.where(z == 0, me == 0, me % (NY * NC) == NY * NC - 1)
     block = jnp.concatenate(
@@ -321,8 +321,7 @@
     for _ in range(2):
         fwd.append(lax.ppermute(fwd[-1], "seq", y_perm(1)))
         bwd.append(lax.ppermute(bwd[-1], "seq", y_perm(-1)))
-    turn = [(sid(z_, y_, c_), sid(z_, y_ + (1 if c_ == 0 else -1), c_)) for z_, y_, c_ in PLACES]
-    half = lax.ppermute(jnp.where(core == 0, fwd[-1], bwd[-1]), "seq", turn)
+    half = lax.ppermute(fwd[-1], "seq", y_perm(1))
 
     state_shapes = [M_SHAPE, ACC_SHAPE, M_SHAPE, ACC_SHAPE]
     m0, a0 = pl.pallas_call(

time: 131 us -> 130 us (level)
  transfers between devices with their start and end apart: 17 -> 17, of which waited for: 7 -> 6; matrix products, arithmetic and copies ran while one was open for 1% -> 1% of each run, Pallas kernels for 12% -> 12%
where the time goes in v8:
time: 130 us
  starting transfers between devices  65.4 us (50%)
  Pallas kernels  21.3 us (16%)
  waiting for transfers between devices  19.8 us (15%)
  blocking collectives  17.3 us (13%)
  local copies, waits for them, and re-layouts  4.2 us (3%)
  between operations  1.68 us (1%)
    all_to_all x1, blocking collectives, shards(): squares = lax.all_to_all(squares, 'tp', 0, 0)  17.3 us
    all_to_all x1, starting transfers between devices, shards(): lax.all_to_all(jnp.broadcast_to(own, (NZ, SLOT, HEAD)), 'seq', 0, 0, axis...  12.6 us
    ppermute x3, starting transfers between devices, shards(): lax.ppermute(here[k], 'tp', [(i, i // NX * NX + (i + k) % NX) for i in ra...  11.9 us
    pallas_call x3, Pallas kernels, shards(): pl.pallas_call(functools.partial(ring_kernel, step), out_shape=state_shap...  11.2 us
    ppermute x2, starting transfers between devices, shards(): bwd.append(lax.ppermute(bwd[-1], 'seq', y_perm(-1)))  10.3 us
    ppermute x1, waiting for transfers between devices, shards(): parts.append(lax.ppermute(there, 'tp', swap))  8.85 us
    ppermute x1, starting transfers between devices, shards(): parts.append(lax.ppermute(there, 'tp', swap))  8.22 us
    ppermute x1, starting transfers between devices, shards(): bwd = [lax.ppermute(block, 'seq', y_perm(-1))]  5.13 us
  transfers between devices with their start and end apart: 17, of which 6 were waited for; matrix products, arithmetic and copies ran while one was open for 1% of the time, Pallas kernels for 12%

profile of v8, /device:TPU:64, one launch (start us, length us, event | category | flops | bytes accessed | tf_op | source)
XLA Modules:
  0.0 129.6 jit_solution(10392000055712208111)
XLA Ops:
  2.9 12.6 %all-to-all-start = ((bf16[4,256,128]{2,1,0:T(8,128)(2,1)}), bf16[4,256,128]{2,1,0:T(8,128)(2,1)S(1)}, u32[]{:S(2)}, u32[]{:S(2)}) async-start(bf16[4,256,128]{2,1,0:T(8,128)(2,1)} %broadcast_in_dim.3), calls=%async_computation | async-start | bytes 524288 | tf_op jit(solution)/shard_map/all_to_all | solution.py:296
  19.1 2.7 %all-to-all-done = bf16[4,256,128]{2,1,0:T(8,128)(2,1)S(1)} async-done(((bf16[4,256,128]{2,1,0:T(8,128)(2,1)}), bf16[4,256,128]{2,1,0:T(8,128)(2,1)S(1)}, u32[]{:S(2)}, u32[]{:S(2)}) %all-to-all-start) | async-done | bytes 262176 | tf_op jit(solution)/shard_map/all_to_all | solution.py:296
  21.8 1.9 %collective-permute-start.2 = (bf16[1024,128]{1,0:T(8,128)(2,1)S(1)}, bf16[1024,128]{1,0:T(8,128)(2,1)S(1)}, u32[]{:S(2)}, u32[]{:S(2)}) collective-permute-start(bf16[1024,128]{1,0:T(8,128)(2,1)S(1)} %pad_maximum_fusion.blk), channel_id=1, source_target_pairs={{0,16},{8,24},{16,32},{24,40},{32,48},{40,56},{48,64},{56,72},{64,... | collective-permute-start | bytes 786440 | tf_op jit(solution)/shard_map/ppermute | solution.py:319
  23.7 5.1 %collective-permute-start.7 = (bf16[1024,128]{1,0:T(8,128)(2,1)S(1)}, bf16[1024,128]{1,0:T(8,128)(2,1)S(1)}, u32[]{:S(2)}, u32[]{:S(2)}) collective-permute-start(bf16[1024,128]{1,0:T(8,128)(2,1)S(1)} %pad_maximum_fusion.blk), channel_id=1, source_target_pairs={{0,112},{8,120},{16,0},{24,8},{32,16},{40,24},{48,32},{56,40},{64,... | collective-permute-start | bytes 786440 | tf_op jit(solution)/shard_map/ppermute | solution.py:320
  29.5 2.2 %attend_own_chip.1 = (f32[4,256,128]{2,1,0:T(8,128)S(1)}, f32[4,256,256]{2,1,0:T(8,128)S(1)}, f32[4,256,128]{2,1,0:T(8,128)S(1)}, f32[4,256,256]{2,1,0:T(8,128)S(1)}) custom-call(s32[1]{0:T(128)} %bitcast.1.me_ref, f32[1]{0:T(128)S(6)} %mul.9.c_ref, bf16[256,512]{1,0:T(8,128)(2,1)S(1)} %copy-done.5, ...), custom_call_target="tpu_custom_call", output_to_operand_aliasing={{0}: (5, {}), {1}: (6, {})} | custom-call | flops 2684354560 | bytes 4194304 | tf_op jit(solution)/shard_map/attend_own_chip/pallas_call | solution.py:337
  31.8 1.9 %collective-permute-start.3 = (bf16[1024,128]{1,0:T(8,128)(2,1)S(1)}, bf16[1024,128]{1,0:T(8,128)(2,1)S(1)}, u32[]{:S(2)}, u32[]{:S(2)}) collective-permute-start(bf16[1024,128]{1,0:T(8,128)(2,1)S(1)} %collective-permute-done.2.fwd), channel_id=1, source_target_pairs={{0,16},{8,24},{16,32},{24,40},{32,48},{40,56},{48,64},{56,72},{64,... | collective-permute-start | bytes 786440 | tf_op jit(solution)/shard_map/ppermute | solution.py:322
  33.7 5.1 %collective-permute-start.8 = (bf16[1024,128]{1,0:T(8,128)(2,1)S(1)}, bf16[1024,128]{1,0:T(8,128)(2,1)S(1)}, u32[]{:S(2)}, u32[]{:S(2)}) collective-permute-start(bf16[1024,128]{1,0:T(8,128)(2,1)S(1)} %collective-permute-done.7.bwd), channel_id=1, source_target_pairs={{0,112},{8,120},{16,0},{24,8},{32,16},{40,24},{48,32},{56,40},{64,... | collective-permute-start | bytes 786440 | tf_op jit(solution)/shard_map/ppermute | solution.py:323
  38.9 3.7 %attend_ring.3 = (f32[4,256,128]{2,1,0:T(8,128)S(1)}, f32[4,256,256]{2,1,0:T(8,128)S(1)}, f32[4,256,128]{2,1,0:T(8,128)S(1)}, f32[4,256,256]{2,1,0:T(8,128)S(1)}) custom-call(s32[1]{0:T(128)} %bitcast.1.me_ref, f32[1]{0:T(128)S(6)} %mul.9.c_ref, ...), custom_call_target="tpu_custom_call", output_to_operand_aliasing={{0}: (6, {}), {1}: (7, {}), {2}: (8, {}), {3}: (9, {})} | custom-call | flops 5368709120 | bytes 4194304 | tf_op jit(solution)/shard_map/attend_ring/pallas_call | solution.py:349
  42.6 1.9 %collective-permute-start.4 = (bf16[1024,128]{1,0:T(8,128)(2,1)S(1)}, bf16[1024,128]{1,0:T(8,128)(2,1)S(1)}, u32[]{:S(2)}, u32[]{:S(2)}) collective-permute-start(bf16[1024,128]{1,0:T(8,128)(2,1)S(1)} %collective-permute-done.3.fwd), channel_id=1, source_target_pairs={{0,16},{8,24},{16,32},{24,40},{32,48},{40,56},{48,64},{56,72},{64,... | collective-permute-start | bytes 786440 | tf_op jit(solution)/shard_map/ppermute | solution.py:322
  44.5 5.1 %collective-permute-start.9 = (bf16[1024,128]{1,0:T(8,128)(2,1)S(1)}, bf16[1024,128]{1,0:T(8,128)(2,1)S(1)}, u32[]{:S(2)}, u32[]{:S(2)}) collective-permute-start(bf16[1024,128]{1,0:T(8,128)(2,1)S(1)} %collective-permute-done.8.bwd), channel_id=1, source_target_pairs={{0,112},{8,120},{16,0},{24,8},{32,16},{40,24},{48,32},{56,40},{64,... | collective-permute-start | bytes 786440 | tf_op jit(solution)/shard_map/ppermute | solution.py:323
  49.7 3.7 %attend_ring.4 = (f32[4,256,128]{2,1,0:T(8,128)S(1)}, f32[4,256,256]{2,1,0:T(8,128)S(1)}, f32[4,256,128]{2,1,0:T(8,128)S(1)}, f32[4,256,256]{2,1,0:T(8,128)S(1)}) custom-call(s32[1]{0:T(128)} %bitcast.1.me_ref, f32[1]{0:T(128)S(6)} %mul.9.c_ref, ...), custom_call_target="tpu_custom_call", output_to_operand_aliasing={{0}: (6, {}), {1}: (7, {}), {2}: (8, {}), {3}: (9, {})} | custom-call | flops 5368709120 | bytes 4194304 | tf_op jit(solution)/shard_map/attend_ring/pallas_call | solution.py:349
  53.4 1.9 %collective-permute-start.5 = (bf16[1024,128]{1,0:T(8,128)(2,1)S(1)}, bf16[1024,128]{1,0:T(8,128)(2,1)S(1)}, u32[]{:S(2)}, u32[]{:S(2)}) collective-permute-start(bf16[1024,128]{1,0:T(8,128)(2,1)S(1)} %collective-permute-done.4.fwd), channel_id=1, source_target_pairs={{0,16},{8,24},{16,32},{24,40},{32,48},{40,56},{48,64},{56,72},{64,... | collective-permute-start | bytes 786440 | tf_op jit(solution)/shard_map/ppermute | solution.py:324
  55.3 3.9 %attend_ring.5 = (f32[4,256,128]{2,1,0:T(8,128)S(1)}, f32[4,256,256]{2,1,0:T(8,128)S(1)}, f32[4,256,128]{2,1,0:T(8,128)S(1)}, f32[4,256,256]{2,1,0:T(8,128)S(1)}) custom-call(s32[1]{0:T(128)} %bitcast.1.me_ref, f32[1]{0:T(128)S(6)} %mul.9.c_ref, ...), custom_call_target="tpu_custom_call", output_to_operand_aliasing={{0}: (6, {}), {1}: (7, {}), {2}: (8, {}), {3}: (9, {})} | custom-call | flops 5368709120 | bytes 4194304 | tf_op jit(solution)/shard_map/attend_ring/pallas_call | solution.py:349
  59.2 3.7 %collective-permute-done.5.blk = bf16[1024,128]{1,0:T(8,128)(2,1)S(1)} collective-permute-done((bf16[1024,128]{1,0:T(8,128)(2,1)S(1)}, bf16[1024,128]{1,0:T(8,128)(2,1)S(1)}, u32[]{:S(2)}, u32[]{:S(2)}) %collective-permute-start.5) | collective-permute-done | bytes 262176 | tf_op jit(solution)/shard_map/ppermute | solution.py:324
  68.4 2.1 %merge_project.1 = (bf16[256,512]{1,0:T(8,128)(2,1)S(1)}, bf16[4,256,512]{2,1,0:T(8,128)(2,1)}) custom-call(s32[1]{0:T(128)} %bitcast.tp_ref, f32[4,256,128]{2,1,0:T(8,128)S(1)} %get-tuple-element.50.m, f32[4,256,256]{2,1,0:T(8,128)S(1)} %get-tuple-element.51.a, bf16[4,256,256]{2,1,0:T(8,128)(2,1)S(1)} %collective-permute-done.10.got, ...), custom_call_target="tpu_custom_call" | custom-call | flops 2147483648 | bytes 8388608 | tf_op jit(solution)/shard_map/merge_project/pallas_call | solution.py:388
  70.5 4.3 %all-to-all-start.1 = ((bf16[4,256,512]{2,1,0:T(8,128)(2,1)}), bf16[4,256,512]{2,1,0:T(8,128)(2,1)S(1)}, u32[]{:S(2)}, u32[]{:S(2)}) async-start(bf16[4,256,512]{2,1,0:T(8,128)(2,1)} %get-tuple-element.60), calls=%async_computation.1 | async-start | bytes 2097152 | tf_op jit(solution)/shard_map/all_to_all | solution.py:402
  74.8 2.2 %copy-done.4 = bf16[512,4096]{1,0:T(8,128)(2,1)S(1)} copy-done((bf16[512,4096]{1,0:T(8,128)(2,1)S(1)}, bf16[512,4096]{1,0:T(8,128)(2,1)}, u32[]{:S(2)}) %copy-start.4) | copy-done | bytes 4194328
  77.7 3.9 %collective-permute-start.11 = (bf16[256,512]{1,0:T(8,128)(2,1)S(1)}, bf16[256,512]{1,0:T(8,128)(2,1)S(1)}, u32[]{:S(2)}, u32[]{:S(2)}) collective-permute-start(bf16[256,512]{1,0:T(8,128)(2,1)S(1)} %get-tuple-element.57), channel_id=1, source_target_pairs={{0,1},{1,2},{2,3},{3,0},{4,5},{5,6},{6,7},{7,4},{8,9},{9,10},{10,1... | collective-permute-start | bytes 786440 | tf_op jit(solution)/shard_map/ppermute | solution.py:413
  81.7 4.6 %collective-permute-start.12 = (bf16[256,512]{1,0:T(8,128)(2,1)S(1)}, bf16[256,512]{1,0:T(8,128)(2,1)S(1)}, u32[]{:S(2)}, u32[]{:S(2)}) collective-permute-start(bf16[256,512]{1,0:T(8,128)(2,1)S(1)} %get-tuple-element.58), channel_id=1, source_target_pairs={{0,2},{1,3},{2,0},{3,1},{4,6},{5,7},{6,4},{7,5},{8,10},{9,11},{10,... | collective-permute-start | bytes 786440 | tf_op jit(solution)/shard_map/ppermute | solution.py:413
  86.3 3.4 %collective-permute-start.13 = (bf16[256,512]{1,0:T(8,128)(2,1)S(1)}, bf16[256,512]{1,0:T(8,128)(2,1)S(1)}, u32[]{:S(2)}, u32[]{:S(2)}) collective-permute-start(bf16[256,512]{1,0:T(8,128)(2,1)S(1)} %get-tuple-element.59), channel_id=1, source_target_pairs={{0,3},{1,0},{2,1},{3,2},{4,7},{5,4},{6,5},{7,6},{8,11},{9,8},{10,9... | collective-permute-start | bytes 786440 | tf_op jit(solution)/shard_map/ppermute | solution.py:413
  91.5 8.2 %collective-permute-start.14 = (bf16[256,512]{1,0:T(8,128)(2,1)S(1)}, bf16[256,512]{1,0:T(8,128)(2,1)S(1)}, u32[]{:S(2)}, u32[]{:S(2)}) collective-permute-start(bf16[256,512]{1,0:T(8,128)(2,1)S(1)} %sum_other_half.1), channel_id=1, source_target_pairs={{0,4},{1,5},{2,6},{3,7},{4,0},{5,1},{6,2},{7,3},{8,12},{9,13},{10,... | collective-permute-start | bytes 786440 | tf_op jit(solution)/shard_map/ppermute | solution.py:424
  99.7 2.2 %collective-permute-done.12.refs_2_ = bf16[256,512]{1,0:T(8,128)(2,1)S(1)} collective-permute-done((bf16[256,512]{1,0:T(8,128)(2,1)S(1)}, bf16[256,512]{1,0:T(8,128)(2,1)S(1)}, u32[]{:S(2)}, u32[]{:S(2)}) %collective-permute-start.12) | collective-permute-done | bytes 262176 | tf_op jit(solution)/shard_map/ppermute | solution.py:413
  101.9 8.8 %collective-permute-done.14.refs_4_ = bf16[256,512]{1,0:T(8,128)(2,1)S(1)} collective-permute-done((bf16[256,512]{1,0:T(8,128)(2,1)S(1)}, bf16[256,512]{1,0:T(8,128)(2,1)S(1)}, u32[]{:S(2)}, u32[]{:S(2)}) %collective-permute-start.14) | collective-permute-done | bytes 262176 | tf_op jit(solution)/shard_map/ppermute | solution.py:424
  111.3 17.3 %all_to_all.15.squares = f32[8,8,256]{2,1,0:T(8,128)S(1)} all-to-all(f32[8,8,256]{2,1,0:T(8,128)S(1)} %get-tuple-element.62), channel_id=1, replica_groups=mesh['seq'=64,'tp'=8] {'tp'}, dimensions={0} | all-to-all | bytes 131072 | tf_op jit(solution)/shard_map/all_to_all | solution.py:436
  (43 shorter events, 15.5 us)
Async XLA Ops:
  1.5 14.0 %collective-permute-start = (bf16[256,128]{1,0:T(8,128)(2,1)S(1)}, bf16[256,128]{1,0:T(8,128)(2,1)S(1)}, u32[]{:S(2)}, u32[]{:S(2)}) collective-permute-start(bf16[256,128]{1,0:T(8,128)(2,1)S(1)} %pad_maximum_fusion.2.here), channel_id=1, source_target_pairs={{0,504},{1,505},{2,506},{3,507},{4,508},{5,509},{6,510},{7,511}} | collective-permute-start | bytes 196616 | tf_op jit(solution)/shard_map/ppermute | solution.py:301
  2.9 18.8 %all-to-all-start = ((bf16[4,256,128]{2,1,0:T(8,128)(2,1)}), bf16[4,256,128]{2,1,0:T(8,128)(2,1)S(1)}, u32[]{:S(2)}, u32[]{:S(2)}) async-start(bf16[4,256,128]{2,1,0:T(8,128)(2,1)} %broadcast_in_dim.3), calls=%async_computation | async-start | bytes 524288 | tf_op jit(solution)/shard_map/all_to_all | solution.py:296
  15.5 1.0 copy-start.5
  15.5 13.4 %copy-start = (bf16[256,128]{1,0:T(8,128)(2,1)S(1)}, bf16[256,128]{1,0:T(8,128)(2,1)}, u32[]{:S(2)}) copy-start(bf16[256,128]{1,0:T(8,128)(2,1)} %k.1) | copy-start | bytes 196612
  15.5 13.4 %copy-start.1 = (bf16[256,128]{1,0:T(8,128)(2,1)S(1)}, bf16[256,128]{1,0:T(8,128)(2,1)}, u32[]{:S(2)}) copy-start(bf16[256,128]{1,0:T(8,128)(2,1)} %v.1) | copy-start | bytes 196612
  15.6 3.5 %collective-permute-start.1 = (bf16[256,128]{1,0:T(8,128)(2,1)S(1)}, bf16[256,128]{1,0:T(8,128)(2,1)S(1)}, u32[]{:S(2)}, u32[]{:S(2)}) collective-permute-start(bf16[256,128]{1,0:T(8,128)(2,1)S(1)} %choose_anchor.1), channel_id=1, source_target_pairs={{0,248},{504,376},{1,249},{505,377},{2,250},{506,378},{3,251},{507... | collective-permute-start | bytes 196616 | tf_op jit(solution)/shard_map/ppermute | solution.py:312
  16.5 13.1 %collective-permute-start.6 = (bf16[256,512]{1,0:T(8,128)(2,1)S(1)}, bf16[256,512]{1,0:T(8,128)(2,1)S(1)}, u32[]{:S(2)}, u32[]{:S(2)}) collective-permute-start(bf16[256,512]{1,0:T(8,128)(2,1)S(1)} %copy-done.5), channel_id=1, source_target_pairs={{0,8},{8,0},{16,24},{24,16},{32,40},{40,32},{48,56},{56,48},{64,72... | collective-permute-start | bytes 786440 | tf_op jit(solution)/shard_map/ppermute | solution.py:302
  21.8 10.0 %collective-permute-start.2 = (bf16[1024,128]{1,0:T(8,128)(2,1)S(1)}, bf16[1024,128]{1,0:T(8,128)(2,1)S(1)}, u32[]{:S(2)}, u32[]{:S(2)}) collective-permute-start(bf16[1024,128]{1,0:T(8,128)(2,1)S(1)} %pad_maximum_fusion.blk), channel_id=1, source_target_pairs={{0,16},{8,24},{16,32},{24,40},{32,48},{40,56},{48,64},{56,72},{64,... | collective-permute-start | bytes 786440 | tf_op jit(solution)/shard_map/ppermute | solution.py:319
  23.7 10.0 %collective-permute-start.7 = (bf16[1024,128]{1,0:T(8,128)(2,1)S(1)}, bf16[1024,128]{1,0:T(8,128)(2,1)S(1)}, u32[]{:S(2)}, u32[]{:S(2)}) collective-permute-start(bf16[1024,128]{1,0:T(8,128)(2,1)S(1)} %pad_maximum_fusion.blk), channel_id=1, source_target_pairs={{0,112},{8,120},{16,0},{24,8},{32,16},{40,24},{48,32},{56,40},{64,... | collective-permute-start | bytes 786440 | tf_op jit(solution)/shard_map/ppermute | solution.py:320
  31.8 10.8 %collective-permute-start.3 = (bf16[1024,128]{1,0:T(8,128)(2,1)S(1)}, bf16[1024,128]{1,0:T(8,128)(2,1)S(1)}, u32[]{:S(2)}, u32[]{:S(2)}) collective-permute-start(bf16[1024,128]{1,0:T(8,128)(2,1)S(1)} %collective-permute-done.2.fwd), channel_id=1, source_target_pairs={{0,16},{8,24},{16,32},{24,40},{32,48},{40,56},{48,64},{56,72},{64,... | collective-permute-start | bytes 786440 | tf_op jit(solution)/shard_map/ppermute | solution.py:322
  33.7 10.8 %collective-permute-start.8 = (bf16[1024,128]{1,0:T(8,128)(2,1)S(1)}, bf16[1024,128]{1,0:T(8,128)(2,1)S(1)}, u32[]{:S(2)}, u32[]{:S(2)}) collective-permute-start(bf16[1024,128]{1,0:T(8,128)(2,1)S(1)} %collective-permute-done.7.bwd), channel_id=1, source_target_pairs={{0,112},{8,120},{16,0},{24,8},{32,16},{40,24},{48,32},{56,40},{64,... | collective-permute-start | bytes 786440 | tf_op jit(solution)/shard_map/ppermute | solution.py:323
  42.6 10.8 %collective-permute-start.4 = (bf16[1024,128]{1,0:T(8,128)(2,1)S(1)}, bf16[1024,128]{1,0:T(8,128)(2,1)S(1)}, u32[]{:S(2)}, u32[]{:S(2)}) collective-permute-start(bf16[1024,128]{1,0:T(8,128)(2,1)S(1)} %collective-permute-done.3.fwd), channel_id=1, source_target_pairs={{0,16},{8,24},{16,32},{24,40},{32,48},{40,56},{48,64},{56,72},{64,... | collective-permute-start | bytes 786440 | tf_op jit(solution)/shard_map/ppermute | solution.py:322
  44.5 10.8 %collective-permute-start.9 = (bf16[1024,128]{1,0:T(8,128)(2,1)S(1)}, bf16[1024,128]{1,0:T(8,128)(2,1)S(1)}, u32[]{:S(2)}, u32[]{:S(2)}) collective-permute-start(bf16[1024,128]{1,0:T(8,128)(2,1)S(1)} %collective-permute-done.8.bwd), channel_id=1, source_target_pairs={{0,112},{8,120},{16,0},{24,8},{32,16},{40,24},{48,32},{56,40},{64,... | collective-permute-start | bytes 786440 | tf_op jit(solution)/shard_map/ppermute | solution.py:323
  53.4 9.5 %collective-permute-start.5 = (bf16[1024,128]{1,0:T(8,128)(2,1)S(1)}, bf16[1024,128]{1,0:T(8,128)(2,1)S(1)}, u32[]{:S(2)}, u32[]{:S(2)}) collective-permute-start(bf16[1024,128]{1,0:T(8,128)(2,1)S(1)} %collective-permute-done.4.fwd), channel_id=1, source_target_pairs={{0,16},{8,24},{16,32},{24,40},{32,48},{40,56},{48,64},{56,72},{64,... | collective-permute-start | bytes 786440 | tf_op jit(solution)/shard_map/ppermute | solution.py:324
  64.3 3.8 %collective-permute-start.10 = (bf16[4,256,256]{2,1,0:T(8,128)(2,1)S(1)}, bf16[4,256,256]{2,1,0:T(8,128)(2,1)S(1)}, u32[]{:S(2)}, u32[]{:S(2)}) collective-permute-start(bf16[4,256,256]{2,1,0:T(8,128)(2,1)S(1)} %get-tuple-element.54), channel_id=1, source_target_pairs={{0,8},{8,0},{16,24},{24,16},{32,40},{40,32},{48,56},{56,48},{64,72... | collective-permute-start | bytes 1572872 | tf_op jit(solution)/shard_map/ppermute | solution.py:372
  66.2 2.2 %copy-start.3 = (bf16[512,4096]{1,0:T(8,128)(2,1)S(1)}, bf16[512,4096]{1,0:T(8,128)(2,1)}, u32[]{:S(2)}) copy-start(bf16[512,4096]{1,0:T(8,128)(2,1)} %w.3) | copy-start | bytes 12582916
  70.5 20.8 %all-to-all-start.1 = ((bf16[4,256,512]{2,1,0:T(8,128)(2,1)}), bf16[4,256,512]{2,1,0:T(8,128)(2,1)S(1)}, u32[]{:S(2)}, u32[]{:S(2)}) async-start(bf16[4,256,512]{2,1,0:T(8,128)(2,1)} %get-tuple-element.60), calls=%async_computation.1 | async-start | bytes 2097152 | tf_op jit(solution)/shard_map/all_to_all | solution.py:402
  74.8 2.2 %copy-start.4 = (bf16[512,4096]{1,0:T(8,128)(2,1)S(1)}, bf16[512,4096]{1,0:T(8,128)(2,1)}, u32[]{:S(2)}) copy-start(bf16[512,4096]{1,0:T(8,128)(2,1)} %w.3) | copy-start | bytes 12582916
  77.0 51.6 %copy-start.2 = (f32[512]{0:T(512)S(1)}, f32[512]{0:T(512)}, u32[]{:S(2)}) copy-start(f32[512]{0:T(512)} %param.13) | copy-start | bytes 6148
  77.7 22.0 %collective-permute-start.11 = (bf16[256,512]{1,0:T(8,128)(2,1)S(1)}, bf16[256,512]{1,0:T(8,128)(2,1)S(1)}, u32[]{:S(2)}, u32[]{:S(2)}) collective-permute-start(bf16[256,512]{1,0:T(8,128)(2,1)S(1)} %get-tuple-element.57), channel_id=1, source_target_pairs={{0,1},{1,2},{2,3},{3,0},{4,5},{5,6},{6,7},{7,4},{8,9},{9,10},{10,1... | collective-permute-start | bytes 786440 | tf_op jit(solution)/shard_map/ppermute | solution.py:413
  81.7 20.2 %collective-permute-start.12 = (bf16[256,512]{1,0:T(8,128)(2,1)S(1)}, bf16[256,512]{1,0:T(8,128)(2,1)S(1)}, u32[]{:S(2)}, u32[]{:S(2)}) collective-permute-start(bf16[256,512]{1,0:T(8,128)(2,1)S(1)} %get-tuple-element.58), channel_id=1, source_target_pairs={{0,2},{1,3},{2,0},{3,1},{4,6},{5,7},{6,4},{7,5},{8,10},{9,11},{10,... | collective-permute-start | bytes 786440 | tf_op jit(solution)/shard_map/ppermute | solution.py:413
  86.3 15.6 %collective-permute-start.13 = (bf16[256,512]{1,0:T(8,128)(2,1)S(1)}, bf16[256,512]{1,0:T(8,128)(2,1)S(1)}, u32[]{:S(2)}, u32[]{:S(2)}) collective-permute-start(bf16[256,512]{1,0:T(8,128)(2,1)S(1)} %get-tuple-element.59), channel_id=1, source_target_pairs={{0,3},{1,0},{2,1},{3,2},{4,7},{5,4},{6,5},{7,6},{8,11},{9,8},{10,9... | collective-permute-start | bytes 786440 | tf_op jit(solution)/shard_map/ppermute | solution.py:413
  91.5 19.2 %collective-permute-start.14 = (bf16[256,512]{1,0:T(8,128)(2,1)S(1)}, bf16[256,512]{1,0:T(8,128)(2,1)S(1)}, u32[]{:S(2)}, u32[]{:S(2)}) collective-permute-start(bf16[256,512]{1,0:T(8,128)(2,1)S(1)} %sum_other_half.1), channel_id=1, source_target_pairs={{0,4},{1,5},{2,6},{3,7},{4,0},{5,1},{6,2},{7,3},{8,12},{9,13},{10,... | collective-permute-start | bytes 786440 | tf_op jit(solution)/shard_map/ppermute | solution.py:424

commit v9 on v8

--- a/solution.py
+++ b/solution.py
@@ -321,7 +321,10 @@
     for _ in range(2):
         fwd.append(lax.ppermute(fwd[-1], "seq", y_perm(1)))
         bwd.append(lax.ppermute(bwd[-1], "seq", y_perm(-1)))
-    half = lax.ppermute(fwd[-1], "seq", y_perm(1))
+    up_pairs = [(sid(z_, y_, c_), sid(z_, y_ + 1, c_)) for z_, y_, c_ in PLACES if y_ % 2 == 0]
+    to_odd = lax.ppermute(fwd[-1], "seq", up_pairs)
+    to_even = lax.ppermute(bwd[-1], "seq", [(b, a) for a, b in up_pairs])
+    half = jnp.where(me // NC % 2 == 0, to_even, to_odd)
 
     state_shapes = [M_SHAPE, ACC_SHAPE, M_SHAPE, ACC_SHAPE]
     m0, a0 = pl.pallas_call(

time: 130 us -> 130 us (level)
  the two profiles are of different devices: /device:TPU:64 before, /device:TPU:72 now
where the time goes in v9:
time: 130 us; the launch traced here: 129 us
  starting transfers between devices  64.4 us (50%)
  Pallas kernels  21.3 us (16%)
  waiting for transfers between devices  19.9 us (15%)
  blocking collectives  17.7 us (14%)
  local copies, waits for them, and re-layouts  4.23 us (3%)
  between operations  1.73 us (1%)
    all_to_all x1, blocking collectives, shards(): squares = lax.all_to_all(squares, 'tp', 0, 0)  17.7 us
    ppermute x3, starting transfers between devices, shards(): lax.ppermute(here[k], 'tp', [(i, i // NX * NX + (i + k) % NX) for i in ra...  11.9 us
    pallas_call x3, Pallas kernels, shards(): pl.pallas_call(functools.partial(ring_kernel, step), out_shape=state_shap...  11.2 us
    ppermute x1, waiting for transfers between devices, shards(): parts.append(lax.ppermute(there, 'tp', swap))  8.75 us
    ppermute x2, starting transfers between devices, shards(): bwd.append(lax.ppermute(bwd[-1], 'seq', y_perm(-1)))  8.38 us
    ppermute x1, starting transfers between devices, shards(): parts.append(lax.ppermute(there, 'tp', swap))  8.22 us
    ppermute x1, starting transfers between devices, shards(): bwd = [lax.ppermute(block, 'seq', y_perm(-1))]  7.22 us
    all_to_all x1, starting transfers between devices, shards(): lax.all_to_all(jnp.broadcast_to(own, (NZ, SLOT, HEAD)), 'seq', 0, 0, axis...  6.91 us
  transfers between devices with their start and end apart: 18, of which 6 were waited for; matrix products, arithmetic and copies ran while one was open for 1% of the time, Pallas kernels for 12%

profile of v9, /device:TPU:72, one launch (start us, length us, event | category | flops | bytes accessed | tf_op | source)
XLA Modules:
  0.0 129.3 jit_solution(1041182247854496617)
XLA Ops:
  3.0 6.9 %all-to-all-start = ((bf16[4,256,128]{2,1,0:T(8,128)(2,1)}), bf16[4,256,128]{2,1,0:T(8,128)(2,1)S(1)}, u32[]{:S(2)}, u32[]{:S(2)}) async-start(bf16[4,256,128]{2,1,0:T(8,128)(2,1)} %broadcast_in_dim.3), calls=%async_computation | async-start | bytes 524288 | tf_op jit(solution)/shard_map/all_to_all | solution.py:296
  13.4 3.5 %all-to-all-done = bf16[4,256,128]{2,1,0:T(8,128)(2,1)S(1)} async-done(((bf16[4,256,128]{2,1,0:T(8,128)(2,1)}), bf16[4,256,128]{2,1,0:T(8,128)(2,1)S(1)}, u32[]{:S(2)}, u32[]{:S(2)}) %all-to-all-start) | async-done | bytes 262176 | tf_op jit(solution)/shard_map/all_to_all | solution.py:296
  17.0 7.2 %collective-permute-start.2 = (bf16[1024,128]{1,0:T(8,128)(2,1)S(1)}, bf16[1024,128]{1,0:T(8,128)(2,1)S(1)}, u32[]{:S(2)}, u32[]{:S(2)}) collective-permute-start(bf16[1024,128]{1,0:T(8,128)(2,1)S(1)} %pad_maximum_fusion.blk), channel_id=1, source_target_pairs={{0,112},{8,120},{16,0},{24,8},{32,16},{40,24},{48,32},{56,40},{64,... | collective-permute-start | bytes 786440 | tf_op jit(solution)/shard_map/ppermute | solution.py:320
  24.2 1.9 %collective-permute-start.6 = (bf16[1024,128]{1,0:T(8,128)(2,1)S(1)}, bf16[1024,128]{1,0:T(8,128)(2,1)S(1)}, u32[]{:S(2)}, u32[]{:S(2)}) collective-permute-start(bf16[1024,128]{1,0:T(8,128)(2,1)S(1)} %pad_maximum_fusion.blk), channel_id=1, source_target_pairs={{0,16},{8,24},{16,32},{24,40},{32,48},{40,56},{48,64},{56,72},{64,... | collective-permute-start | bytes 786440 | tf_op jit(solution)/shard_map/ppermute | solution.py:319
  26.8 2.2 %attend_own_chip.1 = (f32[4,256,128]{2,1,0:T(8,128)S(1)}, f32[4,256,256]{2,1,0:T(8,128)S(1)}, f32[4,256,128]{2,1,0:T(8,128)S(1)}, f32[4,256,256]{2,1,0:T(8,128)S(1)}) custom-call(s32[1]{0:T(128)} %bitcast.1.me_ref, f32[1]{0:T(128)S(6)} %mul.9.c_ref, bf16[256,512]{1,0:T(8,128)(2,1)S(1)} %copy-done.5, ...), custom_call_target="tpu_custom_call", output_to_operand_aliasing={{0}: (5, {}), {1}: (6, {})} | custom-call | flops 2684354560 | bytes 4194304 | tf_op jit(solution)/shard_map/attend_own_chip/pallas_call | solution.py:340
  29.1 3.9 %collective-permute-start.3 = (bf16[1024,128]{1,0:T(8,128)(2,1)S(1)}, bf16[1024,128]{1,0:T(8,128)(2,1)S(1)}, u32[]{:S(2)}, u32[]{:S(2)}) collective-permute-start(bf16[1024,128]{1,0:T(8,128)(2,1)S(1)} %collective-permute-done.2.bwd), channel_id=1, source_target_pairs={{0,112},{8,120},{16,0},{24,8},{32,16},{40,24},{48,32},{56,40},{64,... | collective-permute-start | bytes 786440 | tf_op jit(solution)/shard_map/ppermute | solution.py:323
  33.0 1.9 %collective-permute-start.7 = (bf16[1024,128]{1,0:T(8,128)(2,1)S(1)}, bf16[1024,128]{1,0:T(8,128)(2,1)S(1)}, u32[]{:S(2)}, u32[]{:S(2)}) collective-permute-start(bf16[1024,128]{1,0:T(8,128)(2,1)S(1)} %collective-permute-done.6.fwd), channel_id=1, source_target_pairs={{0,16},{8,24},{16,32},{24,40},{32,48},{40,56},{48,64},{56,72},{64,... | collective-permute-start | bytes 786440 | tf_op jit(solution)/shard_map/ppermute | solution.py:322
  34.9 3.7 %attend_ring.3 = (f32[4,256,128]{2,1,0:T(8,128)S(1)}, f32[4,256,256]{2,1,0:T(8,128)S(1)}, f32[4,256,128]{2,1,0:T(8,128)S(1)}, f32[4,256,256]{2,1,0:T(8,128)S(1)}) custom-call(s32[1]{0:T(128)} %bitcast.1.me_ref, f32[1]{0:T(128)S(6)} %mul.9.c_ref, ...), custom_call_target="tpu_custom_call", output_to_operand_aliasing={{0}: (6, {}), {1}: (7, {}), {2}: (8, {}), {3}: (9, {})} | custom-call | flops 5368709120 | bytes 4194304 | tf_op jit(solution)/shard_map/attend_ring/pallas_call | solution.py:352
  38.6 4.5 %collective-permute-start.4 = (bf16[1024,128]{1,0:T(8,128)(2,1)S(1)}, bf16[1024,128]{1,0:T(8,128)(2,1)S(1)}, u32[]{:S(2)}, u32[]{:S(2)}) collective-permute-start(bf16[1024,128]{1,0:T(8,128)(2,1)S(1)} %collective-permute-done.3.bwd), channel_id=1, source_target_pairs={{0,112},{8,120},{16,0},{24,8},{32,16},{40,24},{48,32},{56,40},{64,... | collective-permute-start | bytes 786440 | tf_op jit(solution)/shard_map/ppermute | solution.py:323
  45.0 3.7 %attend_ring.4 = (f32[4,256,128]{2,1,0:T(8,128)S(1)}, f32[4,256,256]{2,1,0:T(8,128)S(1)}, f32[4,256,128]{2,1,0:T(8,128)S(1)}, f32[4,256,256]{2,1,0:T(8,128)S(1)}) custom-call(s32[1]{0:T(128)} %bitcast.1.me_ref, f32[1]{0:T(128)S(6)} %mul.9.c_ref, ...), custom_call_target="tpu_custom_call", output_to_operand_aliasing={{0}: (6, {}), {1}: (7, {}), {2}: (8, {}), {3}: (9, {})} | custom-call | flops 5368709120 | bytes 4194304 | tf_op jit(solution)/shard_map/attend_ring/pallas_call | solution.py:352
  48.7 5.1 %collective-permute-start.5 = (bf16[1024,128]{1,0:T(8,128)(2,1)S(1)}, bf16[1024,128]{1,0:T(8,128)(2,1)S(1)}, u32[]{:S(2)}, u32[]{:S(2)}) collective-permute-start(bf16[1024,128]{1,0:T(8,128)(2,1)S(1)} %collective-permute-done.4.bwd), channel_id=1, source_target_pairs={{16,0},{24,8},{48,32},{56,40},{80,64},{88,72},{112,96},{120,104},{... | collective-permute-start | bytes 786440 | tf_op jit(solution)/shard_map/ppermute | solution.py:326
  55.2 3.9 %attend_ring.5 = (f32[4,256,128]{2,1,0:T(8,128)S(1)}, f32[4,256,256]{2,1,0:T(8,128)S(1)}, f32[4,256,128]{2,1,0:T(8,128)S(1)}, f32[4,256,256]{2,1,0:T(8,128)S(1)}) custom-call(s32[1]{0:T(128)} %bitcast.1.me_ref, f32[1]{0:T(128)S(6)} %mul.9.c_ref, ...), custom_call_target="tpu_custom_call", output_to_operand_aliasing={{0}: (6, {}), {1}: (7, {}), {2}: (8, {}), {3}: (9, {})} | custom-call | flops 5368709120 | bytes 4194304 | tf_op jit(solution)/shard_map/attend_ring/pallas_call | solution.py:352
  59.1 3.1 %collective-permute-done.9 = bf16[1024,128]{1,0:T(8,128)(2,1)S(1)} collective-permute-done((bf16[1024,128]{1,0:T(8,128)(2,1)S(1)}, bf16[1024,128]{1,0:T(8,128)(2,1)S(1)}, u32[]{:S(2)}, u32[]{:S(2)}) %collective-permute-start.9) | collective-permute-done | bytes 262176 | tf_op jit(solution)/shard_map/ppermute | solution.py:325
  63.7 1.9 %collective-permute-start.11 = (bf16[4,256,256]{2,1,0:T(8,128)(2,1)S(1)}, bf16[4,256,256]{2,1,0:T(8,128)(2,1)S(1)}, u32[]{:S(2)}, u32[]{:S(2)}) collective-permute-start(bf16[4,256,256]{2,1,0:T(8,128)(2,1)S(1)} %get-tuple-element.54), channel_id=1, source_target_pairs={{0,8},{8,0},{16,24},{24,16},{32,40},{40,32},{48,56},{56,48},{64,72... | collective-permute-start | bytes 1572872 | tf_op jit(solution)/shard_map/ppermute | solution.py:375
  67.8 2.1 %merge_project.1 = (bf16[256,512]{1,0:T(8,128)(2,1)S(1)}, bf16[4,256,512]{2,1,0:T(8,128)(2,1)}) custom-call(s32[1]{0:T(128)} %bitcast.tp_ref, f32[4,256,128]{2,1,0:T(8,128)S(1)} %get-tuple-element.50.m, f32[4,256,256]{2,1,0:T(8,128)S(1)} %get-tuple-element.51.a, bf16[4,256,256]{2,1,0:T(8,128)(2,1)S(1)} %collective-permute-done.11.got, ...), custom_call_target="tpu_custom_call" | custom-call | flops 2147483648 | bytes 8388608 | tf_op jit(solution)/shard_map/merge_project/pallas_call | solution.py:391
  69.9 4.3 %all-to-all-start.1 = ((bf16[4,256,512]{2,1,0:T(8,128)(2,1)}), bf16[4,256,512]{2,1,0:T(8,128)(2,1)S(1)}, u32[]{:S(2)}, u32[]{:S(2)}) async-start(bf16[4,256,512]{2,1,0:T(8,128)(2,1)} %get-tuple-element.60), calls=%async_computation.1 | async-start | bytes 2097152 | tf_op jit(solution)/shard_map/all_to_all | solution.py:405
  74.2 2.2 %copy-done.4 = bf16[512,4096]{1,0:T(8,128)(2,1)S(1)} copy-done((bf16[512,4096]{1,0:T(8,128)(2,1)S(1)}, bf16[512,4096]{1,0:T(8,128)(2,1)}, u32[]{:S(2)}) %copy-start.4) | copy-done | bytes 4194328
  77.1 3.9 %collective-permute-start.12 = (bf16[256,512]{1,0:T(8,128)(2,1)S(1)}, bf16[256,512]{1,0:T(8,128)(2,1)S(1)}, u32[]{:S(2)}, u32[]{:S(2)}) collective-permute-start(bf16[256,512]{1,0:T(8,128)(2,1)S(1)} %get-tuple-element.57), channel_id=1, source_target_pairs={{0,1},{1,2},{2,3},{3,0},{4,5},{5,6},{6,7},{7,4},{8,9},{9,10},{10,1... | collective-permute-start | bytes 786440 | tf_op jit(solution)/shard_map/ppermute | solution.py:416
  81.1 4.6 %collective-permute-start.13 = (bf16[256,512]{1,0:T(8,128)(2,1)S(1)}, bf16[256,512]{1,0:T(8,128)(2,1)S(1)}, u32[]{:S(2)}, u32[]{:S(2)}) collective-permute-start(bf16[256,512]{1,0:T(8,128)(2,1)S(1)} %get-tuple-element.58), channel_id=1, source_target_pairs={{0,2},{1,3},{2,0},{3,1},{4,6},{5,7},{6,4},{7,5},{8,10},{9,11},{10,... | collective-permute-start | bytes 786440 | tf_op jit(solution)/shard_map/ppermute | solution.py:416
  85.7 3.4 %collective-permute-start.14 = (bf16[256,512]{1,0:T(8,128)(2,1)S(1)}, bf16[256,512]{1,0:T(8,128)(2,1)S(1)}, u32[]{:S(2)}, u32[]{:S(2)}) collective-permute-start(bf16[256,512]{1,0:T(8,128)(2,1)S(1)} %get-tuple-element.59), channel_id=1, source_target_pairs={{0,3},{1,0},{2,1},{3,2},{4,7},{5,4},{6,5},{7,6},{8,11},{9,8},{10,9... | collective-permute-start | bytes 786440 | tf_op jit(solution)/shard_map/ppermute | solution.py:416
  90.8 8.2 %collective-permute-start.15 = (bf16[256,512]{1,0:T(8,128)(2,1)S(1)}, bf16[256,512]{1,0:T(8,128)(2,1)S(1)}, u32[]{:S(2)}, u32[]{:S(2)}) collective-permute-start(bf16[256,512]{1,0:T(8,128)(2,1)S(1)} %sum_other_half.1), channel_id=1, source_target_pairs={{0,4},{1,5},{2,6},{3,7},{4,0},{5,1},{6,2},{7,3},{8,12},{9,13},{10,... | collective-permute-start | bytes 786440 | tf_op jit(solution)/shard_map/ppermute | solution.py:427
  99.1 2.2 %collective-permute-done.13.refs_2_ = bf16[256,512]{1,0:T(8,128)(2,1)S(1)} collective-permute-done((bf16[256,512]{1,0:T(8,128)(2,1)S(1)}, bf16[256,512]{1,0:T(8,128)(2,1)S(1)}, u32[]{:S(2)}, u32[]{:S(2)}) %collective-permute-start.13) | collective-permute-done | bytes 262176 | tf_op jit(solution)/shard_map/ppermute | solution.py:416
  101.2 8.7 %collective-permute-done.15.refs_4_ = bf16[256,512]{1,0:T(8,128)(2,1)S(1)} collective-permute-done((bf16[256,512]{1,0:T(8,128)(2,1)S(1)}, bf16[256,512]{1,0:T(8,128)(2,1)S(1)}, u32[]{:S(2)}, u32[]{:S(2)}) %collective-permute-start.15) | collective-permute-done | bytes 262176 | tf_op jit(solution)/shard_map/ppermute | solution.py:427
  110.6 17.7 %all_to_all.15.squares = f32[8,8,256]{2,1,0:T(8,128)S(1)} all-to-all(f32[8,8,256]{2,1,0:T(8,128)S(1)} %get-tuple-element.62), channel_id=1, replica_groups=mesh['seq'=64,'tp'=8] {'tp'}, dimensions={0} | all-to-all | bytes 131072 | tf_op jit(solution)/shard_map/all_to_all | solution.py:439
  (46 shorter events, 16.9 us)
Async XLA Ops:
  1.5 8.3 %collective-permute-start = (bf16[256,128]{1,0:T(8,128)(2,1)S(1)}, bf16[256,128]{1,0:T(8,128)(2,1)S(1)}, u32[]{:S(2)}, u32[]{:S(2)}) collective-permute-start(bf16[256,128]{1,0:T(8,128)(2,1)S(1)} %pad_maximum_fusion.2.here), channel_id=1, source_target_pairs={{0,504},{1,505},{2,506},{3,507},{4,508},{5,509},{6,510},{7,511}} | collective-permute-start | bytes 196616 | tf_op jit(solution)/shard_map/ppermute | solution.py:301
  3.0 14.0 %all-to-all-start = ((bf16[4,256,128]{2,1,0:T(8,128)(2,1)}), bf16[4,256,128]{2,1,0:T(8,128)(2,1)S(1)}, u32[]{:S(2)}, u32[]{:S(2)}) async-start(bf16[4,256,128]{2,1,0:T(8,128)(2,1)} %broadcast_in_dim.3), calls=%async_computation | async-start | bytes 524288 | tf_op jit(solution)/shard_map/all_to_all | solution.py:296
  9.9 1.0 copy-start.5
  9.9 16.3 %copy-start = (bf16[256,128]{1,0:T(8,128)(2,1)S(1)}, bf16[256,128]{1,0:T(8,128)(2,1)}, u32[]{:S(2)}) copy-start(bf16[256,128]{1,0:T(8,128)(2,1)} %k.1) | copy-start | bytes 196612
  9.9 16.3 %copy-start.1 = (bf16[256,128]{1,0:T(8,128)(2,1)S(1)}, bf16[256,128]{1,0:T(8,128)(2,1)}, u32[]{:S(2)}) copy-start(bf16[256,128]{1,0:T(8,128)(2,1)} %v.1) | copy-start | bytes 196612
  9.9 3.5 %collective-permute-start.1 = (bf16[256,128]{1,0:T(8,128)(2,1)S(1)}, bf16[256,128]{1,0:T(8,128)(2,1)S(1)}, u32[]{:S(2)}, u32[]{:S(2)}) collective-permute-start(bf16[256,128]{1,0:T(8,128)(2,1)S(1)} %choose_anchor.1), channel_id=1, source_target_pairs={{0,248},{504,376},{1,249},{505,377},{2,250},{506,378},{3,251},{507... | collective-permute-start | bytes 196616 | tf_op jit(solution)/shard_map/ppermute | solution.py:312
  10.8 16.0 %collective-permute-start.10 = (bf16[256,512]{1,0:T(8,128)(2,1)S(1)}, bf16[256,512]{1,0:T(8,128)(2,1)S(1)}, u32[]{:S(2)}, u32[]{:S(2)}) collective-permute-start(bf16[256,512]{1,0:T(8,128)(2,1)S(1)} %copy-done.5), channel_id=1, source_target_pairs={{0,8},{8,0},{16,24},{24,16},{32,40},{40,32},{48,56},{56,48},{64,72... | collective-permute-start | bytes 786440 | tf_op jit(solution)/shard_map/ppermute | solution.py:302
  17.0 12.1 %collective-permute-start.2 = (bf16[1024,128]{1,0:T(8,128)(2,1)S(1)}, bf16[1024,128]{1,0:T(8,128)(2,1)S(1)}, u32[]{:S(2)}, u32[]{:S(2)}) collective-permute-start(bf16[1024,128]{1,0:T(8,128)(2,1)S(1)} %pad_maximum_fusion.blk), channel_id=1, source_target_pairs={{0,112},{8,120},{16,0},{24,8},{32,16},{40,24},{48,32},{56,40},{64,... | collective-permute-start | bytes 786440 | tf_op jit(solution)/shard_map/ppermute | solution.py:320
  24.2 8.8 %collective-permute-start.6 = (bf16[1024,128]{1,0:T(8,128)(2,1)S(1)}, bf16[1024,128]{1,0:T(8,128)(2,1)S(1)}, u32[]{:S(2)}, u32[]{:S(2)}) collective-permute-start(bf16[1024,128]{1,0:T(8,128)(2,1)S(1)} %pad_maximum_fusion.blk), channel_id=1, source_target_pairs={{0,16},{8,24},{16,32},{24,40},{32,48},{40,56},{48,64},{56,72},{64,... | collective-permute-start | bytes 786440 | tf_op jit(solution)/shard_map/ppermute | solution.py:319
  29.1 9.6 %collective-permute-start.3 = (bf16[1024,128]{1,0:T(8,128)(2,1)S(1)}, bf16[1024,128]{1,0:T(8,128)(2,1)S(1)}, u32[]{:S(2)}, u32[]{:S(2)}) collective-permute-start(bf16[1024,128]{1,0:T(8,128)(2,1)S(1)} %collective-permute-done.2.bwd), channel_id=1, source_target_pairs={{0,112},{8,120},{16,0},{24,8},{32,16},{40,24},{48,32},{56,40},{64,... | collective-permute-start | bytes 786440 | tf_op jit(solution)/shard_map/ppermute | solution.py:323
  33.0 10.1 %collective-permute-start.7 = (bf16[1024,128]{1,0:T(8,128)(2,1)S(1)}, bf16[1024,128]{1,0:T(8,128)(2,1)S(1)}, u32[]{:S(2)}, u32[]{:S(2)}) collective-permute-start(bf16[1024,128]{1,0:T(8,128)(2,1)S(1)} %collective-permute-done.6.fwd), channel_id=1, source_target_pairs={{0,16},{8,24},{16,32},{24,40},{32,48},{40,56},{48,64},{56,72},{64,... | collective-permute-start | bytes 786440 | tf_op jit(solution)/shard_map/ppermute | solution.py:322
  38.6 10.1 %collective-permute-start.4 = (bf16[1024,128]{1,0:T(8,128)(2,1)S(1)}, bf16[1024,128]{1,0:T(8,128)(2,1)S(1)}, u32[]{:S(2)}, u32[]{:S(2)}) collective-permute-start(bf16[1024,128]{1,0:T(8,128)(2,1)S(1)} %collective-permute-done.3.bwd), channel_id=1, source_target_pairs={{0,112},{8,120},{16,0},{24,8},{32,16},{40,24},{48,32},{56,40},{64,... | collective-permute-start | bytes 786440 | tf_op jit(solution)/shard_map/ppermute | solution.py:323
  43.1 10.8 %collective-permute-start.8 = (bf16[1024,128]{1,0:T(8,128)(2,1)S(1)}, bf16[1024,128]{1,0:T(8,128)(2,1)S(1)}, u32[]{:S(2)}, u32[]{:S(2)}) collective-permute-start(bf16[1024,128]{1,0:T(8,128)(2,1)S(1)} %collective-permute-done.7.fwd), channel_id=1, source_target_pairs={{0,16},{8,24},{16,32},{24,40},{32,48},{40,56},{48,64},{56,72},{64,... | collective-permute-start | bytes 786440 | tf_op jit(solution)/shard_map/ppermute | solution.py:322
  48.7 10.3 %collective-permute-start.5 = (bf16[1024,128]{1,0:T(8,128)(2,1)S(1)}, bf16[1024,128]{1,0:T(8,128)(2,1)S(1)}, u32[]{:S(2)}, u32[]{:S(2)}) collective-permute-start(bf16[1024,128]{1,0:T(8,128)(2,1)S(1)} %collective-permute-done.4.bwd), channel_id=1, source_target_pairs={{16,0},{24,8},{48,32},{56,40},{80,64},{88,72},{112,96},{120,104},{... | collective-permute-start | bytes 786440 | tf_op jit(solution)/shard_map/ppermute | solution.py:326
  53.9 8.3 %collective-permute-start.9 = (bf16[1024,128]{1,0:T(8,128)(2,1)S(1)}, bf16[1024,128]{1,0:T(8,128)(2,1)S(1)}, u32[]{:S(2)}, u32[]{:S(2)}) collective-permute-start(bf16[1024,128]{1,0:T(8,128)(2,1)S(1)} %collective-permute-done.8.fwd), channel_id=1, source_target_pairs={{0,16},{8,24},{32,48},{40,56},{64,80},{72,88},{96,112},{104,120},{... | collective-permute-start | bytes 786440 | tf_op jit(solution)/shard_map/ppermute | solution.py:325
  63.7 3.8 %collective-permute-start.11 = (bf16[4,256,256]{2,1,0:T(8,128)(2,1)S(1)}, bf16[4,256,256]{2,1,0:T(8,128)(2,1)S(1)}, u32[]{:S(2)}, u32[]{:S(2)}) collective-permute-start(bf16[4,256,256]{2,1,0:T(8,128)(2,1)S(1)} %get-tuple-element.54), channel_id=1, source_target_pairs={{0,8},{8,0},{16,24},{24,16},{32,40},{40,32},{48,56},{56,48},{64,72... | collective-permute-start | bytes 1572872 | tf_op jit(solution)/shard_map/ppermute | solution.py:375
  65.6 2.2 %copy-start.3 = (bf16[512,4096]{1,0:T(8,128)(2,1)S(1)}, bf16[512,4096]{1,0:T(8,128)(2,1)}, u32[]{:S(2)}) copy-start(bf16[512,4096]{1,0:T(8,128)(2,1)} %w.3) | copy-start | bytes 12582916
  69.9 20.8 %all-to-all-start.1 = ((bf16[4,256,512]{2,1,0:T(8,128)(2,1)}), bf16[4,256,512]{2,1,0:T(8,128)(2,1)S(1)}, u32[]{:S(2)}, u32[]{:S(2)}) async-start(bf16[4,256,512]{2,1,0:T(8,128)(2,1)} %get-tuple-element.60), calls=%async_computation.1 | async-start | bytes 2097152 | tf_op jit(solution)/shard_map/all_to_all | solution.py:405
  74.2 2.2 %copy-start.4 = (bf16[512,4096]{1,0:T(8,128)(2,1)S(1)}, bf16[512,4096]{1,0:T(8,128)(2,1)}, u32[]{:S(2)}) copy-start(bf16[512,4096]{1,0:T(8,128)(2,1)} %w.3) | copy-start | bytes 12582916
  76.4 51.9 %copy-start.2 = (f32[512]{0:T(512)S(1)}, f32[512]{0:T(512)}, u32[]{:S(2)}) copy-start(f32[512]{0:T(512)} %param.13) | copy-start | bytes 6148
  77.1 22.0 %collective-permute-start.12 = (bf16[256,512]{1,0:T(8,128)(2,1)S(1)}, bf16[256,512]{1,0:T(8,128)(2,1)S(1)}, u32[]{:S(2)}, u32[]{:S(2)}) collective-permute-start(bf16[256,512]{1,0:T(8,128)(2,1)S(1)} %get-tuple-element.57), channel_id=1, source_target_pairs={{0,1},{1,2},{2,3},{3,0},{4,5},{5,6},{6,7},{7,4},{8,9},{9,10},{10,1... | collective-permute-start | bytes 786440 | tf_op jit(solution)/shard_map/ppermute | solution.py:416
  81.1 20.2 %collective-permute-start.13 = (bf16[256,512]{1,0:T(8,128)(2,1)S(1)}, bf16[256,512]{1,0:T(8,128)(2,1)S(1)}, u32[]{:S(2)}, u32[]{:S(2)}) collective-permute-start(bf16[256,512]{1,0:T(8,128)(2,1)S(1)} %get-tuple-element.58), channel_id=1, source_target_pairs={{0,2},{1,3},{2,0},{3,1},{4,6},{5,7},{6,4},{7,5},{8,10},{9,11},{10,... | collective-permute-start | bytes 786440 | tf_op jit(solution)/shard_map/ppermute | solution.py:416
  85.7 15.6 %collective-permute-start.14 = (bf16[256,512]{1,0:T(8,128)(2,1)S(1)}, bf16[256,512]{1,0:T(8,128)(2,1)S(1)}, u32[]{:S(2)}, u32[]{:S(2)}) collective-permute-start(bf16[256,512]{1,0:T(8,128)(2,1)S(1)} %get-tuple-element.59), channel_id=1, source_target_pairs={{0,3},{1,0},{2,1},{3,2},{4,7},{5,4},{6,5},{7,6},{8,11},{9,8},{10,9... | collective-permute-start | bytes 786440 | tf_op jit(solution)/shard_map/ppermute | solution.py:416
  90.8 19.1 %collective-permute-start.15 = (bf16[256,512]{1,0:T(8,128)(2,1)S(1)}, bf16[256,512]{1,0:T(8,128)(2,1)S(1)}, u32[]{:S(2)}, u32[]{:S(2)}) collective-permute-start(bf16[256,512]{1,0:T(8,128)(2,1)S(1)} %sum_other_half.1), channel_id=1, source_target_pairs={{0,4},{1,5},{2,6},{3,7},{4,0},{5,1},{6,2},{7,3},{8,12},{9,13},{10,... | collective-permute-start | bytes 786440 | tf_op jit(solution)/shard_map/ppermute | solution.py:427
